TPU v7x, 32 devices: a whole 2x2x4 slice. The times are simulated.
32 devices in a mesh: seq: 8 (over z, x), head: 4 (over y, core).
Axes of the slice: x: 2, y: 2, z: 4, core: 2. Of those that a mesh axis runs over, the one named last changes fastest.
Arguments:
- block_in: bfloat16 [12288, 1024], P(('seq', 'head')), may hold values from -6 to 6
- out_grad: bfloat16 [12288, 1024], P(('seq', 'head')), may hold values from -6 to 6
- utt_ends: int32 [27], replicated, may hold values from 1 to 12288, as said below
- valid_ends: int32 [27], replicated, may hold values from 1 to 12288, as said below
- ffn1_in: bfloat16 [1024, 4096], P('seq', 'head'), may hold values from -0.1875 to 0.1875
- ffn1_out: bfloat16 [4096, 1024], P('head', 'seq'), may hold values from -0.09375 to 0.09375
- att_qkv: bfloat16 [1024, 3072], P(('seq', 'head')), may hold values from -0.1875 to 0.1875
- att_out: bfloat16 [1024, 1024], P(('seq', 'head')), may hold values from -0.5 to 0.5
- content_bias: bfloat16 [1024], P(('seq', 'head')), may hold values from -3 to 3
- conv_in: bfloat16 [1024, 2048], P(('seq', 'head')), may hold values from -0.1875 to 0.1875
- conv_out: bfloat16 [1024, 1024], P(('seq', 'head')), may hold values from -0.1875 to 0.1875
- ffn2_in: bfloat16 [1024, 4096], P('seq', 'head'), may hold values from -0.1875 to 0.1875
- ffn2_out: bfloat16 [4096, 1024], P('head', 'seq'), may hold values from -0.09375 to 0.09375
- conv_depth: bfloat16 [5, 1024], P(None, ('seq', 'head')), may hold values from -3 to 3
- norm_gain: bfloat16 [6, 1024], P(None, ('seq', 'head')), may hold values from 0.5 to 1.5
- norm_bias: bfloat16 [6, 1024], P(None, ('seq', 'head')), may hold values from -1.75 to 1.75
Outputs:
- block_out: bfloat16 [12288, 1024], P(('seq', 'head'))
- grad_in: bfloat16 [12288, 1024], P(('seq', 'head'))
- grad_ffn1_in: float32 [1024, 4096], P('seq', 'head')
- grad_ffn1_out: float32 [4096, 1024], P('head', 'seq')
- grad_att_qkv: float32 [1024, 3072], P(('seq', 'head'))
- grad_att_out: float32 [1024, 1024], P(('seq', 'head'))
- grad_content_bias: float32 [1024], P(('seq', 'head'))
- grad_conv_in: float32 [1024, 2048], P(('seq', 'head'))
- grad_conv_out: float32 [1024, 1024], P(('seq', 'head'))
- grad_ffn2_in: float32 [1024, 4096], P('seq', 'head')
- grad_ffn2_out: float32 [4096, 1024], P('head', 'seq')
- grad_conv_depth: float32 [5, 1024], P(None, ('seq', 'head'))
- grad_norm_gain: float32 [6, 1024], P(None, ('seq', 'head'))
- grad_norm_bias: float32 [6, 1024], P(None, ('seq', 'head'))
Inputs may be any that keep to these rules, and one draw needn't show every extreme that they name: `utt_ends`: Non-decreasing; the utterance u spans frames from the previous entry (0 for the first) to this one; every utterance is shorter than 1536 frames; the final entries equal 12288, the last ones as empty utterances. `valid_ends`: for each utterance, a frame between its start plus one and its end; frames from there to its end are padding.
All inputs are finite; a program needn't handle non-finite values.
Results may differ from a plain program's by a relative error of at most 0.019.
Values may be sent and summed in bfloat16 or wider, within the bound.
No kernel may reach another device: no remote copies, remote signals or barrier semaphores. Data moves between devices by JAX's collectives and lax.ppermute only.
A program may use at most 320 MiB of HBM per device.

v0:
```python
import jax
import jax.numpy as jnp
from jax import lax
from jax.sharding import PartitionSpec as P

DH = 128
KSIZE = 5


EPSILON = 1e-05
MASKED = -1e30


def extended(cells, sides, width):
    for axis, dim in sides:
        count = lax.axis_size(axis)
        ends = count - 1
        head = lax.slice_in_dim(cells, 0, width, axis=dim)
        tail = lax.slice_in_dim(cells, cells.shape[dim] - width, cells.shape[dim], axis=dim)
        cells = jnp.concatenate(
            [
                lax.ppermute(tail, axis, [(i, (i + 1) % count) for i in range(ends)]),
                cells,
                lax.ppermute(head, axis, [((i + 1) % count, i) for i in range(ends)]),
            ],
            axis=dim,
        )
    return cells


def norm_forward(values, norm_gains, shifts):
    centred = values - jnp.mean(values, axis=-1, keepdims=True)
    variance = jnp.mean(centred * centred, axis=-1, keepdims=True)
    inv_std = lax.rsqrt(variance + EPSILON)
    normed = centred * inv_std
    return (normed * norm_gains + shifts, normed, inv_std)


def norm_backward(upstream, normed, inv_std, norm_gains):
    scaled = upstream * norm_gains
    inner = (
        scaled
        - jnp.mean(scaled, axis=-1, keepdims=True)
        - normed * jnp.mean(scaled * normed, axis=-1, keepdims=True)
    )
    return (inv_std * inner, jnp.sum(upstream * normed, axis=0), jnp.sum(upstream, axis=0))


def weight_grad(left_side, right_side):
    return lax.dot_general(
        left_side, right_side, (((0,), (0,)), ((), ())), preferred_element_type=jnp.float32
    )


def input_grad(upstream, weights):
    return lax.dot_general(
        upstream, weights, (((1,), (1,)), ((), ())), preferred_element_type=jnp.float32
    )


def join_inward(stacked, seq_count, head_count):
    pieces, rows, cols = stacked.shape
    return (
        stacked.reshape(seq_count, head_count, rows, cols)
        .transpose(0, 2, 1, 3)
        .reshape(seq_count * rows, head_count * cols)
    )


def join_outward(stacked, seq_count, head_count):
    pieces, rows, cols = stacked.shape
    return (
        stacked.reshape(seq_count, head_count, rows, cols)
        .transpose(1, 2, 0, 3)
        .reshape(head_count * rows, seq_count * cols)
    )


def split_inward(whole, seq_count, head_count):
    rows = whole.shape[0] // seq_count
    cols = whole.shape[1] // head_count
    return (
        whole.reshape(seq_count, rows, head_count, cols)
        .transpose(0, 2, 1, 3)
        .reshape(seq_count * head_count, rows, cols)
    )


def split_outward(whole, seq_count, head_count):
    rows = whole.shape[0] // head_count
    cols = whole.shape[1] // seq_count
    return (
        whole.reshape(head_count, rows, seq_count, cols)
        .transpose(2, 0, 1, 3)
        .reshape(seq_count * head_count, rows, cols)
    )


def frame_info(positions, end_frames, valid_frames, all_frames):
    segment = jnp.sum((end_frames[None, :] <= positions[:, None]).astype(jnp.int32), axis=1)
    valid_seg = jnp.sum((valid_frames[None, :] <= positions[:, None]).astype(jnp.int32), axis=1)
    inside = (positions >= 0) & (positions < all_frames)
    valid = (segment == valid_seg) & inside
    segment = jnp.where(positions < 0, -1, jnp.where(positions >= all_frames, -2, segment))
    return (segment, valid)


def feed_forward(values, w_in, w_out, norm_gains, shifts):
    normed_out, normed, inv_std = norm_forward(values, norm_gains, shifts)
    hidden_in = normed_out.astype(jnp.bfloat16)
    hidden = jnp.dot(hidden_in, w_in, preferred_element_type=jnp.float32)
    active = jax.nn.silu(hidden).astype(jnp.bfloat16)
    result = jnp.dot(active, w_out, preferred_element_type=jnp.float32)
    return (result, (hidden_in, hidden, active, normed, inv_std))


def feed_backward(upstream, kept_values, w_in, w_out, norm_gains):
    hidden_in, hidden, active, normed, inv_std = kept_values
    result_grad = (0.5 * upstream).astype(jnp.bfloat16)
    grad_out = weight_grad(active, result_grad)
    active_grad = input_grad(result_grad, w_out)
    sigmoid_val = jax.nn.sigmoid(hidden)
    hidden_grad = (active_grad * sigmoid_val * (1.0 + hidden * (1.0 - sigmoid_val))).astype(
        jnp.bfloat16
    )
    grad_inner = weight_grad(hidden_in, hidden_grad)
    normed_grad = input_grad(hidden_grad, w_in)
    values_grad, gain_grad, shift_grad = norm_backward(normed_grad, normed, inv_std, norm_gains)
    return (values_grad, grad_inner, grad_out, gain_grad, shift_grad)


def body(
    block_in,
    out_grad,
    utt_ends,
    valid_ends,
    ffn1_in,
    ffn1_out,
    att_qkv,
    att_out,
    content_bias,
    conv_in,
    conv_out,
    ffn2_in,
    ffn2_out,
    conv_depth,
    norm_gain,
    norm_bias,
):
    seq_count = lax.axis_size("seq")
    head_count = lax.axis_size("head")
    gathered = (
        lax.all_gather(ffn1_in[None], ("seq", "head"), axis=0, tiled=True),
        lax.all_gather(ffn2_in[None], ("seq", "head"), axis=0, tiled=True),
        lax.all_gather(ffn1_out[None], ("seq", "head"), axis=0, tiled=True),
        lax.all_gather(ffn2_out[None], ("seq", "head"), axis=0, tiled=True),
        lax.all_gather(att_qkv, ("seq", "head"), axis=0, tiled=True),
        lax.all_gather(att_out, ("seq", "head"), axis=0, tiled=True),
        lax.all_gather(content_bias, ("seq", "head"), axis=0, tiled=True),
        lax.all_gather(conv_in, ("seq", "head"), axis=0, tiled=True),
        lax.all_gather(conv_out, ("seq", "head"), axis=0, tiled=True),
        lax.all_gather(conv_depth, ("seq", "head"), axis=1, tiled=True),
        lax.all_gather(norm_gain, ("seq", "head"), axis=1, tiled=True),
        lax.all_gather(norm_bias, ("seq", "head"), axis=1, tiled=True),
    )
    w_f1i = join_inward(gathered[0], seq_count, head_count)
    w_f2i = join_inward(gathered[1], seq_count, head_count)
    w_f1o = join_outward(gathered[2], seq_count, head_count)
    w_f2o = join_outward(gathered[3], seq_count, head_count)
    w_qkv, w_att, w_bias, w_cin, w_cout, w_depth, w_gain, w_shift = gathered[4:]
    norm_gains = w_gain.astype(jnp.float32)
    shifts = w_shift.astype(jnp.float32)
    depth_taps = w_depth.astype(jnp.float32)
    frames, model_width = block_in.shape
    block_span = frames * head_count
    all_frames = block_span * seq_count
    seq_pos = lax.axis_index("seq")
    head_pos = lax.axis_index("head")
    first_frame = (seq_pos * head_count + head_pos) * frames
    block_first = seq_pos * block_span
    own_seg, own_valid = frame_info(
        first_frame + jnp.arange(frames, dtype=jnp.int32), utt_ends, valid_ends, all_frames
    )
    start_frames = jnp.concatenate([jnp.zeros((1,), jnp.int32), utt_ends[:-1]])
    valid_count = jnp.sum((valid_ends - start_frames).astype(jnp.float32))
    valid_col = own_valid.astype(jnp.float32)[:, None]
    inputs = block_in.astype(jnp.float32)
    ffn1_res, kept_ffn1 = feed_forward(inputs, w_f1i, w_f1o, norm_gains[0], shifts[0])
    after_ffn1 = inputs + 0.5 * ffn1_res
    attn_normed, normed_attn, inv_attn = norm_forward(after_ffn1, norm_gains[1], shifts[1])
    attn_in = attn_normed.astype(jnp.bfloat16)
    projected = jnp.dot(attn_in, w_qkv, preferred_element_type=jnp.float32)
    queries = (projected[:, :model_width] + w_bias.astype(jnp.float32)).astype(jnp.bfloat16)
    key_vals = projected[:, model_width : 2 * model_width].astype(jnp.bfloat16)
    value_vals = projected[:, 2 * model_width :].astype(jnp.bfloat16)
    q_heads, k_heads, v_heads = (
        lax.all_to_all(queries, "head", split_axis=1, concat_axis=0, tiled=True),
        lax.all_to_all(key_vals, "head", split_axis=1, concat_axis=0, tiled=True),
        lax.all_to_all(value_vals, "head", split_axis=1, concat_axis=0, tiled=True),
    )
    head_cols = q_heads.shape[1]
    local_heads = head_cols // DH
    key_rows = extended(jnp.concatenate([k_heads, v_heads], axis=1), (("seq", 0),), block_span)
    query_seg = frame_info(
        block_first + jnp.arange(block_span, dtype=jnp.int32), utt_ends, valid_ends, all_frames
    )[0]
    key_seg, key_valid = frame_info(
        block_first - block_span + jnp.arange(3 * block_span, dtype=jnp.int32),
        utt_ends,
        valid_ends,
        all_frames,
    )
    slopes = 32.0 * jnp.exp2(
        -(head_pos * local_heads + jnp.arange(local_heads, dtype=jnp.int32)).astype(jnp.float32)
    )
    block_rows = min(512, block_span)
    window = block_rows + 2 * block_span
    block_total = block_span // block_rows
    score_scale = DH ** (-0.5)

    def block_inputs(row_start):
        q_rows = lax.dynamic_slice_in_dim(q_heads, row_start, block_rows, 0).reshape(
            block_rows, local_heads, DH
        )
        both_rows = lax.dynamic_slice_in_dim(key_rows, row_start, window, 0)
        k_rows = both_rows[:, :head_cols].reshape(window, local_heads, DH)
        v_rows = both_rows[:, head_cols:].reshape(window, local_heads, DH)
        return (q_rows, k_rows, v_rows)

    def block_scores(row_start, q_rows, k_rows):
        raw = (
            jnp.einsum("qhd,khd->hqk", q_rows, k_rows, preferred_element_type=jnp.float32)
            * score_scale
        )
        q_pos = block_first + row_start + jnp.arange(block_rows, dtype=jnp.int32)
        k_pos = block_first - block_span + row_start + jnp.arange(window, dtype=jnp.int32)
        distance = jnp.abs(q_pos[:, None] - k_pos[None, :]).astype(jnp.float32)
        q_part = lax.dynamic_slice_in_dim(query_seg, row_start, block_rows, 0)
        k_part = lax.dynamic_slice_in_dim(key_seg, row_start, window, 0)
        valid_part = lax.dynamic_slice_in_dim(key_valid, row_start, window, 0)
        allowed = (q_part[:, None] == k_part[None, :]) & valid_part[None, :]
        return jnp.where(
            allowed[None], raw - slopes[:, None, None] * distance[None] / block_span, MASKED
        )

    def attend(block_index):
        row_start = block_index * block_rows
        q_rows, k_rows, v_rows = block_inputs(row_start)
        scores = block_scores(row_start, q_rows, k_rows)
        row_max = jnp.max(scores, axis=-1, keepdims=True)
        expo = jnp.exp(scores - row_max)
        row_total = jnp.sum(expo, axis=-1, keepdims=True)
        probabilities = (expo / row_total).astype(jnp.bfloat16)
        mixed = jnp.einsum(
            "hqk,khd->qhd", probabilities, v_rows, preferred_element_type=jnp.float32
        )
        return (
            mixed.astype(jnp.bfloat16).reshape(block_rows, head_cols),
            (row_max + jnp.log(row_total))[:, :, 0],
        )

    block_ids = jnp.arange(block_total, dtype=jnp.int32)
    mixed_blocks, log_totals = lax.map(attend, block_ids)
    mixed_heads = mixed_blocks.reshape(block_span, head_cols)
    mixed_frames = lax.all_to_all(mixed_heads, "head", split_axis=0, concat_axis=1, tiled=True)
    after_attn = after_ffn1 + jnp.dot(mixed_frames, w_att, preferred_element_type=jnp.float32)
    conv_normed, normed_conv, inv_conv = norm_forward(after_attn, norm_gains[2], shifts[2])
    conv_in_low = conv_normed.astype(jnp.bfloat16)
    pointwise = jnp.dot(conv_in_low, w_cin, preferred_element_type=jnp.float32)
    linear_half = pointwise[:, :model_width]
    gate_sig = jax.nn.sigmoid(pointwise[:, model_width:])
    gated = (linear_half * gate_sig * valid_col).astype(jnp.bfloat16)
    conv_reach = (KSIZE - 1) // 2
    gated_ext = extended(gated, ((("seq", "head"), 0),), conv_reach)
    ext_seg = frame_info(
        first_frame - conv_reach + jnp.arange(frames + 2 * conv_reach, dtype=jnp.int32),
        utt_ends,
        valid_ends,
        all_frames,
    )[0]
    tap_masks = [
        (ext_seg[offset : offset + frames] == own_seg).astype(jnp.float32)[:, None]
        for offset in range(KSIZE)
    ]
    conv_sum = jnp.zeros((frames, model_width), jnp.float32)
    for offset in range(KSIZE):
        conv_sum = (
            conv_sum
            + depth_taps[offset]
            * gated_ext[offset : offset + frames].astype(jnp.float32)
            * tap_masks[offset]
        )
    moments = lax.psum(
        (jnp.sum(valid_col * conv_sum, axis=0), jnp.sum(valid_col * conv_sum * conv_sum, axis=0)),
        ("seq", "head"),
    )
    mean_c = moments[0] / valid_count
    variance_c = moments[1] / valid_count - mean_c * mean_c
    inv_batch = lax.rsqrt(variance_c + EPSILON)
    conv_hat = (conv_sum - mean_c) * inv_batch
    batch_out = conv_hat * norm_gains[3] + shifts[3]
    swished = jax.nn.silu(batch_out).astype(jnp.bfloat16)
    after_conv = after_attn + jnp.dot(swished, w_cout, preferred_element_type=jnp.float32)
    ffn2_res, kept_ffn2 = feed_forward(after_conv, w_f2i, w_f2o, norm_gains[4], shifts[4])
    after_ffn2 = after_conv + 0.5 * ffn2_res
    final_out, normed_final, inv_final = norm_forward(after_ffn2, norm_gains[5], shifts[5])
    grad_final = out_grad.astype(jnp.float32)
    grad_x4, final_gain, final_shift = norm_backward(
        grad_final, normed_final, inv_final, norm_gains[5]
    )
    ffn2_back, grad_f2i, grad_f2o, ffn2_gain, ffn2_shift = feed_backward(
        grad_x4, kept_ffn2, w_f2i, w_f2o, norm_gains[4]
    )
    grad_x3 = grad_x4 + ffn2_back
    conv_res_grad = grad_x3.astype(jnp.bfloat16)
    grad_cout = weight_grad(swished, conv_res_grad)
    swish_grad = input_grad(conv_res_grad, w_cout)
    sigmoid_bn = jax.nn.sigmoid(batch_out)
    batch_grad = swish_grad * sigmoid_bn * (1.0 + batch_out * (1.0 - sigmoid_bn))
    batch_gain = jnp.sum(batch_grad * conv_hat, axis=0)
    batch_shift = jnp.sum(batch_grad, axis=0)
    hat_grad = batch_grad * norm_gains[3]
    batch_sums = lax.psum(
        (jnp.sum(hat_grad, axis=0), jnp.sum(hat_grad * conv_hat, axis=0)), ("seq", "head")
    )
    conv_grad = (
        inv_batch
        * (hat_grad - valid_col * (batch_sums[0] + conv_hat * batch_sums[1]) / valid_count)
    ).astype(jnp.bfloat16)
    grad_ext = extended(conv_grad, ((("seq", "head"), 0),), conv_reach)
    conv_grad_f = conv_grad.astype(jnp.float32)
    gated_grad = jnp.zeros((frames, model_width), jnp.float32)
    depth_rows = []
    for offset in range(KSIZE):
        back_start = 2 * conv_reach - offset
        back_mask = (ext_seg[back_start : back_start + frames] == own_seg).astype(jnp.float32)[
            :, None
        ]
        gated_grad = (
            gated_grad
            + depth_taps[offset]
            * grad_ext[back_start : back_start + frames].astype(jnp.float32)
            * back_mask
        )
        depth_rows.append(
            jnp.sum(
                conv_grad_f
                * gated_ext[offset : offset + frames].astype(jnp.float32)
                * tap_masks[offset],
                axis=0,
            )
        )
    grad_depth = jnp.stack(depth_rows)
    glu_grad = gated_grad * valid_col
    point_grad = jnp.concatenate(
        [glu_grad * gate_sig, glu_grad * linear_half * gate_sig * (1.0 - gate_sig)], axis=1
    ).astype(jnp.bfloat16)
    grad_cin = weight_grad(conv_in_low, point_grad)
    conv_norm_grad, conv_gain, conv_shift = norm_backward(
        input_grad(point_grad, w_cin), normed_conv, inv_conv, norm_gains[2]
    )
    grad_x2 = grad_x3 + conv_norm_grad
    attn_res_grad = grad_x2.astype(jnp.bfloat16)
    grad_att = weight_grad(mixed_frames, attn_res_grad)
    mixed_grad = input_grad(attn_res_grad, w_att).astype(jnp.bfloat16)
    mixed_grad_heads = lax.all_to_all(mixed_grad, "head", split_axis=1, concat_axis=0, tiled=True)

    def attend_back(key_carry, block_index):
        row_start = block_index * block_rows
        q_rows, k_rows, v_rows = block_inputs(row_start)
        scores = block_scores(row_start, q_rows, k_rows)
        probabilities = jnp.exp(scores - log_totals[block_index][:, :, None])
        probs_low = probabilities.astype(jnp.bfloat16)
        out_rows = lax.dynamic_slice_in_dim(mixed_grad_heads, row_start, block_rows, 0).reshape(
            block_rows, local_heads, DH
        )
        prob_grad = jnp.einsum("qhd,khd->hqk", out_rows, v_rows, preferred_element_type=jnp.float32)
        score_grad = (
            probabilities * (prob_grad - jnp.sum(probabilities * prob_grad, axis=-1, keepdims=True))
        ).astype(jnp.bfloat16)
        query_part = (
            jnp.einsum("hqk,khd->qhd", score_grad, k_rows, preferred_element_type=jnp.float32)
            * score_scale
        )
        key_part = (
            jnp.einsum("hqk,qhd->khd", score_grad, q_rows, preferred_element_type=jnp.float32)
            * score_scale
        )
        value_part = jnp.einsum(
            "hqk,qhd->khd", probs_low, out_rows, preferred_element_type=jnp.float32
        )
        update = jnp.concatenate(
            [key_part.reshape(window, head_cols), value_part.reshape(window, head_cols)], axis=1
        )
        current = lax.dynamic_slice_in_dim(key_carry, row_start, window, 0)
        key_carry = lax.dynamic_update_slice_in_dim(key_carry, current + update, row_start, 0)
        return (key_carry, query_part.reshape(block_rows, head_cols))

    key_acc, query_parts = lax.scan(
        attend_back, jnp.zeros((3 * block_span, 2 * head_cols), jnp.float32), block_ids
    )
    query_grad = query_parts.reshape(block_span, head_cols)
    bias_grad = lax.dynamic_update_slice_in_dim(
        jnp.zeros((model_width,), jnp.float32), jnp.sum(query_grad, axis=0), head_pos * head_cols, 0
    )
    outward = jnp.concatenate([key_acc[:block_span], key_acc[2 * block_span :]], axis=0)
    inward = extended(outward.astype(jnp.bfloat16), (("seq", 0),), block_span).astype(outward.dtype)
    key_grad = key_acc[block_span : 2 * block_span] + inward[:block_span] + inward[3 * block_span :]
    grad_query, grad_key, grad_value = (
        lax.all_to_all(
            query_grad.astype(jnp.bfloat16), "head", split_axis=0, concat_axis=1, tiled=True
        ),
        lax.all_to_all(
            key_grad[:, :head_cols].astype(jnp.bfloat16),
            "head",
            split_axis=0,
            concat_axis=1,
            tiled=True,
        ),
        lax.all_to_all(
            key_grad[:, head_cols:].astype(jnp.bfloat16),
            "head",
            split_axis=0,
            concat_axis=1,
            tiled=True,
        ),
    )
    proj_grad = jnp.concatenate([grad_query, grad_key, grad_value], axis=1)
    grad_qkv = weight_grad(attn_in, proj_grad)
    attn_norm_grad, attn_gain, attn_shift = norm_backward(
        input_grad(proj_grad, w_qkv), normed_attn, inv_attn, norm_gains[1]
    )
    grad_x1 = grad_x2 + attn_norm_grad
    ffn1_back, grad_f1i, grad_f1o, ffn1_gain, ffn1_shift = feed_backward(
        grad_x1, kept_ffn1, w_f1i, w_f1o, norm_gains[0]
    )
    grad_input = (grad_x1 + ffn1_back).astype(jnp.bfloat16)
    gain_stack = jnp.stack([ffn1_gain, attn_gain, conv_gain, batch_gain, ffn2_gain, final_gain])
    shift_stack = jnp.stack(
        [ffn1_shift, attn_shift, conv_shift, batch_shift, ffn2_shift, final_shift]
    )
    reduced = (
        lax.psum_scatter(
            split_inward(grad_f1i, seq_count, head_count),
            ("seq", "head"),
            scatter_dimension=0,
            tiled=True,
        ),
        lax.psum_scatter(
            split_inward(grad_f2i, seq_count, head_count),
            ("seq", "head"),
            scatter_dimension=0,
            tiled=True,
        ),
        lax.psum_scatter(
            split_outward(grad_f1o, seq_count, head_count),
            ("seq", "head"),
            scatter_dimension=0,
            tiled=True,
        ),
        lax.psum_scatter(
            split_outward(grad_f2o, seq_count, head_count),
            ("seq", "head"),
            scatter_dimension=0,
            tiled=True,
        ),
        lax.psum_scatter(grad_qkv, ("seq", "head"), scatter_dimension=0, tiled=True),
        lax.psum_scatter(grad_att, ("seq", "head"), scatter_dimension=0, tiled=True),
        lax.psum_scatter(bias_grad, ("seq", "head"), scatter_dimension=0, tiled=True),
        lax.psum_scatter(grad_cin, ("seq", "head"), scatter_dimension=0, tiled=True),
        lax.psum_scatter(grad_cout, ("seq", "head"), scatter_dimension=0, tiled=True),
        lax.psum_scatter(grad_depth, ("seq", "head"), scatter_dimension=1, tiled=True),
        lax.psum_scatter(gain_stack, ("seq", "head"), scatter_dimension=1, tiled=True),
        lax.psum_scatter(shift_stack, ("seq", "head"), scatter_dimension=1, tiled=True),
    )
    out_f1i = reduced[0][0]
    out_f2i = reduced[1][0]
    out_f1o = reduced[2][0]
    out_f2o = reduced[3][0]
    rest = reduced[4:]
    return (
        final_out.astype(jnp.bfloat16),
        grad_input,
        out_f1i,
        out_f1o,
        rest[0],
        rest[1],
        rest[2],
        rest[3],
        rest[4],
        out_f2i,
        out_f2o,
        rest[5],
        rest[6],
        rest[7],
    )


def solution(mesh):
    return jax.shard_map(
        body,
        mesh=mesh,
        in_specs=(
            P(("seq", "head"), None),
            P(("seq", "head"), None),
            P(),
            P(),
            P("seq", "head"),
            P("head", "seq"),
            P(("seq", "head"), None),
            P(("seq", "head"), None),
            P(("seq", "head")),
            P(("seq", "head"), None),
            P(("seq", "head"), None),
            P("seq", "head"),
            P("head", "seq"),
            P(None, ("seq", "head")),
            P(None, ("seq", "head")),
            P(None, ("seq", "head")),
        ),
        out_specs=(
            P(("seq", "head"), None),
            P(("seq", "head"), None),
            P("seq", "head"),
            P("head", "seq"),
            P(("seq", "head"), None),
            P(("seq", "head"), None),
            P(("seq", "head")),
            P(("seq", "head"), None),
            P(("seq", "head"), None),
            P("seq", "head"),
            P("head", "seq"),
            P(None, ("seq", "head")),
            P(None, ("seq", "head")),
            P(None, ("seq", "head")),
        ),
        check_vma=False,
    )
```

profile of v0, /device:TPU:0, one launch (start us, length us, event | category | flops | bytes accessed | tf_op | source)
XLA Modules:
  0.0 2916.4 jit_solution(14122785424782788239)
XLA Ops:
  11.9 44.4 %all-gather.4 = bf16[32,32,6]{1,2,0:T(8,128)(2,1)S(1)} all-gather(bf16[1,32,6]{1,2,0:T(8,128)(2,1)} %bitcast.421), channel_id=1, replica_groups=mesh['seq'=8,'head'=4] {'seq','head'}, dimensions={0}, use_global_device_ids=true | all-gather | bytes 12672 | tf_op jit(solution)/shard_map/all_gather | solution.py:163
  56.4 37.6 %all-gather.5 = bf16[32,32,6]{1,2,0:T(8,128)(2,1)S(1)} all-gather(bf16[1,32,6]{1,2,0:T(8,128)(2,1)S(1)} %bitcast.422), channel_id=1, replica_groups=mesh['seq'=8,'head'=4] {'seq','head'}, dimensions={0}, use_global_device_ids=true | all-gather | bytes 12672 | tf_op jit(solution)/shard_map/all_gather | solution.py:164
  108.4 62.3 %all-gather.26.cloned.1.call-done = bf16[32768,128]{1,0:T(8,128)(2,1)} async-done(((bf16[1024,128]{1,0:T(8,128)(2,1)}), bf16[32768,128]{1,0:T(8,128)(2,1)}) %all-gather.26.cloned.1.call-update) | async-done | bytes 8388624 | tf_op jit(solution)/shard_map/all_gather | solution.py:155
  193.1 48.7 %all-gather.16.cloned.1.call-done = bf16[1024,3072]{1,0:T(8,128)(2,1)} async-done(((bf16[32,3072]{1,0:T(8,128)(2,1)}), bf16[1024,3072]{1,0:T(8,128)(2,1)}) %all-gather.16.cloned.1.call-update) | async-done | bytes 6291472 | tf_op jit(solution)/shard_map/all_gather | solution.py:157
  289.4 102.7 %all-reduce = bf16[1024]{0:T(1024)(128)(2,1)S(1)} all-reduce(bf16[1024]{0:T(1024)(128)(2,1)S(1)} %dynamic-update-slice), channel_id=1, replica_groups=mesh['seq'=8,'head'=4] {'seq','head'}, use_global_device_ids=true, to_apply=%add | all-reduce | flops 1024 | bytes 4096
  392.1 40.5 %all-gather.6 = bf16[32,32,5]{1,2,0:T(8,128)(2,1)S(1)} all-gather(bf16[1,32,5]{1,2,0:T(8,128)(2,1)S(1)} %bitcast.423), channel_id=1, replica_groups=mesh['seq'=8,'head'=4] {'seq','head'}, dimensions={0}, use_global_device_ids=true | all-gather | bytes 10560 | tf_op jit(solution)/shard_map/all_gather | solution.py:162
  466.1 90.9 %while.30 = (s32[]{:T(128)}, bf16[3,512,256]{2,1,0:T(8,128)(2,1)}, f32[3,2,512]{2,1,0:T(2,128)S(1)}, s32[3]{0:T(128)S(1)}, bf16[4608,512]{0,1:T(8,128)(2,1)}, /*...) while((s32[]{:T(128)}, bf16[3,512,256]{2,1,0:T(8,128)(2,1)}, ...), condition=%wide.region_10.11_spmd.clone, body=%wide.region_7.0_spmd.clone.sunk | while | flops 1928727552 | bytes 75623256 | solution.py:263
  616.5 37.8 %all-reduce.3 = (f32[1024]{0:T(1024)S(1)}, f32[1024]{0:T(1024)S(1)}) all-reduce(f32[1024]{0:T(1024)S(1)} %get-tuple-element.476, f32[1024]{0:T(1024)S(1)} %get-tuple-element.475), channel_id=1, replica_groups=mesh['seq'=8,'head'=4] {'seq','head'}, use_global_device_ids=true, to_apply=%region_20.21 | all-reduce | flops 2048 | bytes 16384 | tf_op jit(solution)/shard_map/psum | solution.py:293
  697.1 42.9 %all-reduce.2 = (f32[1024]{0:T(1024)S(1)}, f32[1024]{0:T(1024)S(1)}) all-reduce(f32[1024]{0:T(1024)S(1)} %get-tuple-element.455, f32[1024]{0:T(1024)S(1)} %get-tuple-element.470), channel_id=1, replica_groups=mesh['seq'=8,'head'=4] {'seq','head'}, use_global_device_ids=true, to_apply=%region_32.33 | all-reduce | flops 2048 | bytes 16384 | tf_op jit(solution)/shard_map/psum | solution.py:323
  784.8 284.0 %while.31 = (s32[]{:T(128)}, f32[4608,512]{1,0:T(8,128)}, f32[3,512,256]{1,2,0:T(8,128)}, s32[3]{0:T(128)S(1)}, bf16[1536,256]{0,1:T(8,128)(2,1)}, /*index=5*/s3...) while((s32[]{:T(128)}, f32[4608,512]{1,0:T(8,128)}, ...), condition=%wide.region_37.38_spmd.clone, body=%wide.region_35.37_spmd.clone.sunk | while | flops 4755557376 | bytes 343784480 | solution.py:399
  1086.5 60.0 %collective-permute-done.6 = bf16[1536,512]{1,0:T(8,128)(2,1)} collective-permute-done((bf16[1536,512]{1,0:T(8,128)(2,1)S(1)}, bf16[1536,512]{1,0:T(8,128)(2,1)}, u32[]{:S(2)}, u32[]{:S(2)}) %collective-permute-start.6) | collective-permute-done | bytes 1572896 | tf_op jit(solution)/shard_map/ppermute | solution.py:22
  1271.4 20.4 reshape.503
  1341.7 20.5 reshape.499
  1362.2 17.8 copy.194
  1381.9 42.4 %all-reduce.1 = f32[1024]{0:T(1024)S(1)} all-reduce(f32[1024]{0:T(1024)S(1)} %dynamic_update_slice.26), channel_id=10, replica_groups=mesh['seq'=8,'head'=4] {'seq','head'}, use_global_device_ids=true, to_apply=%region_47.48.clone | all-reduce | flops 1024 | bytes 8192
  1445.0 130.9 %reduce-scatter.36.cloned.1.call-done = f32[32,6]{1,0:T(8,128)} async-done(((f32[1024,6]{1,0:T(8,128)}), f32[32,6]{1,0:T(8,128)}) %reduce-scatter.36.cloned.1.call-update) | async-done | bytes 784
  1577.3 138.7 %reduce-scatter.28.cloned.1.call-done = f32[32,1024]{1,0:T(8,128)} async-done(((f32[1024,1024]{1,0:T(8,128)}), f32[32,1024]{1,0:T(8,128)}) %reduce-scatter.28.cloned.1.call-update) | async-done | bytes 131088 | tf_op jit(solution)/shard_map/reduce_scatter | solution.py:471
  1716.0 140.2 %reduce-scatter.24.cloned.1.call-done = f32[32,1024]{1,0:T(8,128)} async-done(((f32[1024,1024]{1,0:T(8,128)}), f32[32,1024]{1,0:T(8,128)}) %reduce-scatter.24.cloned.1.call-update) | async-done | bytes 131088 | tf_op jit(solution)/shard_map/reduce_scatter | solution.py:468
  1856.2 147.8 %reduce-scatter.26.cloned.1.call-done = f32[32,2048]{1,0:T(8,128)} async-done(((f32[1024,2048]{1,0:T(8,128)}), f32[32,2048]{1,0:T(8,128)}) %reduce-scatter.26.cloned.1.call-update) | async-done | bytes 262160 | tf_op jit(solution)/shard_map/reduce_scatter | solution.py:470
  2004.0 158.7 %reduce-scatter.22.cloned.1.call-done = f32[32,3072]{1,0:T(8,128)} async-done(((f32[1024,3072]{1,0:T(8,128)}), f32[32,3072]{1,0:T(8,128)}) %reduce-scatter.22.cloned.1.call-update) | async-done | bytes 393232 | tf_op jit(solution)/shard_map/reduce_scatter | solution.py:467
  2162.7 184.9 %reduce-scatter.32.cloned.1.call-done = f32[1,1024,128]{2,1,0:T(8,128)} async-done(((f32[32,1024,128]{2,1,0:T(8,128)}), f32[1,1024,128]{2,1,0:T(8,128)}) %reduce-scatter.32.cloned.1.call-update) | async-done | bytes 524304 | tf_op jit(solution)/shard_map/reduce_scatter | solution.py:461
  2347.6 187.3 %reduce-scatter.30.cloned.1.call-done = f32[1,128,1024]{2,1,0:T(8,128)} async-done(((f32[32,128,1024]{2,1,0:T(8,128)}), f32[1,128,1024]{2,1,0:T(8,128)}) %reduce-scatter.30.cloned.1.call-update) | async-done | bytes 524304 | tf_op jit(solution)/shard_map/reduce_scatter | solution.py:449
  2534.9 187.3 %reduce-scatter.20.cloned.1.call-done = f32[1,1024,128]{2,1,0:T(8,128)} async-done(((f32[32,1024,128]{2,1,0:T(8,128)}), f32[1,1024,128]{2,1,0:T(8,128)}) %reduce-scatter.20.cloned.1.call-update) | async-done | bytes 524304 | tf_op jit(solution)/shard_map/reduce_scatter | solution.py:455
  2722.2 187.4 %reduce-scatter.18.cloned.1.call-done = f32[1,128,1024]{2,1,0:T(8,128)} async-done(((f32[32,128,1024]{2,1,0:T(8,128)}), f32[1,128,1024]{2,1,0:T(8,128)}) %reduce-scatter.18.cloned.1.call-update) | async-done | bytes 524304 | tf_op jit(solution)/shard_map/reduce_scatter | solution.py:443
  (618 shorter events, 848.6 us)
Async XLA Ops:
  7.2 88.7 %all-gather.24.cloned.1.call-start = ((), (), s32[]{:S(2)}) async-start(), calls=%async_computation.31 | async-start | bytes 8650752 | tf_op jit(solution)/shard_map/all_gather | solution.py:153
  7.9 162.8 %all-gather.26.cloned.1.call-start = ((), (), s32[]{:S(2)}) async-start(), calls=%async_computation.32 | async-start | bytes 8650752 | tf_op jit(solution)/shard_map/all_gather | solution.py:155
  8.7 233.2 %all-gather.16.cloned.1.call-start = ((), (), s32[]{:S(2)}) async-start(), calls=%async_computation.19 | async-start | bytes 6488064 | tf_op jit(solution)/shard_map/all_gather | solution.py:157
  9.4 565.8 %all-gather.18.cloned.1.call-start = ((), (), s32[]{:S(2)}) async-start(), calls=%async_computation.20 | async-start | bytes 2162688 | tf_op jit(solution)/shard_map/all_gather | solution.py:158
  10.0 568.5 %all-gather.20.cloned.1.call-start = ((), (), s32[]{:S(2)}) async-start(), calls=%async_computation.21 | async-start | bytes 4325376 | tf_op jit(solution)/shard_map/all_gather | solution.py:160
  10.6 577.7 %all-gather.28.cloned.1.call-start = ((), (), s32[]{:S(2)}) async-start(), calls=%async_computation.33 | async-start | bytes 8650752 | tf_op jit(solution)/shard_map/all_gather | solution.py:154
  11.2 589.5 %all-gather.30.cloned.1.call-start = ((), (), s32[]{:S(2)}) async-start(), calls=%async_computation.34 | async-start | bytes 8650752 | tf_op jit(solution)/shard_map/all_gather | solution.py:156
  269.0 386.0 %all-gather.22.cloned.1.call-start = ((), (), s32[]{:S(2)}) async-start(), calls=%async_computation.22 | async-start | bytes 2162688 | tf_op jit(solution)/shard_map/all_gather | solution.py:161
  282.2 168.7 %collective-permute-start.1 = (bf16[1536,512]{0,1:T(8,128)(2,1)}, bf16[1536,512]{0,1:T(8,128)(2,1)}, u32[]{:S(2)}, u32[]{:S(2)}) collective-permute-start(bf16[1536,512]{0,1:T(8,128)(2,1)} %pad_maximum_fusion.5), channel_id=1, source_target_pairs={{4,0},{8,4},{12,8},{16,12},{20,16},{24,20},{28,24},{5,1},{9,5},{13... | collective-permute-start | bytes 4718600 | tf_op jit(solution)/shard_map/ppermute | solution.py:24
  283.5 167.4 %collective-permute-start = (bf16[1536,512]{0,1:T(8,128)(2,1)}, bf16[1536,512]{0,1:T(8,128)(2,1)}, u32[]{:S(2)}, u32[]{:S(2)}) collective-permute-start(bf16[1536,512]{0,1:T(8,128)(2,1)} %pad_maximum_fusion.5), channel_id=1, source_target_pairs={{0,4},{4,8},{8,12},{12,16},{16,20},{20,24},{24,28},{1,5},{5,9},{9,... | collective-permute-start | bytes 4718600 | tf_op jit(solution)/shard_map/ppermute | solution.py:22
  1074.4 72.1 %collective-permute-start.6 = (bf16[1536,512]{1,0:T(8,128)(2,1)S(1)}, bf16[1536,512]{1,0:T(8,128)(2,1)}, u32[]{:S(2)}, u32[]{:S(2)}) collective-permute-start(bf16[1536,512]{1,0:T(8,128)(2,1)S(1)} %get-tuple-element.559), channel_id=1, source_target_pairs={{0,4},{4,8},{8,12},{12,16},{16,20},{20,24},{24,28},{1,5},{5,9},{9,... | collective-permute-start | bytes 4718600 | tf_op jit(solution)/shard_map/ppermute | solution.py:22
  1080.5 66.0 %collective-permute-start.7 = (bf16[1536,512]{1,0:T(8,128)(2,1)}, bf16[1536,512]{1,0:T(8,128)(2,1)}, u32[]{:S(2)}, u32[]{:S(2)}) collective-permute-start(bf16[1536,512]{1,0:T(8,128)(2,1)} %get-tuple-element.560), channel_id=1, source_target_pairs={{4,0},{8,4},{12,8},{16,12},{20,16},{24,20},{28,24},{5,1},{9,5},{13... | collective-permute-start | bytes 4718600 | tf_op jit(solution)/shard_map/ppermute | solution.py:24
  1083.0 72.0 %all-to-all-start.5 = ((bf16[4,384,256]{2,1,0:T(8,128)(2,1)}), bf16[4,384,256]{2,1,0:T(8,128)(2,1)S(1)}, u32[]{:S(2)}, u32[]{:S(2)}) async-start(bf16[4,384,256]{2,1,0:T(8,128)(2,1)} %bitcast.342), calls=%async_computation.5 | async-start | bytes 1572864 | tf_op jit(solution)/shard_map/all_to_all | solution.py:410
  1172.6 207.4 %reduce-scatter.34.cloned.1.call-start = ((), (), s32[]{:S(2)}) async-start(), calls=%async_computation.35 | async-start | bytes 540672
  1173.8 269.9 %reduce-scatter.38.cloned.1.call-start = ((), (), s32[]{:S(2)}) async-start(), calls=%async_computation.37 | async-start | bytes 540672
  1208.6 367.3 %reduce-scatter.36.cloned.1.call-start = ((), (), s32[]{:S(2)}) async-start(), calls=%async_computation.36 | async-start | bytes 540672
  1209.8 506.2 %reduce-scatter.28.cloned.1.call-start = ((), (), s32[]{:S(2)}) async-start(), calls=%async_computation.28 | async-start | bytes 4325376 | tf_op jit(solution)/shard_map/reduce_scatter | solution.py:471
  1215.3 640.9 %reduce-scatter.24.cloned.1.call-start = ((), (), s32[]{:S(2)}) async-start(), calls=%async_computation.26 | async-start | bytes 4325376 | tf_op jit(solution)/shard_map/reduce_scatter | solution.py:468
  1219.8 784.2 %reduce-scatter.26.cloned.1.call-start = ((), (), s32[]{:S(2)}) async-start(), calls=%async_computation.27 | async-start | bytes 8650752 | tf_op jit(solution)/shard_map/reduce_scatter | solution.py:470
  1228.3 934.5 %reduce-scatter.22.cloned.1.call-start = ((), (), s32[]{:S(2)}) async-start(), calls=%async_computation.25 | async-start | bytes 12976128 | tf_op jit(solution)/shard_map/reduce_scatter | solution.py:467
  1237.8 1109.8 %reduce-scatter.32.cloned.1.call-start = ((), (), s32[]{:S(2)}) async-start(), calls=%async_computation.30 | async-start | bytes 17301504 | tf_op jit(solution)/shard_map/reduce_scatter | solution.py:461
  1259.4 1275.5 %reduce-scatter.30.cloned.1.call-start = ((), (), s32[]{:S(2)}) async-start(), calls=%async_computation.29 | async-start | bytes 17301504 | tf_op jit(solution)/shard_map/reduce_scatter | solution.py:449
  1309.6 1412.6 %reduce-scatter.20.cloned.1.call-start = ((), (), s32[]{:S(2)}) async-start(), calls=%async_computation.24 | async-start | bytes 17301504 | tf_op jit(solution)/shard_map/reduce_scatter | solution.py:455
  1330.2 1579.4 %reduce-scatter.18.cloned.1.call-start = ((), (), s32[]{:S(2)}) async-start(), calls=%async_computation.23 | async-start | bytes 17301504 | tf_op jit(solution)/shard_map/reduce_scatter | solution.py:443
  (146 other events, 3123.4 us)
Sparse Core Ops, SparseCore 0:
  10.9 80.5 all-gather.23
  94.3 76.3 all-gather.25
  173.6 68.1 all-gather.15
  244.6 91.4 all-gather.17
  338.7 61.7 all-gather.19
  403.3 76.5 all-gather.27
  482.7 76.2 all-gather.29
  561.9 55.2 all-gather.21
  1175.6 135.6 reduce-scatter.33
  1313.5 130.1 reduce-scatter.37
  1445.9 129.9 reduce-scatter.35
  1578.7 137.2 reduce-scatter.27
  1718.9 137.1 reduce-scatter.23
  1859.0 144.9 reduce-scatter.25
  2011.5 151.1 reduce-scatter.21
  2165.5 182.1 reduce-scatter.31
  2350.3 184.5 reduce-scatter.29
  2537.6 184.5 reduce-scatter.19
  2725.1 184.5 reduce-scatter.17
where the time goes:
time: 2930 us; the launch traced here: 2920 us
  waiting for transfers between devices  1720 us (59%)
  blocking collectives  362 us (12%)
  local copies, waits for them, and re-layouts  322 us (11%)
  matrix products  278 us (9%)
  other arithmetic  159 us (5%)
  starting transfers between devices  49.2 us (2%)
    reduce_scatter x1, waiting for transfers between devices, body(): lax.psum_scatter(split_inward(grad_f1i, seq_count, head_count), ('seq', '...  187 us
    reduce_scatter x1, waiting for transfers between devices, body(): lax.psum_scatter(split_outward(grad_f1o, seq_count, head_count), ('seq',...  187 us
    reduce_scatter x1, waiting for transfers between devices, body(): lax.psum_scatter(split_inward(grad_f2i, seq_count, head_count), ('seq', '...  187 us
    reduce_scatter x1, waiting for transfers between devices, body(): lax.psum_scatter(split_outward(grad_f2o, seq_count, head_count), ('seq',...  185 us
    reduce_scatter x1, waiting for transfers between devices, body(): lax.psum_scatter(grad_qkv, ('seq', 'head'), scatter_dimension=0, tiled=True)  159 us
    unnamed x22, waiting for transfers between devices  152 us
    reduce_scatter x1, waiting for transfers between devices, body(): lax.psum_scatter(grad_cin, ('seq', 'head'), scatter_dimension=0, tiled=True)  148 us
    unnamed x2, blocking collectives  145 us
  transfers between devices with their start and end apart: 34, of which 20 were waited for; matrix products, arithmetic and copies ran while one was open for 14% of the time, Pallas kernels for 0%

commit v1 on v0

v1 whole, which is shorter than its diff:
```python
import math

import jax
import jax.numpy as jnp
from jax import lax
from jax.experimental import pallas as pl
from jax.experimental.pallas import tpu as pltpu
from jax.sharding import Mesh
from jax.sharding import PartitionSpec as P

DH = 128
KSIZE = 5
REACH = (KSIZE - 1) // 2
EPSILON = 1e-05
MASKED = -1e30
LOG2E = math.log2(math.e)
DEV = ("z", "x", "y", "c")
LAYER = ("x", "y", "c")
WIDE = ("y", "c", "z", "x")
BQ = 256
BK = 512
BF = jnp.bfloat16
F32 = jnp.float32
VMEM_BYTES = 56 * 1024 * 1024


def pick(cells, index, dim):
    return lax.dynamic_index_in_dim(cells, index, dim, keepdims=False)


def xor_send(cells, axis, bit):
    count = lax.axis_size(axis)
    return lax.ppermute(cells, axis, [(i, i ^ bit) for i in range(count)])


def neighbour_rows(cells):
    count = 1
    for axis in DEV:
        count *= lax.axis_size(axis)
    before = lax.ppermute(cells[-REACH:], DEV, [(i, i + 1) for i in range(count - 1)])
    after = lax.ppermute(cells[:REACH], DEV, [(i + 1, i) for i in range(count - 1)])
    return jnp.concatenate([before, cells, after], axis=0)


def sum_everywhere(rows):
    count = 1
    for axis in DEV:
        count *= lax.axis_size(axis)
    spread = jnp.broadcast_to(rows[None], (count,) + rows.shape)
    return jnp.sum(lax.all_to_all(spread, DEV, split_axis=0, concat_axis=0, tiled=True), axis=0)


def dot_nn(a, b):
    return lax.dot_general(a, b, (((1,), (0,)), ((), ())), preferred_element_type=F32)


def dot_nt(a, b):
    return lax.dot_general(a, b, (((1,), (1,)), ((), ())), preferred_element_type=F32)


def dot_tn(a, b):
    return lax.dot_general(a, b, (((0,), (0,)), ((), ())), preferred_element_type=F32)


def norm_stats(values):
    centred = values - jnp.mean(values, axis=-1, keepdims=True)
    inv_std = lax.rsqrt(jnp.mean(centred * centred, axis=-1, keepdims=True) + EPSILON)
    return centred * inv_std, inv_std


def norm_back(upstream, normed, inv_std, gain):
    scaled = upstream * gain
    inner = (
        scaled
        - jnp.mean(scaled, axis=-1, keepdims=True)
        - normed * jnp.mean(scaled * normed, axis=-1, keepdims=True)
    )
    return inv_std * inner


def ffn_fwd_kernel(x_ref, w_ref, vec_ref, x1_ref, n_ref, s_ref, d_ref, n2_ref, acc_ref):
    step = pl.program_id(0)
    width = x_ref.shape[1]

    @pl.when(step == 0)
    def _():
        normed, _ = norm_stats(x_ref[...].astype(F32))
        n_ref[...] = (normed * vec_ref[0:1, :] + vec_ref[1:2, :]).astype(BF)
        acc_ref[...] = jnp.zeros_like(acc_ref)

    chunk = 256
    for at in range(0, width, chunk):
        a = dot_nn(n_ref[...], w_ref[0, :, at : at + chunk])
        sig = jax.nn.sigmoid(a)
        s_ref[0, :, at : at + chunk] = (a * sig).astype(BF)
        d_ref[0, :, at : at + chunk] = (sig * (1.0 + a * (1.0 - sig))).astype(BF)
    acc_ref[...] += dot_nt(s_ref[0], w_ref[0, :, width:])

    @pl.when(step == pl.num_programs(0) - 1)
    def _():
        x1 = x_ref[...].astype(F32) + 0.5 * acc_ref[...]
        x1_ref[...] = x1
        normed, _ = norm_stats(x1)
        n2_ref[...] = (normed * vec_ref[2:3, :] + vec_ref[3:4, :]).astype(BF)


def ffn_fwd(x, w, vectors):
    frames, width = x.shape
    blocks = w.shape[0]
    whole = lambda j: (0, 0)
    slab = lambda j: (j, 0, 0)
    return pl.pallas_call(
        ffn_fwd_kernel,
        grid=(blocks,),
        in_specs=[
            pl.BlockSpec((frames, width), whole),
            pl.BlockSpec((1, width, 2 * width), slab),
            pl.BlockSpec(vectors.shape, whole),
        ],
        out_specs=[
            pl.BlockSpec((frames, width), whole),
            pl.BlockSpec((frames, width), whole),
            pl.BlockSpec((1, frames, width), slab),
            pl.BlockSpec((1, frames, width), slab),
            pl.BlockSpec((frames, width), whole),
        ],
        out_shape=[
            jax.ShapeDtypeStruct((frames, width), F32),
            jax.ShapeDtypeStruct((frames, width), BF),
            jax.ShapeDtypeStruct((blocks, frames, width), BF),
            jax.ShapeDtypeStruct((blocks, frames, width), BF),
            jax.ShapeDtypeStruct((frames, width), BF),
        ],
        scratch_shapes=[pltpu.VMEM((frames, width), F32)],
        compiler_params=pltpu.CompilerParams(vmem_limit_bytes=VMEM_BYTES),
        cost_estimate=pl.CostEstimate(
            flops=4 * frames * width * width * blocks,
            bytes_accessed=4 * width * width * blocks + 8 * frames * width * blocks,
            transcendentals=frames * width * blocks,
        ),
        name="ffn_forward",
    )(x, w, vectors)


def ffn_last_kernel(
    x_ref, w_ref, vec_ref, og_ref, out_ref, n_ref, s_ref, d_ref, dx_ref, sums_ref, acc_ref
):
    step = pl.program_id(0)
    width = x_ref.shape[1]

    @pl.when(step == 0)
    def _():
        normed, _ = norm_stats(x_ref[...])
        n_ref[...] = (normed * vec_ref[0:1, :] + vec_ref[1:2, :]).astype(BF)
        acc_ref[...] = jnp.zeros_like(acc_ref)

    chunk = 256
    for at in range(0, width, chunk):
        a = dot_nn(n_ref[...], w_ref[0, :, at : at + chunk])
        sig = jax.nn.sigmoid(a)
        s_ref[0, :, at : at + chunk] = (a * sig).astype(BF)
        d_ref[0, :, at : at + chunk] = (sig * (1.0 + a * (1.0 - sig))).astype(BF)
    acc_ref[...] += dot_nt(s_ref[0], w_ref[0, :, width:])

    @pl.when(step == pl.num_programs(0) - 1)
    def _():
        x4 = x_ref[...] + 0.5 * acc_ref[...]
        normed, inv_std = norm_stats(x4)
        gain = vec_ref[2:3, :]
        out_ref[...] = (normed * gain + vec_ref[3:4, :]).astype(BF)
        upstream = og_ref[...].astype(F32)
        dx_ref[...] = norm_back(upstream, normed, inv_std, gain)
        sums_ref[0:1, :] = jnp.sum(upstream * normed, axis=0, keepdims=True)
        sums_ref[1:2, :] = jnp.sum(upstream, axis=0, keepdims=True)


def ffn_last(x, w, vectors, out_grad):
    frames, width = x.shape
    blocks = w.shape[0]
    whole = lambda j: (0, 0)
    slab = lambda j: (j, 0, 0)
    return pl.pallas_call(
        ffn_last_kernel,
        grid=(blocks,),
        in_specs=[
            pl.BlockSpec((frames, width), whole),
            pl.BlockSpec((1, width, 2 * width), slab),
            pl.BlockSpec(vectors.shape, whole),
            pl.BlockSpec((frames, width), whole),
        ],
        out_specs=[
            pl.BlockSpec((frames, width), whole),
            pl.BlockSpec((frames, width), whole),
            pl.BlockSpec((1, frames, width), slab),
            pl.BlockSpec((1, frames, width), slab),
            pl.BlockSpec((frames, width), whole),
            pl.BlockSpec((2, width), whole),
        ],
        out_shape=[
            jax.ShapeDtypeStruct((frames, width), BF),
            jax.ShapeDtypeStruct((frames, width), BF),
            jax.ShapeDtypeStruct((blocks, frames, width), BF),
            jax.ShapeDtypeStruct((blocks, frames, width), BF),
            jax.ShapeDtypeStruct((frames, width), F32),
            jax.ShapeDtypeStruct((2, width), F32),
        ],
        scratch_shapes=[pltpu.VMEM((frames, width), F32)],
        compiler_params=pltpu.CompilerParams(vmem_limit_bytes=VMEM_BYTES),
        cost_estimate=pl.CostEstimate(
            flops=4 * frames * width * width * blocks,
            bytes_accessed=4 * width * width * blocks + 8 * frames * width * blocks,
            transcendentals=frames * width * blocks,
        ),
        name="ffn_last",
    )(x, w, vectors, out_grad)


def ffn_bwd_kernel(up_ref, x_ref, w_ref, d_ref, vec_ref, ef_ref, da_ref, dx_ref, sums_ref, acc_ref):
    step = pl.program_id(0)
    width = up_ref.shape[1]

    @pl.when(step == 0)
    def _():
        ef_ref[...] = (0.5 * up_ref[...]).astype(BF)
        acc_ref[...] = jnp.zeros_like(acc_ref)

    chunk = 256
    for at in range(0, width, chunk):
        ds = dot_nn(ef_ref[...], w_ref[0, :, width + at : width + at + chunk])
        da_ref[0, :, at : at + chunk] = (ds * d_ref[0, :, at : at + chunk].astype(F32)).astype(BF)
    acc_ref[...] += dot_nt(da_ref[0], w_ref[0, :, :width])

    @pl.when(step == pl.num_programs(0) - 1)
    def _():
        normed, inv_std = norm_stats(x_ref[...].astype(F32))
        dn = acc_ref[...]
        dx = up_ref[...] + norm_back(dn, normed, inv_std, vec_ref[0:1, :])
        dx_ref[...] = dx.astype(dx_ref.dtype)
        sums_ref[0:1, :] = jnp.sum(dn * normed, axis=0, keepdims=True)
        sums_ref[1:2, :] = jnp.sum(dn, axis=0, keepdims=True)


def ffn_bwd(upstream, x, w, slope, vectors, out_type):
    frames, width = upstream.shape
    blocks = w.shape[0]
    whole = lambda j: (0, 0)
    slab = lambda j: (j, 0, 0)
    return pl.pallas_call(
        ffn_bwd_kernel,
        grid=(blocks,),
        in_specs=[
            pl.BlockSpec((frames, width), whole),
            pl.BlockSpec((frames, width), whole),
            pl.BlockSpec((1, width, 2 * width), slab),
            pl.BlockSpec((1, frames, width), slab),
            pl.BlockSpec(vectors.shape, whole),
        ],
        out_specs=[
            pl.BlockSpec((frames, width), whole),
            pl.BlockSpec((1, frames, width), slab),
            pl.BlockSpec((frames, width), whole),
            pl.BlockSpec((2, width), whole),
        ],
        out_shape=[
            jax.ShapeDtypeStruct((frames, width), BF),
            jax.ShapeDtypeStruct((blocks, frames, width), BF),
            jax.ShapeDtypeStruct((frames, width), out_type),
            jax.ShapeDtypeStruct((2, width), F32),
        ],
        scratch_shapes=[pltpu.VMEM((frames, width), F32)],
        compiler_params=pltpu.CompilerParams(vmem_limit_bytes=VMEM_BYTES),
        cost_estimate=pl.CostEstimate(
            flops=4 * frames * width * width * blocks,
            bytes_accessed=4 * width * width * blocks + 4 * frames * width * blocks,
            transcendentals=0,
        ),
        name="ffn_backward",
    )(upstream, x, w, slope, vectors)


def attn_fwd_kernel(origin, low_ref, high_ref, c2_ref, q_ref, kv_ref, lo_ref, hi_ref, o_ref, lse_ref):
    block = pl.program_id(0)
    rows = q_ref.shape[0]
    q = q_ref[...]
    c1 = LOG2E * DH**-0.5
    c2 = c2_ref[0]
    at = lax.broadcasted_iota(jnp.int32, (1, rows), 1) + (origin + block * rows)
    q_pos = at.astype(F32)
    lo_q, hi_q = lo_ref[...], hi_ref[...]
    first = low_ref[block]
    steps = (high_ref[block] - first + (BK - 1)) // BK

    def step(t, carry):
        top, total, mixed = carry
        start = pl.multiple_of(first + t * BK, 128)
        k = kv_ref[pl.ds(start, BK), :DH]
        v = kv_ref[pl.ds(start, BK), DH:]
        k_pos = (lax.broadcasted_iota(jnp.int32, (BK, 1), 0) + start).astype(F32)
        scores = dot_nt(k, q) * c1 - jnp.abs(k_pos - q_pos) * c2
        scores = jnp.where((k_pos >= lo_q) & (k_pos < hi_q), scores, MASKED)
        new_top = jnp.maximum(top, jnp.max(scores, axis=0, keepdims=True))
        expo = jnp.exp2(scores - new_top)
        keep = jnp.exp2(top - new_top)
        total = total * keep + jnp.sum(expo, axis=0, keepdims=True)
        mixed = mixed * keep + dot_tn(v, expo.astype(BF))
        return new_top, total, mixed

    top, total, mixed = lax.fori_loop(
        0,
        steps,
        step,
        (
            jnp.full((1, rows), MASKED, F32),
            jnp.zeros((1, rows), F32),
            jnp.zeros((DH, rows), F32),
        ),
    )
    o_ref[...] = (mixed / total).T.astype(BF)
    lse_ref[...] = top + jnp.log2(total)


def attn_fwd(q, kv, low, high, c2, lo_q, hi_q, origin):
    frames = q.shape[0]
    blocks = frames // BQ
    pairs = frames * 1024 * DH
    grid_spec = pltpu.PrefetchScalarGridSpec(
        num_scalar_prefetch=3,
        grid=(blocks,),
        in_specs=[
            pl.BlockSpec((BQ, DH), lambda i, *_: (i, 0)),
            pl.BlockSpec(kv.shape, lambda i, *_: (0, 0)),
            pl.BlockSpec((1, BQ), lambda i, *_: (0, i)),
            pl.BlockSpec((1, BQ), lambda i, *_: (0, i)),
        ],
        out_specs=[
            pl.BlockSpec((BQ, DH), lambda i, *_: (i, 0)),
            pl.BlockSpec((1, BQ), lambda i, *_: (0, i)),
        ],
    )

    def kernel(*refs):
        attn_fwd_kernel(origin, *refs)

    return pl.pallas_call(
        kernel,
        grid_spec=grid_spec,
        out_shape=[
            jax.ShapeDtypeStruct((frames, DH), BF),
            jax.ShapeDtypeStruct((1, frames), F32),
        ],
        compiler_params=pltpu.CompilerParams(vmem_limit_bytes=VMEM_BYTES),
        cost_estimate=pl.CostEstimate(
            flops=4 * pairs, bytes_accessed=4 * kv.size, transcendentals=frames * 1024
        ),
        name="attention_forward",
    )(low, high, c2, q, kv, lo_q, hi_q)


def attn_bwd_kernel(
    origin,
    low_ref,
    high_ref,
    c2_ref,
    q_ref,
    o_ref,
    do_ref,
    lse_ref,
    lo_ref,
    hi_ref,
    kv_ref,
    dq_ref,
    prev_ref,
    own_ref,
    next_ref,
    dk_acc,
    dv_acc,
):
    block = pl.program_id(0)
    rows = q_ref.shape[0]
    frames = own_ref.shape[0]
    scale = DH**-0.5
    c1 = LOG2E * scale

    @pl.when(block == 0)
    def _():
        dk_acc[...] = jnp.zeros_like(dk_acc)
        dv_acc[...] = jnp.zeros_like(dv_acc)

    q = q_ref[...]
    do = do_ref[...]
    c2 = c2_ref[0]
    delta = jnp.sum((o_ref[...].astype(F32) * do.astype(F32)).T, axis=0, keepdims=True)
    lse = lse_ref[...]
    at = lax.broadcasted_iota(jnp.int32, (1, rows), 1) + (origin + block * rows)
    q_pos = at.astype(F32)
    lo_q, hi_q = lo_ref[...], hi_ref[...]
    first = low_ref[block]
    steps = (high_ref[block] - first + (BK - 1)) // BK

    def step(t, dq):
        start = pl.multiple_of(first + t * BK, 128)
        here = pl.ds(start, BK)
        k = kv_ref[here, :DH]
        v = kv_ref[here, DH:]
        k_pos = (lax.broadcasted_iota(jnp.int32, (BK, 1), 0) + start).astype(F32)
        scores = dot_nt(k, q) * c1 - jnp.abs(k_pos - q_pos) * c2 - lse
        scores = jnp.where((k_pos >= lo_q) & (k_pos < hi_q), scores, MASKED)
        probs = jnp.exp2(scores)
        grads = (probs * (dot_nt(v, do) - delta)).astype(BF)
        dv_acc[here, :] += dot_nn(probs.astype(BF), do)
        dk_acc[here, :] += dot_nn(grads, q)
        return dq + dot_tn(k, grads)

    dq = lax.fori_loop(0, steps, step, jnp.zeros((DH, rows), F32))
    dq_ref[...] = (dq * scale).T.astype(BF)

    @pl.when(block == pl.num_programs(0) - 1)
    def _():
        prev_ref[:, :DH] = (dk_acc[:origin, :] * scale).astype(BF)
        prev_ref[:, DH:] = dv_acc[:origin, :].astype(BF)
        own_ref[:, :DH] = dk_acc[origin : origin + frames, :] * scale
        own_ref[:, DH:] = dv_acc[origin : origin + frames, :]
        next_ref[:, :DH] = (dk_acc[origin + frames : 2 * origin + frames, :] * scale).astype(BF)
        next_ref[:, DH:] = dv_acc[origin + frames : 2 * origin + frames, :].astype(BF)


def attn_bwd(q, o, do, lse, kv, low, high, c2, lo_q, hi_q, origin):
    frames = q.shape[0]
    blocks = frames // BQ
    pairs = frames * 1024 * DH
    tile = pl.BlockSpec((BQ, DH), lambda i, *_: (i, 0))
    row = pl.BlockSpec((1, BQ), lambda i, *_: (0, i))
    grid_spec = pltpu.PrefetchScalarGridSpec(
        num_scalar_prefetch=3,
        grid=(blocks,),
        in_specs=[
            tile,
            tile,
            tile,
            row,
            row,
            row,
            pl.BlockSpec(kv.shape, lambda i, *_: (0, 0)),
        ],
        out_specs=[
            tile,
            pl.BlockSpec((origin, 2 * DH), lambda i, *_: (0, 0)),
            pl.BlockSpec((frames, 2 * DH), lambda i, *_: (0, 0)),
            pl.BlockSpec((origin, 2 * DH), lambda i, *_: (0, 0)),
        ],
        scratch_shapes=[
            pltpu.VMEM((kv.shape[0], DH), F32),
            pltpu.VMEM((kv.shape[0], DH), F32),
        ],
    )

    def kernel(*refs):
        attn_bwd_kernel(origin, *refs)

    return pl.pallas_call(
        kernel,
        grid_spec=grid_spec,
        out_shape=[
            jax.ShapeDtypeStruct((frames, DH), BF),
            jax.ShapeDtypeStruct((origin, 2 * DH), BF),
            jax.ShapeDtypeStruct((frames, 2 * DH), F32),
            jax.ShapeDtypeStruct((origin, 2 * DH), BF),
        ],
        compiler_params=pltpu.CompilerParams(vmem_limit_bytes=VMEM_BYTES),
        cost_estimate=pl.CostEstimate(
            flops=10 * pairs, bytes_accessed=8 * kv.size, transcendentals=frames * 1024
        ),
        name="attention_backward",
    )(low, high, c2, q, o, do, lse, lo_q, hi_q, kv)


def halve(send, keep, axis, bit):
    return keep.astype(F32) + xor_send(send, axis, bit).astype(F32)


def finish_over_z(part):
    place = lax.axis_index("z")
    bit = 1
    while part.shape[0] > 1:
        pairs = part.reshape((part.shape[0] // 2, 2) + part.shape[1:])
        mine = (place // bit) % 2
        send = pick(pairs, 1 - mine, 1).astype(BF)
        part = halve(send, pick(pairs, mine, 1), "z", bit)
        bit *= 2
    return part[0]


def pair_up(cells):
    return xor_send(cells, "c", 1)


def ffn_grads(left, right, first):
    zs, xs = lax.axis_size("z"), lax.axis_size("x")
    width = left.shape[-1]
    rows = width // (zs * xs)
    x, y = lax.axis_index("x"), lax.axis_index("y")
    hidden = right.shape[-1]

    def product(one_x, one_y):
        lhs = left if one_x is None else pick(left.reshape(2, -1, zs, xs, rows), one_x, 3)
        lhs = lhs.reshape(2, lhs.shape[1], -1)
        out = [
            dot_tn(lhs[0], right[0, j]) + dot_tn(lhs[1], right[1, j])
            for j in range(right.shape[1])
        ] if one_y is None else None
        if one_y is not None:
            rhs = pick(right, one_y, 1)
            return dot_tn(lhs[0], rhs[0]) + dot_tn(lhs[1], rhs[1])
        return jnp.stack(out)

    if first == "x":
        part = halve(product(1 - x, None).astype(BF), product(x, None), "x", 1)
        part = halve(pick(part, 1 - y, 0).astype(BF), pick(part, y, 0), "y", 1)
    else:
        part = halve(product(None, 1 - y).astype(BF), product(None, y), "y", 1)
        part = part.reshape(zs, xs, rows, hidden)
        part = halve(pick(part, 1 - x, 1).astype(BF), pick(part, x, 1), "x", 1)
    return finish_over_z(part.reshape(zs, rows, hidden))


def row_grads(whole):
    zs = lax.axis_size("z")
    x, y, c = lax.axis_index("x"), lax.axis_index("y"), lax.axis_index("c")
    rows = whole.shape[0] // (8 * zs)
    part = whole.reshape(zs, 2, 2, 2, rows, whole.shape[1])
    part = halve(pick(part, 1 - c, 3).astype(BF), pick(part, c, 3), "c", 1)
    part = halve(pick(part, 1 - x, 1).astype(BF), pick(part, x, 1), "x", 1)
    part = halve(pick(part, 1 - y, 1).astype(BF), pick(part, y, 1), "y", 1)
    return finish_over_z(part)


def body(
    block_in,
    out_grad,
    utt_ends,
    valid_ends,
    ffn1_in,
    ffn1_out,
    att_qkv,
    att_out,
    content_bias,
    conv_in,
    conv_out,
    ffn2_in,
    ffn2_out,
    conv_depth,
    norm_gain,
    norm_bias,
):
    zs = lax.axis_size("z")
    devices = 8 * zs
    frames, width = block_in.shape
    heads = width // DH
    z, x, y, c = (lax.axis_index(axis) for axis in DEV)
    place = ((z * 2 + x) * 2 + y) * 2 + c
    head = (x * 2 + y) * 2 + c

    small = jnp.concatenate([norm_gain, norm_bias, conv_depth, content_bias[None]], axis=0)
    small = jnp.broadcast_to(small[None], (devices,) + small.shape)
    small = lax.all_to_all(small, DEV, split_axis=0, concat_axis=0, tiled=True)
    small = small.transpose(1, 0, 2).reshape(small.shape[1], width).astype(F32)
    gains, shifts, taps, q_bias = small[:6], small[6:12], small[12 : 12 + KSIZE], small[12 + KSIZE]

    def gather_ffn(w_in, w_out):
        both = jnp.concatenate([w_in, w_out.T], axis=1)
        return lax.all_gather(both, WIDE, axis=0, tiled=True).reshape(4, width, 2 * width)

    w_f1 = gather_ffn(ffn1_in, ffn1_out)
    w_qkv = lax.all_gather(att_qkv, DEV, axis=0, tiled=True)
    w_mid = lax.all_gather(jnp.concatenate([att_out, conv_in, conv_out], axis=1), DEV, axis=0, tiled=True)
    w_f2 = gather_ffn(ffn2_in, ffn2_out)
    w_att, w_cin, w_cout = w_mid[:, :width], w_mid[:, width : 3 * width], w_mid[:, 3 * width :]

    all_frames = frames * devices
    first_frame = place * frames
    span = 4 * frames
    group = 8 * frames
    origin = span
    group_first = z * group
    starts = jnp.concatenate([jnp.zeros((1,), jnp.int32), utt_ends[:-1]])
    valid_count = jnp.sum((valid_ends - starts).astype(F32))

    def segments(positions):
        seg = jnp.sum((utt_ends[None, :] <= positions[:, None]).astype(jnp.int32), axis=1)
        valid_seg = jnp.sum((valid_ends[None, :] <= positions[:, None]).astype(jnp.int32), axis=1)
        valid = seg == valid_seg
        return jnp.where(positions < 0, -1, jnp.where(positions >= all_frames, -2, seg)), valid

    ext_seg, ext_valid = segments(
        first_frame - REACH + jnp.arange(frames + 2 * REACH, dtype=jnp.int32)
    )
    own_seg = ext_seg[REACH : REACH + frames]
    valid_col = ext_valid[REACH : REACH + frames].astype(F32)[:, None]
    masks = [
        (ext_seg[m : m + frames] == own_seg).astype(F32)[:, None] for m in range(KSIZE)
    ]
    group_pos = group_first + jnp.arange(group, dtype=jnp.int32)
    ended = utt_ends[None, :] <= group_pos[:, None]
    group_seg = jnp.sum(ended.astype(jnp.int32), axis=1)
    group_lo = jnp.max(jnp.where(ended, utt_ends[None, :], 0), axis=1)
    slots = jnp.arange(utt_ends.shape[0], dtype=jnp.int32)
    group_hi = jnp.sum(
        jnp.where(group_seg[:, None] == slots[None, :], valid_ends[None, :], 0), axis=1
    )
    window_first = group_first - origin
    lo_q = group_lo - window_first
    hi_q = group_hi - window_first
    low = (lo_q[::BQ] // 128) * 128
    high = hi_q[BQ - 1 :: BQ]
    lo_q = lo_q.astype(F32)[None, :]
    hi_q = hi_q.astype(F32)[None, :]
    c2 = (32.0 * jnp.exp2(-head.astype(F32)) * (LOG2E / span))[None]

    def vectors(*rows):
        rows = jnp.stack(rows)
        return jnp.concatenate([rows, jnp.zeros((8 - rows.shape[0], width), F32)], axis=0)

    x1, n0, s1, d1, n2 = ffn_fwd(
        block_in, w_f1, vectors(gains[0], shifts[0], gains[1], shifts[1])
    )

    def for_sibling(first, slabs):
        theirs = pick(slabs.reshape((2, 2) + slabs.shape[1:]), 1 - c, 1)
        got = pair_up(jnp.concatenate([first[None], theirs], axis=0))
        own = pick(slabs.reshape((2, 2) + slabs.shape[1:]), c, 1)
        return jnp.stack([first, got[0]]), jnp.stack([own, got[1:]])

    n0_pair, s1_pair = for_sibling(n0, s1)

    projected = dot_nn(n2, w_qkv)
    queries = (projected[:, :width] + q_bias).astype(BF)
    key_vals = projected[:, width:].astype(BF).reshape(frames, 2, heads, DH)
    key_vals = key_vals.transpose(0, 2, 1, 3).reshape(frames, 2 * width)
    kv_own = lax.all_to_all(key_vals, LAYER, split_axis=1, concat_axis=0, tiled=True)
    up = [(i, i + 1) for i in range(zs - 1)]
    down = [(i + 1, i) for i in range(zs - 1)]
    kv_prev = lax.ppermute(kv_own[-span:], "z", up)
    kv_next = lax.ppermute(kv_own[:span], "z", down)
    q_own = lax.all_to_all(queries, LAYER, split_axis=1, concat_axis=0, tiled=True)
    kv = jnp.concatenate([kv_prev, kv_own, kv_next, jnp.zeros((BK, 2 * DH), BF)], axis=0)
    o_own, lse = attn_fwd(q_own, kv, low, high, c2, lo_q, hi_q, origin)
    mixed = lax.all_to_all(o_own, LAYER, split_axis=0, concat_axis=1, tiled=True)
    x2 = x1 + dot_nn(mixed, w_att)

    hat2, inv2 = norm_stats(x2)
    n3 = (hat2 * gains[2] + shifts[2]).astype(BF)
    pointwise = dot_nn(n3, w_cin)
    linear_half = pointwise[:, :width]
    gate = jax.nn.sigmoid(pointwise[:, width:])
    gated = neighbour_rows((linear_half * gate * valid_col).astype(BF))
    conv = jnp.zeros((frames, width), F32)
    for m in range(KSIZE):
        conv = conv + taps[m] * gated[m : m + frames].astype(F32) * masks[m]
    moments = sum_everywhere(
        jnp.stack([jnp.sum(valid_col * conv, axis=0), jnp.sum(valid_col * conv * conv, axis=0)])
    )
    mean_c = moments[0] / valid_count
    inv_batch = lax.rsqrt(moments[1] / valid_count - mean_c * mean_c + EPSILON)
    conv_hat = (conv - mean_c) * inv_batch
    batch_out = conv_hat * gains[3] + shifts[3]
    sig_bn = jax.nn.sigmoid(batch_out)
    swished = (batch_out * sig_bn).astype(BF)
    x3 = x2 + dot_nn(swished, w_cout)

    final_out, n4, s2, d2, dx4, sums5 = ffn_last(
        x3, w_f2, vectors(gains[4], shifts[4], gains[5], shifts[5]), out_grad
    )
    n4_pair, s2_pair = for_sibling(n4, s2)
    ef2, da2, dx3, sums4 = ffn_bwd(dx4, x3, w_f2, d2, vectors(gains[4]), F32)
    ef2_pair, da2_pair = for_sibling(ef2, da2)
    grad_f2i = ffn_grads(n4_pair, da2_pair, "x")
    grad_f2o = ffn_grads(ef2_pair, s2_pair, "y")

    ew = dx3.astype(BF)
    grad_cout = dot_tn(swished, ew)
    batch_grad = dot_nt(ew, w_cout) * (sig_bn * (1.0 + batch_out * (1.0 - sig_bn)))
    sums3 = jnp.stack([jnp.sum(batch_grad * conv_hat, axis=0), jnp.sum(batch_grad, axis=0)])
    totals = sum_everywhere(sums3 * gains[3])
    conv_grad = (
        inv_batch
        * (
            batch_grad * gains[3]
            - valid_col * (totals[1] + conv_hat * totals[0]) / valid_count
        )
    ).astype(BF)
    grad_ext = neighbour_rows(conv_grad)
    conv_grad_f = conv_grad.astype(F32)
    gated_grad = jnp.zeros((frames, width), F32)
    depth_rows = []
    for m in range(KSIZE):
        back = 2 * REACH - m
        gated_grad = gated_grad + taps[m] * grad_ext[back : back + frames].astype(F32) * masks[back]
        depth_rows.append(
            jnp.sum(conv_grad_f * gated[m : m + frames].astype(F32) * masks[m], axis=0)
        )
    glu_grad = gated_grad * valid_col
    point_grad = jnp.concatenate(
        [glu_grad * gate, glu_grad * linear_half * gate * (1.0 - gate)], axis=1
    ).astype(BF)
    grad_cin = dot_tn(n3, point_grad)
    dn3 = dot_nt(point_grad, w_cin)
    sums2 = jnp.stack([jnp.sum(dn3 * hat2, axis=0), jnp.sum(dn3, axis=0)])
    dx2 = dx3 + norm_back(dn3, hat2, inv2, gains[2])
    ey = dx2.astype(BF)
    grad_att = dot_tn(mixed, ey)
    mixed_grad = dot_nt(ey, w_att).astype(BF)
    do_own = lax.all_to_all(mixed_grad, LAYER, split_axis=1, concat_axis=0, tiled=True)
    mid = row_grads(jnp.concatenate([grad_att, grad_cin, grad_cout], axis=1))
    out_att, out_cin, out_cout = mid[:, :width], mid[:, width : 3 * width], mid[:, 3 * width :]

    dq, dkv_prev, dkv, dkv_next = attn_bwd(
        q_own, o_own, do_own, lse, kv, low, high, c2, lo_q, hi_q, origin
    )
    from_next = lax.ppermute(dkv_prev, "z", down).astype(F32)
    from_prev = lax.ppermute(dkv_next, "z", up).astype(F32)
    grad_query = lax.all_to_all(dq, LAYER, split_axis=0, concat_axis=1, tiled=True)
    dkv = jnp.concatenate(
        [dkv[:span] + from_prev, dkv[span:-span], dkv[-span:] + from_next], axis=0
    ).astype(BF)
    grad_kv = lax.all_to_all(dkv, LAYER, split_axis=0, concat_axis=1, tiled=True)
    grad_kv = grad_kv.reshape(frames, heads, 2, DH).transpose(0, 2, 1, 3).reshape(frames, 2 * width)
    proj_grad = jnp.concatenate([grad_query, grad_kv], axis=1)
    bias_grad = jnp.sum(grad_query.astype(F32), axis=0)

    dn2 = dot_nt(proj_grad, w_qkv)
    hat1, inv1 = norm_stats(x1)
    sums1 = jnp.stack([jnp.sum(dn2 * hat1, axis=0), jnp.sum(dn2, axis=0)])
    dx1 = dx2 + norm_back(dn2, hat1, inv1, gains[1])
    ef1, da1, grad_input, sums0 = ffn_bwd(dx1, block_in, w_f1, d1, vectors(gains[0]), BF)
    ef1_pair, da1_pair = for_sibling(ef1, da1)
    grad_f1o = ffn_grads(ef1_pair, s1_pair, "y")
    grad_f1i = ffn_grads(n0_pair, da1_pair, "x")
    out_qkv = row_grads(dot_tn(n2, proj_grad))

    rows = [sums0, sums1, sums2, sums3, sums4, sums5]
    rows = jnp.concatenate(
        [r[:1] for r in rows] + [r[1:] for r in rows] + [jnp.stack(depth_rows), bias_grad[None]],
        axis=0,
    )
    rows = rows.reshape(rows.shape[0], devices, width // devices).transpose(1, 0, 2)
    rows = jnp.sum(lax.all_to_all(rows, DEV, split_axis=0, concat_axis=0, tiled=True), axis=0)

    return (
        final_out,
        grad_input,
        grad_f1i,
        grad_f1o.T,
        out_qkv,
        out_att,
        rows[12 + KSIZE],
        out_cin,
        out_cout,
        grad_f2i,
        grad_f2o.T,
        rows[12 : 12 + KSIZE],
        rows[:6],
        rows[6:12],
    )


def solution(mesh):
    seq, heads = mesh.shape["seq"], mesh.shape["head"]
    grid = Mesh(mesh.devices.reshape(seq // 2, 2, heads // 2, 2), DEV)
    both = P(DEV, None)
    inward = P(("z", "x"), ("y", "c"))
    outward = P(("y", "c"), ("z", "x"))
    columns = P(None, DEV)
    return jax.shard_map(
        body,
        mesh=grid,
        in_specs=(
            both,
            both,
            P(),
            P(),
            inward,
            outward,
            both,
            both,
            P(DEV),
            both,
            both,
            inward,
            outward,
            columns,
            columns,
            columns,
        ),
        out_specs=(
            both,
            both,
            inward,
            outward,
            both,
            both,
            P(DEV),
            both,
            both,
            inward,
            outward,
            columns,
            columns,
            columns,
        ),
        check_vma=False,
    )
```

time: 2930 us -> 1110 us (0.38)
  waiting for transfers between devices: 1720 us -> 473 us
  blocking collectives: 362 us -> 0 us
  matrix products: 278 us -> 101 us
  local copies, waits for them, and re-layouts: 322 us -> 171 us
  Pallas kernels: 0 us -> 113 us
  starting transfers between devices: 49.2 us -> 101 us
  other arithmetic: 159 us -> 116 us
    reduce_scatter x8 -> x0, waiting for transfers between devices: 1330 us -> none  [the longest x1 187 us: body(): lax.psum_scatter(split_inward(grad_f1i, seq_count, head_count), ('seq', '...]
    dot_general x45 -> x36, matrix products: 278 us -> 101 us  [the longest x28 66.4 us: dot_tn(): lax.dot_general(a, b, (((0,), (0,)), ((), ())), preferred_element_type=F32)]
    all_gather x8 -> x4, waiting for transfers between devices: 111 us -> 280 us  [the longest x2 190 us: gather_ffn(): lax.all_gather(both, WIDE, axis=0, tiled=True).reshape(4, width, 2 * width)]
    unnamed x22 -> x4, waiting for transfers between devices: 152 us -> 0.74 us
    unnamed x2 -> x0, blocking collectives: 145 us -> none
    all_gather x3 -> x0, blocking collectives: 123 us -> none  [the longest x1 44.4 us: body(): lax.all_gather(norm_gain, ('seq', 'head'), axis=1, tiled=True)]
    pallas_call x0 -> x6, Pallas kernels: none -> 113 us  [the longest x1 29.4 us: attn_bwd(): pl.pallas_call(kernel, grid_spec=grid_spec, out_shape=[jax.ShapeDtypeStru...]
    ppermute x8 -> x38, waiting for transfers between devices: 60.8 us -> 159 us  [the longest x30 143 us: xor_send(): return lax.ppermute(cells, axis, [(i, i ^ bit) for i in range(count)])]
  transfers between devices with their start and end apart: 34 -> 52, of which waited for: 20 -> 21; matrix products, arithmetic and copies ran while one was open for 14% -> 30% of each run, Pallas kernels for 0% -> 8%
where the time goes in v1:
time: 1110 us; the launch traced here: 1090 us
  waiting for transfers between devices  473 us (43%)
  local copies, waits for them, and re-layouts  171 us (15%)
  other arithmetic  116 us (10%)
  Pallas kernels  113 us (10%)
  starting transfers between devices  101 us (9%)
  matrix products  101 us (9%)
  between operations  16.4 us (1%)
    all_gather x2, waiting for transfers between devices, gather_ffn(): lax.all_gather(both, WIDE, axis=0, tiled=True).reshape(4, width, 2 * width)  190 us
    ppermute x30, waiting for transfers between devices, xor_send(): return lax.ppermute(cells, axis, [(i, i ^ bit) for i in range(count)])  143 us
    dot_general x28, matrix products, dot_tn(): lax.dot_general(a, b, (((0,), (0,)), ((), ())), preferred_element_type=F32)  66.4 us
    all_gather x1, waiting for transfers between devices, body(): lax.all_gather(jnp.concatenate([att_out, conv_in, conv_out], axis=1), DEV...  55.9 us
    all_gather x2, local copies, waits for them, and re-layouts, gather_ffn(): lax.all_gather(both, WIDE, axis=0, tiled=True).reshape(4, width, 2 * width)  43.4 us
    all_gather x1, waiting for transfers between devices, body(): w_qkv = lax.all_gather(att_qkv, DEV, axis=0, tiled=True)  34.8 us
    add x20, other arithmetic, halve(): return keep.astype(F32) + xor_send(send, axis, bit).astype(F32)  33.9 us
    ppermute x30, starting transfers between devices, xor_send(): return lax.ppermute(cells, axis, [(i, i ^ bit) for i in range(count)])  33.7 us
  transfers between devices with their start and end apart: 52, of which 21 were waited for; matrix products, arithmetic and copies ran while one was open for 30% of the time, Pallas kernels for 8%

profile of v1, /device:TPU:0, one launch (start us, length us, event | category | flops | bytes accessed | tf_op | source)
XLA Modules:
  0.0 1092.8 jit_solution(1735930140370517522)
XLA Ops:
  30.6 130.9 %all-gather.5.cloned.1.call-done = bf16[4096,2048]{0,1:T(8,128)(2,1)} async-done(((bf16[128,2048]{0,1:T(8,128)(2,1)}), bf16[4096,2048]{0,1:T(8,128)(2,1)}) %all-gather.5.cloned.1.call-update) | async-done | bytes 16777232 | tf_op jit(solution)/shard_map/all_gather | solution.py:571
  161.5 21.1 %copy.172 = bf16[4096,2048]{1,0:T(8,128)(2,1)} copy(bf16[4096,2048]{0,1:T(8,128)(2,1)} %all-gather.5.cloned.1.call-done) | data formatting | bytes 33554432 | tf_op jit(solution)/shard_map/all_gather | solution.py:571
  182.6 14.8 %ffn_forward.1 = (f32[384,1024]{1,0:T(8,128)}, bf16[384,1024]{1,0:T(8,128)(2,1)}, bf16[4,384,1024]{2,1,0:T(8,128)(2,1)}, bf16[4,384,1024]{2,1,0:T(8,128)(2,1)}, bf16[384,1024]{1,0:T(8,128)(2,1)}) custom-call(bf16[384,1024]{1,0:T(8,128)(2,1)} %x_ref.3, bf16[4,1024,2048]{2,1,0:T(8,128)(2,1)} %bitcast.334, f32[8,1024]{1,0:T(8,128)} %concatenate.122.vec_ref), custom_call_target="tpu_custom_call" | custom-call | flops 6442450944 | bytes 29360128 | tf_op jit(solution)/shard_map/ffn_forward/pallas_call | solution.py:112
  197.4 34.8 %all-gather.7.cloned.1.call-done = bf16[1024,3072]{1,0:T(8,128)(2,1)} async-done(((bf16[32,3072]{1,0:T(8,128)(2,1)}), bf16[1024,3072]{1,0:T(8,128)(2,1)}) %all-gather.7.cloned.1.call-update) | async-done | bytes 6291472 | tf_op jit(solution)/shard_map/all_gather | solution.py:574
  248.9 19.4 %all-to-all-done.2 = bf16[384,8,256]{2,0,1:T(8,128)(2,1)S(1)} async-done(((bf16[384,8,256]{2,0,1:T(8,128)(2,1)}), bf16[384,8,256]{2,0,1:T(8,128)(2,1)S(1)}, u32[]{:S(2)}, u32[]{:S(2)}) %all-to-all-start.2) | async-done | bytes 1572896 | tf_op jit(solution)/shard_map/all_to_all | solution.py:639
  295.8 15.4 %collective-permute-done.1 = bf16[1536,256]{1,0:T(8,128)(2,1)} collective-permute-done((bf16[1536,256]{1,0:T(8,128)(2,1)}, bf16[1536,256]{1,0:T(8,128)(2,1)}, u32[]{:S(2)}, u32[]{:S(2)}) %collective-permute-start.1) | collective-permute-done | bytes 786464 | tf_op jit(solution)/shard_map/ppermute | solution.py:643
  311.2 9.5 maximum_maximum_fusion.refs_4_.refs_9_
  320.8 24.4 %attention_forward.1 = (bf16[3072,128]{1,0:T(8,128)(2,1)}, f32[1,3072]{1,0:T(1,128)}) custom-call(s32[12]{0:T(128)} %fusion.117.refs_0_, s32[12]{0:T(128)} %slice.427.refs_1_, f32[1]{0:T(128)} %bitcast.4.refs_2_, bf16[3072,128]{1,0:T(8,128)(2,1)} %bitcast.6.refs_3_, bf16[6656,256]{1,0:T(8,128)(2,1)} %maximum_maximum_fusion.refs_4_.refs_9_, ...), custom_call_target="tpu_custom_call" | custom-call | flops 1610612736 | bytes 6815744 | tf_op jit(solution)/shard_map/attention_forward/pallas_call | solution.py:344
  357.8 58.7 %all-gather.11.cloned.1.call-done = bf16[4096,2048]{0,1:T(8,128)(2,1)} async-done(((bf16[128,2048]{0,1:T(8,128)(2,1)}), bf16[4096,2048]{0,1:T(8,128)(2,1)}) %all-gather.11.cloned.1.call-update) | async-done | bytes 16777232 | tf_op jit(solution)/shard_map/all_gather | solution.py:571
  416.5 22.4 %copy.178 = bf16[4096,2048]{1,0:T(8,128)(2,1)} copy(bf16[4096,2048]{0,1:T(8,128)(2,1)} %all-gather.11.cloned.1.call-done) | data formatting | bytes 33554432 | tf_op jit(solution)/shard_map/all_gather | solution.py:571
  439.7 55.9 %all-gather.9.cloned.1.call-done = bf16[1024,4096]{1,0:T(8,128)(2,1)} async-done(((bf16[32,4096]{1,0:T(8,128)(2,1)}), bf16[1024,4096]{1,0:T(8,128)(2,1)}) %all-gather.9.cloned.1.call-update) | async-done | bytes 8388624 | tf_op jit(solution)/shard_map/all_gather | solution.py:575
  540.4 16.0 %ffn_last.1 = (bf16[384,1024]{1,0:T(8,128)(2,1)}, bf16[384,1024]{1,0:T(8,128)(2,1)}, bf16[4,384,1024]{2,1,0:T(8,128)(2,1)}, bf16[4,384,1024]{2,1,0:T(8,128)(2,1)...) custom-call(f32[384,1024]{1,0:T(8,128)} %fusion.52.x_ref, bf16[4,1024,2048]{2,1,0:T(8,128)(2,1)} %bitcast.336, ...), custom_call_target="tpu_custom_call" | custom-call | flops 6442450944 | bytes 29360128 | tf_op jit(solution)/shard_map/ffn_last/pallas_call | solution.py:182
  556.4 14.6 %ffn_backward.2 = (bf16[384,1024]{1,0:T(8,128)(2,1)}, bf16[4,384,1024]{2,1,0:T(8,128)(2,1)}, f32[384,1024]{1,0:T(8,128)}, f32[2,1024]{1,0:T(2,128)}) custom-call(f32[384,1024]{1,0:T(8,128)} %get-tuple-element.43.up_ref, f32[384,1024]{1,0:T(8,128)} %fusion.52.x_ref, bf16[4,1024,2048]{2,1,0:T(8,128)(2,1)} %bitcast.337, ...), custom_call_target="tpu_custom_call" | custom-call | flops 6442450944 | bytes 23068672 | tf_op jit(solution)/shard_map/ffn_backward/pallas_call | solution.py:248
  676.3 29.4 %attention_backward.1 = (bf16[3072,128]{1,0:T(8,128)(2,1)}, bf16[1536,256]{1,0:T(8,128)(2,1)}, f32[3072,256]{1,0:T(8,128)}, bf16[1536,256]{1,0:T(8,128)(2,1)}) custom-call(s32[12]{0:T(128)} %fusion.117.refs_0_, s32[12]{0:T(128)} %slice.427.refs_1_, f32[1]{0:T(128)} %bitcast.4.refs_2_, bf16[3072,128]{1,0:T(8,128)(2,1)} %bitcast.6.refs_3_, ...), custom_call_target="tpu_custom_call" | custom-call | flops 4026531840 | bytes 13631488 | tf_op jit(solution)/shard_map/attention_backward/pallas_call | solution.py:460
  716.4 11.6 %pad_maximum_fusion = f32[1024,4096]{1,0:T(8,128)} fusion(f32[1024,1024]{1,0:T(8,128)} %fusion.108, f32[1024,2048]{1,0:T(8,128)} %fusion.72, f32[1024,1024]{1,0:T(8,128)} %fusion.105), kind=kLoop, calls=%fused_computation | loop fusion | flops 8388608 | bytes 33554432 | tf_op jit(solution)/shard_map/concatenate | solution.py:713
  795.6 14.2 %ffn_backward.3 = (bf16[384,1024]{1,0:T(8,128)(2,1)}, bf16[4,384,1024]{2,1,0:T(8,128)(2,1)}, bf16[384,1024]{1,0:T(8,128)(2,1)}, f32[2,1024]{1,0:T(2,128)}) custom-call(f32[384,1024]{1,0:T(8,128)} %multiply_add_fusion.up_ref, bf16[384,1024]{1,0:T(8,128)(2,1)} %x_ref.3, bf16[4,1024,2048]{2,1,0:T(8,128)(2,1)} %bitcast.335, ...), custom_call_target="tpu_custom_call" | custom-call | flops 6442450944 | bytes 23068672 | tf_op jit(solution)/shard_map/ffn_backward/pallas_call | solution.py:248
  910.7 19.0 %collective-permute-done.37 = bf16[1,128,1024]{2,1,0:T(8,128)(2,1)S(1)} collective-permute-done((bf16[1,128,1024]{2,1,0:T(8,128)(2,1)S(1)}, bf16[1,128,1024]{2,1,0:T(8,128)(2,1)S(1)}, u32[]{:S(2)}, u32[]{:S(2)}) %collective-permute-start.37) | collective-permute-done | bytes 262176 | tf_op jit(solution)/shard_map/ppermute | solution.py:33
  945.8 28.5 %collective-permute-done.10 = bf16[2,512,1024]{2,1,0:T(8,128)(2,1)} collective-permute-done((bf16[2,512,1024]{2,1,0:T(8,128)(2,1)}, bf16[2,512,1024]{2,1,0:T(8,128)(2,1)}, u32[]{:S(2)}, u32[]{:S(2)}) %collective-permute-start.10) | collective-permute-done | bytes 2097184 | tf_op jit(solution)/shard_map/ppermute | solution.py:33
  983.4 17.6 %collective-permute-done.25 = bf16[4,32,4096]{2,1,0:T(8,128)(2,1)} collective-permute-done((bf16[4,32,4096]{2,1,0:T(8,128)(2,1)}, bf16[4,32,4096]{2,1,0:T(8,128)(2,1)}, u32[]{:S(2)}, u32[]{:S(2)}) %collective-permute-start.25) | collective-permute-done | bytes 1048608 | tf_op jit(solution)/shard_map/ppermute | solution.py:33
  1016.9 9.9 collective-permute-done.27
  1028.8 10.3 collective-permute-done.20
  1041.9 9.5 collective-permute-done.21
  1056.7 11.7 %collective-permute-done.16 = bf16[2,128,1024]{2,1,0:T(8,128)(2,1)S(1)} collective-permute-done((bf16[2,128,1024]{2,1,0:T(8,128)(2,1)S(1)}, bf16[2,128,1024]{2,1,0:T(8,128)(2,1)S(1)}, u32[]{:S(2)}, u32[]{:S(2)}) %collective-permute-start.16) | collective-permute-done | bytes 524320 | tf_op jit(solution)/shard_map/ppermute | solution.py:33
  1069.5 14.4 %collective-permute-done.17 = bf16[1,128,1024]{2,1,0:T(8,128)(2,1)S(1)} collective-permute-done((bf16[1,128,1024]{2,1,0:T(8,128)(2,1)S(1)}, bf16[1,128,1024]{2,1,0:T(8,128)(2,1)S(1)}, u32[]{:S(2)}, u32[]{:S(2)}) %collective-permute-start.17) | collective-permute-done | bytes 262176 | tf_op jit(solution)/shard_map/ppermute | solution.py:33
  (573 shorter events, 462.4 us)
Async XLA Ops:
  7.2 154.3 %all-gather.5.cloned.1.call-start = ((), (), s32[]{:S(2)}) async-start(), calls=%async_computation.10 | async-start | bytes 17301504 | tf_op jit(solution)/shard_map/all_gather | solution.py:571
  10.3 221.9 %all-gather.7.cloned.1.call-start = ((), (), s32[]{:S(2)}) async-start(), calls=%async_computation.11 | async-start | bytes 6488064 | tf_op jit(solution)/shard_map/all_gather | solution.py:574
  11.0 405.5 %all-gather.11.cloned.1.call-start = ((), (), s32[]{:S(2)}) async-start(), calls=%async_computation.13 | async-start | bytes 17301504 | tf_op jit(solution)/shard_map/all_gather | solution.py:571
  12.1 483.5 %all-gather.9.cloned.1.call-start = ((), (), s32[]{:S(2)}) async-start(), calls=%async_computation.12 | async-start | bytes 8650752 | tf_op jit(solution)/shard_map/all_gather | solution.py:575
  269.5 41.7 %collective-permute-start.1 = (bf16[1536,256]{1,0:T(8,128)(2,1)}, bf16[1536,256]{1,0:T(8,128)(2,1)}, u32[]{:S(2)}, u32[]{:S(2)}) collective-permute-start(bf16[1536,256]{1,0:T(8,128)(2,1)} %bitcast.11), channel_id=1, source_target_pairs={{8,0},{16,8},{24,16},{9,1},{17,9},{25,17},{10,2},{18,10},{26,18},{... | collective-permute-start | bytes 2359304 | tf_op jit(solution)/shard_map/ppermute | solution.py:643
  270.8 40.4 %collective-permute-start = (bf16[1536,256]{1,0:T(8,128)(2,1)}, bf16[1536,256]{1,0:T(8,128)(2,1)}, u32[]{:S(2)}, u32[]{:S(2)}) collective-permute-start(bf16[1536,256]{1,0:T(8,128)(2,1)} %bitcast.9), channel_id=1, source_target_pairs={{0,8},{8,16},{16,24},{1,9},{9,17},{17,25},{2,10},{10,18},{18,26},{... | collective-permute-start | bytes 2359304 | tf_op jit(solution)/shard_map/ppermute | solution.py:642
  291.3 29.4 %all-to-all-start.1 = ((bf16[384,8,128]{2,0,1:T(8,128)(2,1)}), bf16[384,8,128]{2,0,1:T(8,128)(2,1)}, u32[]{:S(2)}, u32[]{:S(2)}) async-start(bf16[384,8,128]{2,0,1:T(8,128)(2,1)} %copy_bitcast_fusion.2), calls=%async_computation.1 | async-start | bytes 1572864 | tf_op jit(solution)/shard_map/all_to_all | solution.py:644
  347.6 148.0 %all-to-all-start.3 = ((bf16[8,384,128]{1,2,0:T(8,128)(2,1)}), bf16[8,384,128]{1,2,0:T(8,128)(2,1)}, u32[]{:S(2)}, u32[]{:S(2)}) async-start(bf16[8,384,128]{1,2,0:T(8,128)(2,1)} %copy.175), calls=%async_computation.3 | async-start | bytes 1572864 | tf_op jit(solution)/shard_map/all_to_all | solution.py:647
  357.0 149.2 %collective-permute-start.8 = (bf16[3,384,1024]{1,2,0:T(8,128)(2,1)}, bf16[3,384,1024]{1,2,0:T(8,128)(2,1)}, u32[]{:S(2)}, u32[]{:S(2)}) collective-permute-start(bf16[3,384,1024]{1,2,0:T(8,128)(2,1)} %pad_maximum_fusion.2), channel_id=1, source_target_pairs={{0,1},{1,0},{2,3},{3,2},{4,5},{5,4},{6,7},{7,6},{8,9},{9,8},{10,11... | collective-permute-start | bytes 7077896 | tf_op jit(solution)/shard_map/ppermute | solution.py:33
  630.9 122.1 %collective-permute-start.29 = (bf16[3,384,1024]{2,1,0:T(8,128)(2,1)}, bf16[3,384,1024]{2,1,0:T(8,128)(2,1)}, u32[]{:S(2)}, u32[]{:S(2)}) collective-permute-start(bf16[3,384,1024]{2,1,0:T(8,128)(2,1)} %pad_maximum_fusion.5), channel_id=1, source_target_pairs={{0,1},{1,0},{2,3},{3,2},{4,5},{5,4},{6,7},{7,6},{8,9},{9,8},{10,11... | collective-permute-start | bytes 7077896 | tf_op jit(solution)/shard_map/ppermute | solution.py:33
  634.5 113.4 %collective-permute-start.28 = (bf16[3,384,1024]{1,2,0:T(8,128)(2,1)}, bf16[3,384,1024]{1,2,0:T(8,128)(2,1)}, u32[]{:S(2)}, u32[]{:S(2)}) collective-permute-start(bf16[3,384,1024]{1,2,0:T(8,128)(2,1)} %pad_maximum_fusion.4), channel_id=1, source_target_pairs={{0,1},{1,0},{2,3},{3,2},{4,5},{5,4},{6,7},{7,6},{8,9},{9,8},{10,11... | collective-permute-start | bytes 7077896 | tf_op jit(solution)/shard_map/ppermute | solution.py:33
  736.2 123.7 %collective-permute-start.23 = (bf16[4,2,2,32,4096]{4,3,0,2,1:T(8,128)(2,1)}, bf16[4,2,2,32,4096]{4,3,0,2,1:T(8,128)(2,1)}, u32[]{:S(2)}, u32[]{:S(2)}) collective-permute-start(bf16[4,2,2,32,4096]{4,3,0,2,1:T(8,128)(2,1)} %fusion), channel_id=1, source_target_pairs={{0,1},{1,0},{2,3},{3,2},{4,5},{5,4},{6,7},{7,6},{8,9},{9,8},{10,11... | collective-permute-start | bytes 12582920 | tf_op jit(solution)/shard_map/ppermute | solution.py:33
  743.3 38.2 %all-to-all-start.8 = ((bf16[8,384,256]{2,1,0:T(8,128)(2,1)}), bf16[8,384,256]{2,1,0:T(8,128)(2,1)S(1)}, u32[]{:S(2)}, u32[]{:S(2)}) async-start(bf16[8,384,256]{2,1,0:T(8,128)(2,1)} %bitcast.358), calls=%async_computation.8 | async-start | bytes 3145728 | tf_op jit(solution)/shard_map/all_to_all | solution.py:725
  757.5 89.9 %collective-permute-start.30 = (bf16[2,512,1024]{2,1,0:T(8,128)(2,1)}, bf16[2,512,1024]{2,1,0:T(8,128)(2,1)}, u32[]{:S(2)}, u32[]{:S(2)}) collective-permute-start(bf16[2,512,1024]{2,1,0:T(8,128)(2,1)} %pad_maximum_fusion.7), channel_id=1, source_target_pairs={{0,4},{4,0},{1,5},{5,1},{2,6},{6,2},{3,7},{7,3},{8,12},{12,8},{9,1... | collective-permute-start | bytes 6291464 | tf_op jit(solution)/shard_map/ppermute | solution.py:33
  767.3 85.9 %collective-permute-start.34 = (bf16[1024,1024]{1,0:T(8,128)(2,1)}, bf16[1024,1024]{1,0:T(8,128)(2,1)}, u32[]{:S(2)}, u32[]{:S(2)}) collective-permute-start(bf16[1024,1024]{1,0:T(8,128)(2,1)} %add_convert_fusion), channel_id=1, source_target_pairs={{0,2},{2,0},{1,3},{3,1},{4,6},{6,4},{5,7},{7,5},{8,10},{10,8},{9,1... | collective-permute-start | bytes 6291464 | tf_op jit(solution)/shard_map/ppermute | solution.py:33
  822.0 66.1 %collective-permute-start.9 = (bf16[3,384,1024]{2,1,0:T(8,128)(2,1)}, bf16[3,384,1024]{2,1,0:T(8,128)(2,1)}, u32[]{:S(2)}, u32[]{:S(2)}) collective-permute-start(bf16[3,384,1024]{2,1,0:T(8,128)(2,1)} %pad_maximum_fusion.3), channel_id=1, source_target_pairs={{0,1},{1,0},{2,3},{3,2},{4,5},{5,4},{6,7},{7,6},{8,9},{9,8},{10,11... | collective-permute-start | bytes 7077896 | tf_op jit(solution)/shard_map/ppermute | solution.py:33
  843.8 90.4 %collective-permute-start.18 = (bf16[4,2,2,32,3072]{4,3,0,2,1:T(8,128)(2,1)}, bf16[4,2,2,32,3072]{4,3,0,2,1:T(8,128)(2,1)}, u32[]{:S(2)}, u32[]{:S(2)}) collective-permute-start(bf16[4,2,2,32,3072]{4,3,0,2,1:T(8,128)(2,1)} %fusion.5), channel_id=1, source_target_pairs={{0,1},{1,0},{2,3},{3,2},{4,5},{5,4},{6,7},{7,6},{8,9},{9,8},{10,11... | collective-permute-start | bytes 9437192 | tf_op jit(solution)/shard_map/ppermute | solution.py:33
  867.5 74.4 %collective-permute-start.24 = (bf16[4,2,32,4096]{3,2,0,1:T(8,128)(2,1)}, bf16[4,2,32,4096]{3,2,0,1:T(8,128)(2,1)}, u32[]{:S(2)}, u32[]{:S(2)}) collective-permute-start(bf16[4,2,32,4096]{3,2,0,1:T(8,128)(2,1)} %fusion.6), channel_id=1, source_target_pairs={{0,4},{4,0},{1,5},{5,1},{2,6},{6,2},{3,7},{7,3},{8,12},{12,8},{9,1... | collective-permute-start | bytes 6291464 | tf_op jit(solution)/shard_map/ppermute | solution.py:33
  893.4 80.9 %collective-permute-start.10 = (bf16[2,512,1024]{2,1,0:T(8,128)(2,1)}, bf16[2,512,1024]{2,1,0:T(8,128)(2,1)}, u32[]{:S(2)}, u32[]{:S(2)}) collective-permute-start(bf16[2,512,1024]{2,1,0:T(8,128)(2,1)} %pad_maximum_fusion.6), channel_id=1, source_target_pairs={{0,4},{4,0},{1,5},{5,1},{2,6},{6,2},{3,7},{7,3},{8,12},{12,8},{9,1... | collective-permute-start | bytes 6291464 | tf_op jit(solution)/shard_map/ppermute | solution.py:33
  929.7 49.3 %collective-permute-start.14 = (bf16[1024,1024]{1,0:T(8,128)(2,1)}, bf16[1024,1024]{1,0:T(8,128)(2,1)}, u32[]{:S(2)}, u32[]{:S(2)}) collective-permute-start(bf16[1024,1024]{1,0:T(8,128)(2,1)} %add_convert_fusion.1), channel_id=1, source_target_pairs={{0,2},{2,0},{1,3},{3,1},{4,6},{6,4},{5,7},{7,5},{8,10},{10,8},{9,1... | collective-permute-start | bytes 6291464 | tf_op jit(solution)/shard_map/ppermute | solution.py:33
  940.4 67.6 %collective-permute-start.19 = (bf16[4,2,32,3072]{3,2,0,1:T(8,128)(2,1)}, bf16[4,2,32,3072]{3,2,0,1:T(8,128)(2,1)}, u32[]{:S(2)}, u32[]{:S(2)}) collective-permute-start(bf16[4,2,32,3072]{3,2,0,1:T(8,128)(2,1)} %fusion.24), channel_id=1, source_target_pairs={{0,4},{4,0},{1,5},{5,1},{2,6},{6,2},{3,7},{7,3},{8,12},{12,8},{9,1... | collective-permute-start | bytes 4718600 | tf_op jit(solution)/shard_map/ppermute | solution.py:33
  945.2 55.8 %collective-permute-start.25 = (bf16[4,32,4096]{2,1,0:T(8,128)(2,1)}, bf16[4,32,4096]{2,1,0:T(8,128)(2,1)}, u32[]{:S(2)}, u32[]{:S(2)}) collective-permute-start(bf16[4,32,4096]{2,1,0:T(8,128)(2,1)} %fusion.68), channel_id=1, source_target_pairs={{0,2},{2,0},{1,3},{3,1},{4,6},{6,4},{5,7},{7,5},{8,10},{10,8},{9,1... | collective-permute-start | bytes 3145736 | tf_op jit(solution)/shard_map/ppermute | solution.py:33
  977.1 51.2 %collective-permute-start.11 = (bf16[512,1024]{1,0:T(8,128)(2,1)S(1)}, bf16[512,1024]{1,0:T(8,128)(2,1)S(1)}, u32[]{:S(2)}, u32[]{:S(2)}) collective-permute-start(bf16[512,1024]{1,0:T(8,128)(2,1)S(1)} %fusion.67), channel_id=1, source_target_pairs={{0,2},{2,0},{1,3},{3,1},{4,6},{6,4},{5,7},{7,5},{8,10},{10,8},{9,1... | collective-permute-start | bytes 3145736 | tf_op jit(solution)/shard_map/ppermute | solution.py:33
  981.9 57.5 %collective-permute-start.15 = (bf16[4,128,1024]{2,1,0:T(8,128)(2,1)S(1)}, bf16[4,128,1024]{2,1,0:T(8,128)(2,1)S(1)}, u32[]{:S(2)}, u32[]{:S(2)}) collective-permute-start(bf16[4,128,1024]{2,1,0:T(8,128)(2,1)S(1)} %fusion.70), channel_id=1, source_target_pairs={{0,4},{4,0},{1,5},{5,1},{2,6},{6,2},{3,7},{7,3},{8,12},{12,8},{9,1... | collective-permute-start | bytes 3145736 | tf_op jit(solution)/shard_map/ppermute | solution.py:33
  (144 other events, 3347.0 us)
Sparse Core Ops, SparseCore 0:
  11.5 149.9 all-gather.4
  164.4 67.7 all-gather.6
  235.6 180.8 all-gather.10
  419.8 75.7 all-gather.8

commit v2 on v1

v2 whole, which is shorter than its diff:
```python
import functools
import math

import jax
import jax.numpy as jnp
from jax import lax
from jax.experimental import pallas as pl
from jax.experimental.pallas import tpu as pltpu
from jax.sharding import Mesh
from jax.sharding import PartitionSpec as P

DH = 128
KSIZE = 5
REACH = (KSIZE - 1) // 2
EPSILON = 1e-05
MASKED = -1e30
LOG2E = math.log2(math.e)
DEV = ("z", "x", "y", "c")
LAYER = ("x", "y", "c")
BQ = 256
BK = 512
BF = jnp.bfloat16
F32 = jnp.float32
VMEM_BYTES = 56 * 1024 * 1024


def pick(cells, index, dim):
    return lax.dynamic_index_in_dim(cells, index, dim, keepdims=False)


def xor_send(cells, axis, bit):
    count = lax.axis_size(axis)
    return lax.ppermute(cells, axis, [(i, i ^ bit) for i in range(count)])


def neighbour_rows(tail, head=None):
    if head is None:
        tail, head = tail[-REACH:], tail[:REACH]
    count = 1
    for axis in DEV:
        count *= lax.axis_size(axis)
    before = lax.ppermute(tail, DEV, [(i, i + 1) for i in range(count - 1)])
    after = lax.ppermute(head, DEV, [(i + 1, i) for i in range(count - 1)])
    return before, after


def dot_nn(a, b):
    return lax.dot_general(a, b, (((1,), (0,)), ((), ())), preferred_element_type=F32)


def dot_nt(a, b):
    return lax.dot_general(a, b, (((1,), (1,)), ((), ())), preferred_element_type=F32)


def dot_tn(a, b):
    return lax.dot_general(a, b, (((0,), (0,)), ((), ())), preferred_element_type=F32)


def norm_stats(values):
    centred = values - jnp.mean(values, axis=-1, keepdims=True)
    inv_std = lax.rsqrt(jnp.mean(centred * centred, axis=-1, keepdims=True) + EPSILON)
    return centred * inv_std, inv_std


def norm_back(upstream, normed, inv_std, gain):
    scaled = upstream * gain
    inner = (
        scaled
        - jnp.mean(scaled, axis=-1, keepdims=True)
        - normed * jnp.mean(scaled * normed, axis=-1, keepdims=True)
    )
    return inv_std * inner


def pack_kernel(extra, in_ref, out_ref, *refs):
    rows = in_ref.shape[0]
    refs[extra][:rows] = in_ref[...]
    refs[extra][rows:] = out_ref[...].T


def pack_ffn(w_in, w_out, order=()):
    rows, width = w_in.shape
    whole = lambda v: pl.BlockSpec(v.shape, lambda: (0, 0))
    if rows % 128:
        return jnp.concatenate([w_in, w_out.T], axis=0)
    return pl.pallas_call(
        functools.partial(pack_kernel, len(order)),
        in_specs=[whole(w_in), whole(w_out)] + [pl.BlockSpec(memory_space=pl.ANY)] * len(order),
        out_specs=pl.BlockSpec((2 * rows, width), lambda: (0, 0)),
        out_shape=jax.ShapeDtypeStruct((2 * rows, width), BF),
        name="pack_ffn",
    )(w_in, w_out, *order)


class Rows:
    def __init__(self, gathered, first, count):
        self.stepped = count % 16 == 0 and first % count == 0
        devices, _, width = gathered.shape
        self.count = count
        if self.stepped:
            self.at = first // count
            self.array = gathered
            self.block = (devices, count, width)
        else:
            self.first = first
            self.gathered = gathered
            self.width = width

    def blocks(self, pick_block, total):
        if self.stepped:
            at = self.at
            return self.array, pl.BlockSpec(self.block, lambda j, *_: (0, at + pick_block(j), 0))
        cut = [
            self.gathered[:, self.first + i * self.count : self.first + (i + 1) * self.count]
            for i in range(total)
        ]
        cut = jnp.stack([v.reshape(-1, self.width) for v in cut])
        return cut, pl.BlockSpec((1,) + cut.shape[1:], lambda j, *_: (pick_block(j), 0, 0))


def square(ref):
    return ref[...].reshape(-1, ref.shape[-1])


def slab_of(step, core):
    return (step % 2) * 2 + jnp.where(step < 2, 1 - core, core)


def slab_specs(gathered, rows, step_of):
    devices, total, width = gathered.shape
    array = gathered.reshape(devices // 4, 4, total, width)
    block = (devices // 4, 1, rows, width)
    specs = [
        pl.BlockSpec(block, lambda j, c, i=i: (0, slab_of(step_of(j), c[0]), i, 0)) for i in (0, 1)
    ]
    return [array, array], specs


def heads_of(ref, lo, hi):
    return jnp.concatenate([ref[h, :, lo:hi] for h in range(ref.shape[0])], axis=1)


def forward_slab(n, w1_ref, w2_ref, s_ref, d_out):
    width = n.shape[1]
    w1 = square(w1_ref)
    chunk = 256
    for at in range(0, width, chunk):
        a = dot_nn(n, w1[:, at : at + chunk])
        sig = jax.nn.sigmoid(a)
        s_ref[:, at : at + chunk] = (a * sig).astype(BF)
        d_out[:, at : at + chunk] = (sig * (1.0 + a * (1.0 - sig))).astype(BF)
    return dot_nt(s_ref[...], square(w2_ref))


def backward_slab(ef, w1_ref, w2_ref, d_in, da_ref):
    width = ef.shape[1]
    w2 = square(w2_ref)
    chunk = 256
    for at in range(0, width, chunk):
        ds = dot_nn(ef, w2[:, at : at + chunk])
        da_ref[:, at : at + chunk] = (ds * d_in[:, at : at + chunk].astype(F32)).astype(BF)
    return dot_nt(da_ref[...], square(w1_ref))


def keep_slab(step, cells, pack_ref, pack_at, own_ref):
    @pl.when(step < 2)
    def _():
        pack_ref[pack_at + step] = cells

    @pl.when(step >= 2)
    def _():
        own_ref[0] = cells


def first_kernel(
    core_ref,
    x_ref,
    w1_ref,
    w2_ref,
    wp_ref,
    vec_ref,
    x1_ref,
    n2_ref,
    pack_ref,
    own_ref,
    d_ref,
    q_ref,
    k_ref,
    v_ref,
    acc_ref,
    s_ref,
):
    step = pl.program_id(0)

    @pl.when(step == 0)
    def _():
        normed, _ = norm_stats(x_ref[...].astype(F32))
        pack_ref[0] = (normed * vec_ref[0:1, :] + vec_ref[1:2, :]).astype(BF)
        acc_ref[...] = jnp.zeros_like(acc_ref)

    @pl.when(step < 4)
    def _():
        acc_ref[...] += forward_slab(pack_ref[0], w1_ref, w2_ref, s_ref, d_ref.at[0])
        keep_slab(step, s_ref[...], pack_ref, 1, own_ref)

    @pl.when(step == 3)
    def _():
        x1 = x_ref[...].astype(F32) + 0.5 * acc_ref[...]
        x1_ref[...] = x1
        normed, _ = norm_stats(x1)
        n2_ref[...] = (normed * vec_ref[2:3, :] + vec_ref[3:4, :]).astype(BF)

    for part, ref in enumerate((q_ref, k_ref, v_ref)):

        @pl.when(step == 4 + part)
        def _():
            projected = dot_nn(n2_ref[...], square(wp_ref))
            if part == 0:
                projected = projected + vec_ref[4:5, :]
            projected = projected.astype(BF)
            for h in range(ref.shape[0]):
                ref[h] = projected[:, h * DH : (h + 1) * DH]


def first_call(core, x, gathered, rows, proj, vectors):
    frames, width = x.shape
    heads = width // DH
    fixed = lambda *shape: pl.BlockSpec(shape, lambda j, c: (0,) * len(shape))
    slabs, slab_blocks = slab_specs(gathered, rows, lambda j: jnp.minimum(j, 3))
    proj_array, proj_block = proj.blocks(lambda j: jnp.clip(j - 4, 0, 2), 3)
    return pl.pallas_call(
        first_kernel,
        grid_spec=pltpu.PrefetchScalarGridSpec(
            num_scalar_prefetch=1,
            grid=(7,),
            in_specs=[fixed(frames, width)] + slab_blocks + [proj_block, fixed(*vectors.shape)],
            out_specs=[
                fixed(frames, width),
                fixed(frames, width),
                fixed(3, frames, width),
                pl.BlockSpec((1, frames, width), lambda j, c: (jnp.clip(j - 2, 0, 1), 0, 0)),
                pl.BlockSpec((1, frames, width), lambda j, c: (jnp.minimum(j, 3), 0, 0)),
                fixed(heads, frames, DH),
                fixed(heads, frames, DH),
                fixed(heads, frames, DH),
            ],
            scratch_shapes=[pltpu.VMEM((frames, width), F32), pltpu.VMEM((frames, width), BF)],
        ),
        out_shape=[
            jax.ShapeDtypeStruct((frames, width), F32),
            jax.ShapeDtypeStruct((frames, width), BF),
            jax.ShapeDtypeStruct((3, frames, width), BF),
            jax.ShapeDtypeStruct((2, frames, width), BF),
            jax.ShapeDtypeStruct((4, frames, width), BF),
            jax.ShapeDtypeStruct((heads, frames, DH), BF),
            jax.ShapeDtypeStruct((heads, frames, DH), BF),
            jax.ShapeDtypeStruct((heads, frames, DH), BF),
        ],
        compiler_params=pltpu.CompilerParams(vmem_limit_bytes=VMEM_BYTES),
        cost_estimate=pl.CostEstimate(
            flops=22 * frames * width * width,
            bytes_accessed=22 * width * width + 40 * frames * width,
            transcendentals=4 * frames * width,
        ),
        name="first_part",
    )(core, x, *slabs, proj_array, vectors)


def gate_kernel(
    mh_ref,
    x1_ref,
    w_ref,
    vec_ref,
    cols_ref,
    mixed_ref,
    x2_ref,
    n3_ref,
    lin_ref,
    sig_ref,
    g_ref,
):
    step = pl.program_id(0)

    @pl.when(step == 0)
    def _():
        mixed = heads_of(mh_ref, 0, DH)
        mixed_ref[...] = mixed
        x2 = x1_ref[...] + dot_nn(mixed, square(w_ref))
        x2_ref[...] = x2
        normed, _ = norm_stats(x2)
        n3_ref[...] = (normed * vec_ref[0:1, :] + vec_ref[1:2, :]).astype(BF)

    @pl.when(step == 1)
    def _():
        lin_ref[...] = dot_nn(n3_ref[...], square(w_ref))

    @pl.when(step == 2)
    def _():
        sig = jax.nn.sigmoid(dot_nn(n3_ref[...], square(w_ref)))
        sig_ref[...] = sig
        g_ref[...] = (lin_ref[...] * sig * cols_ref[:, KSIZE : KSIZE + 1]).astype(BF)


def gate_call(mixed_heads, x1, weights, vectors, columns):
    frames, width = x1.shape
    fixed = lambda *shape: pl.BlockSpec(shape, lambda j: (0,) * len(shape))
    array, block = weights.blocks(lambda j: j, 3)
    return pl.pallas_call(
        gate_kernel,
        grid=(3,),
        in_specs=[
            fixed(*mixed_heads.shape),
            fixed(frames, width),
            block,
            fixed(*vectors.shape),
            fixed(*columns.shape),
        ],
        out_specs=[fixed(frames, width)] * 6,
        out_shape=[jax.ShapeDtypeStruct((frames, width), t) for t in (BF, F32, BF, F32, F32, BF)],
        compiler_params=pltpu.CompilerParams(vmem_limit_bytes=VMEM_BYTES),
        cost_estimate=pl.CostEstimate(
            flops=6 * frames * width * width,
            bytes_accessed=6 * width * width + 24 * frames * width,
            transcendentals=frames * width,
        ),
        name="attention_out_and_gate",
    )(mixed_heads, x1, array, vectors, columns)


PAD = 8


def lay_out(scratch, before, cells, after):
    frames = cells.shape[0]
    scratch[PAD - REACH : PAD, :] = before
    scratch[PAD : PAD + frames, :] = cells
    scratch[PAD + frames : PAD + frames + REACH, :] = after


def conv_kernel(g_ref, before_ref, after_ref, vec_ref, cols_ref, conv_ref, sums_ref, ext):
    frames = g_ref.shape[0]
    lay_out(
        ext, before_ref[...].astype(F32), g_ref[...].astype(F32), after_ref[...].astype(F32)
    )
    conv = jnp.zeros(g_ref.shape, F32)
    for m in range(KSIZE):
        rows = ext[PAD - REACH + m : PAD - REACH + m + frames, :]
        conv = conv + vec_ref[m : m + 1, :] * rows * cols_ref[:, m : m + 1]
    conv_ref[...] = conv
    counted = conv * cols_ref[:, KSIZE : KSIZE + 1]
    sums = jnp.concatenate(
        [jnp.sum(counted, axis=0, keepdims=True), jnp.sum(counted * conv, axis=0, keepdims=True)]
    )
    sums_ref[...] = jnp.broadcast_to(sums[None], sums_ref.shape)


def conv_call(g, before, after, taps, columns, devices):
    frames, width = g.shape
    return pl.pallas_call(
        conv_kernel,
        out_shape=[
            jax.ShapeDtypeStruct((frames, width), F32),
            jax.ShapeDtypeStruct((devices, 2, width), F32),
        ],
        scratch_shapes=[pltpu.VMEM((frames + 2 * PAD, width), F32)],
        compiler_params=pltpu.CompilerParams(vmem_limit_bytes=VMEM_BYTES),
        cost_estimate=pl.CostEstimate(
            flops=20 * frames * width, bytes_accessed=8 * frames * width, transcendentals=0
        ),
        name="depthwise",
    )(g, before, after, taps, columns)


def batch_stats(moments_ref, count):
    sums = jnp.sum(moments_ref[...], axis=0)
    mean = sums[0:1, :] / count
    return mean, lax.rsqrt(sums[1:2, :] / count - mean * mean + EPSILON)


def second_kernel(
    core_ref,
    x2_ref,
    conv_ref,
    mom_ref,
    wc_ref,
    w1_ref,
    w2_ref,
    vec_ref,
    og_ref,
    out_ref,
    swish_ref,
    dx_ref,
    ew_ref,
    dz_ref,
    sums_ref,
    spread_ref,
    pack_ref,
    s_own_ref,
    da_own_ref,
    x3_ref,
    acc_ref,
    d_ref,
    dsilu_ref,
    s_ref,
    dx4_ref,
):
    step = pl.program_id(0)
    count = vec_ref[6:7, :]

    @pl.when(step == 0)
    def _():
        mean, inv = batch_stats(mom_ref, count)
        z = (conv_ref[...] - mean) * inv * vec_ref[0:1, :] + vec_ref[1:2, :]
        sig = jax.nn.sigmoid(z)
        swish = (z * sig).astype(BF)
        swish_ref[...] = swish
        dsilu_ref[...] = sig * (1.0 + z * (1.0 - sig))
        x3 = x2_ref[...] + dot_nn(swish, square(wc_ref))
        x3_ref[...] = x3
        normed, _ = norm_stats(x3)
        pack_ref[0] = (normed * vec_ref[2:3, :] + vec_ref[3:4, :]).astype(BF)
        acc_ref[...] = jnp.zeros_like(acc_ref)

    @pl.when(step < 4)
    def _():
        acc_ref[...] += forward_slab(pack_ref[0], w1_ref, w2_ref, s_ref, d_ref.at[step])
        keep_slab(step, s_ref[...], pack_ref, 1, s_own_ref)

    @pl.when(step == 3)
    def _():
        normed, inv_std = norm_stats(x3_ref[...] + 0.5 * acc_ref[...])
        gain = vec_ref[4:5, :]
        out_ref[...] = (normed * gain + vec_ref[5:6, :]).astype(BF)
        upstream = og_ref[...].astype(F32)
        dx4 = norm_back(upstream, normed, inv_std, gain)
        dx4_ref[...] = dx4
        pack_ref[3] = (0.5 * dx4).astype(BF)
        sums_ref[0:1, :] = jnp.sum(upstream * normed, axis=0, keepdims=True)
        sums_ref[1:2, :] = jnp.sum(upstream, axis=0, keepdims=True)
        acc_ref[...] = jnp.zeros_like(acc_ref)

    @pl.when(step >= 4)
    def _():
        acc_ref[...] += backward_slab(pack_ref[3], w1_ref, w2_ref, d_ref.at[step - 4], s_ref)
        keep_slab(step - 4, s_ref[...], pack_ref, 4, da_own_ref)

    @pl.when(step == 7)
    def _():
        normed, inv_std = norm_stats(x3_ref[...])
        dn = acc_ref[...]
        dx3 = dx4_ref[...] + norm_back(dn, normed, inv_std, vec_ref[2:3, :])
        dx_ref[...] = dx3
        sums_ref[2:3, :] = jnp.sum(dn * normed, axis=0, keepdims=True)
        sums_ref[3:4, :] = jnp.sum(dn, axis=0, keepdims=True)
        ew = dx3.astype(BF)
        ew_ref[...] = ew
        dz = dot_nt(ew, square(wc_ref)) * dsilu_ref[...]
        dz_ref[...] = dz
        mean, inv = batch_stats(mom_ref, count)
        zhat = (conv_ref[...] - mean) * inv
        totals = jnp.concatenate(
            [jnp.sum(dz * zhat, axis=0, keepdims=True), jnp.sum(dz, axis=0, keepdims=True)]
        )
        sums_ref[4:6, :] = totals
        sums_ref[6:8, :] = jnp.zeros((2, dz.shape[1]), F32)
        spread_ref[...] = jnp.broadcast_to(totals[None], spread_ref.shape)


def second_call(core, x2, conv, moments, weights, gathered, rows, vectors, out_grad):
    frames, width = x2.shape
    fixed = lambda *shape: pl.BlockSpec(shape, lambda j, c: (0,) * len(shape))
    slabs, slab_blocks = slab_specs(gathered, rows, lambda j: j % 4)
    array, block = weights.blocks(lambda j: 0, 1)
    whole = fixed(frames, width)
    return pl.pallas_call(
        second_kernel,
        grid_spec=pltpu.PrefetchScalarGridSpec(
            num_scalar_prefetch=1,
            grid=(8,),
            in_specs=[whole, whole, fixed(*moments.shape), block]
            + slab_blocks
            + [fixed(*vectors.shape), whole],
            out_specs=[
                whole,
                whole,
                whole,
                whole,
                whole,
                fixed(8, width),
                fixed(*moments.shape),
                fixed(6, frames, width),
                pl.BlockSpec((1, frames, width), lambda j, c: (jnp.clip(j - 2, 0, 1), 0, 0)),
                pl.BlockSpec((1, frames, width), lambda j, c: (jnp.clip(j - 6, 0, 1), 0, 0)),
            ],
            scratch_shapes=[
                pltpu.VMEM((frames, width), F32),
                pltpu.VMEM((frames, width), F32),
                pltpu.VMEM((4, frames, width), BF),
                pltpu.VMEM((frames, width), F32),
                pltpu.VMEM((frames, width), BF),
                pltpu.VMEM((frames, width), F32),
            ],
        ),
        out_shape=[
            jax.ShapeDtypeStruct((frames, width), BF),
            jax.ShapeDtypeStruct((frames, width), BF),
            jax.ShapeDtypeStruct((frames, width), F32),
            jax.ShapeDtypeStruct((frames, width), BF),
            jax.ShapeDtypeStruct((frames, width), F32),
            jax.ShapeDtypeStruct((8, width), F32),
            jax.ShapeDtypeStruct(moments.shape, F32),
            jax.ShapeDtypeStruct((6, frames, width), BF),
            jax.ShapeDtypeStruct((2, frames, width), BF),
            jax.ShapeDtypeStruct((2, frames, width), BF),
        ],
        compiler_params=pltpu.CompilerParams(vmem_limit_bytes=VMEM_BYTES),
        cost_estimate=pl.CostEstimate(
            flops=36 * frames * width * width,
            bytes_accessed=34 * width * width + 40 * frames * width,
            transcendentals=5 * frames * width,
        ),
        name="second_part",
    )(core, x2, conv, moments, array, *slabs, vectors, out_grad)


def back_kernel(
    extra,
    dz_ref,
    conv_ref,
    edge_before_ref,
    edge_after_ref,
    g_ref,
    g_before_ref,
    g_after_ref,
    mom_ref,
    tot_ref,
    lin_ref,
    sig_ref,
    x2_ref,
    dx3_ref,
    w_ref,
    vec_ref,
    cols_ref,
    *refs,
):
    pg_ref, dx2_ref, ey_ref, do_ref, sums_ref, ext, g_ext, acc_ref, b_ref = refs[extra:]
    step = pl.program_id(0)
    frames, width = dz_ref.shape

    @pl.when(step == 0)
    def _():
        count = vec_ref[8:9, :]
        gain = vec_ref[5:6, :]
        mean, inv = batch_stats(mom_ref, count)
        totals = jnp.sum(tot_ref[...], axis=0) * gain

        def conv_grad(dz, conv, valid):
            zhat = (conv - mean) * inv
            dc = inv * (dz * gain - valid * (totals[1:2, :] + zhat * totals[0:1, :]) / count)
            return dc.astype(BF).astype(F32)

        valid = cols_ref[:, KSIZE : KSIZE + 1]
        dc = conv_grad(dz_ref[...], conv_ref[...], valid)
        edges = []
        for at, ref in ((0, edge_before_ref), (REACH, edge_after_ref)):
            edges.append(
                conv_grad(
                    ref[0:REACH, :],
                    ref[REACH : 2 * REACH, :],
                    cols_ref[at : at + REACH, KSIZE + 1 : KSIZE + 2],
                )
            )
        lay_out(ext, edges[0], dc, edges[1])
        lay_out(
            g_ext,
            g_before_ref[...].astype(F32),
            g_ref[...].astype(F32),
            g_after_ref[...].astype(F32),
        )
        dg = jnp.zeros((frames, width), F32)
        for m in range(KSIZE):
            back = 2 * REACH - m
            rows = ext[PAD - REACH + back : PAD - REACH + back + frames, :]
            dg = dg + vec_ref[m : m + 1, :] * rows * cols_ref[:, back : back + 1]
            there = g_ext[PAD - REACH + m : PAD - REACH + m + frames, :]
            sums_ref[2 + m : 3 + m, :] = jnp.sum(
                dc * there * cols_ref[:, m : m + 1], axis=0, keepdims=True
            )
        sums_ref[7:8, :] = jnp.zeros((1, width), F32)
        de = dg * valid
        sig = sig_ref[...]
        pa = (de * sig).astype(BF)
        pb = (de * lin_ref[...] * sig * (1.0 - sig)).astype(BF)
        pg_ref[:, :width] = pa
        pg_ref[:, width:] = pb
        b_ref[...] = pb
        acc_ref[...] = dot_nt(pa, square(w_ref))

    @pl.when(step == 1)
    def _():
        dn = acc_ref[...] + dot_nt(b_ref[...], square(w_ref))
        normed, inv_std = norm_stats(x2_ref[...])
        dx2 = dx3_ref[...] + norm_back(dn, normed, inv_std, vec_ref[6:7, :])
        dx2_ref[...] = dx2
        ey_ref[...] = dx2.astype(BF)
        sums_ref[0:1, :] = jnp.sum(dn * normed, axis=0, keepdims=True)
        sums_ref[1:2, :] = jnp.sum(dn, axis=0, keepdims=True)

    @pl.when(step == 2)
    def _():
        grads = dot_nt(ey_ref[...], square(w_ref)).astype(BF)
        for h in range(do_ref.shape[0]):
            do_ref[h] = grads[:, h * DH : (h + 1) * DH]


def back_call(dz, conv, edges, g, g_edges, moments, totals, lin, sig, x2, dx3, weights, vectors, columns, order):
    frames, width = dz.shape
    fixed = lambda *shape: pl.BlockSpec(shape, lambda j: (0,) * len(shape))
    array, block = weights.blocks(lambda j: (j + 1) % 3, 3)
    whole = fixed(frames, width)
    return pl.pallas_call(
        functools.partial(back_kernel, len(order)),
        grid=(3,),
        in_specs=[
            whole,
            whole,
            fixed(2 * REACH, width),
            fixed(2 * REACH, width),
            whole,
            fixed(REACH, width),
            fixed(REACH, width),
            fixed(*moments.shape),
            fixed(*totals.shape),
            whole,
            whole,
            whole,
            whole,
            block,
            fixed(*vectors.shape),
            fixed(*columns.shape),
        ]
        + [pl.BlockSpec(memory_space=pl.ANY)] * len(order),
        out_specs=[
            fixed(frames, 2 * width),
            whole,
            whole,
            fixed(width // DH, frames, DH),
            fixed(8, width),
        ],
        out_shape=[
            jax.ShapeDtypeStruct((frames, 2 * width), BF),
            jax.ShapeDtypeStruct((frames, width), F32),
            jax.ShapeDtypeStruct((frames, width), BF),
            jax.ShapeDtypeStruct((width // DH, frames, DH), BF),
            jax.ShapeDtypeStruct((8, width), F32),
        ],
        scratch_shapes=[
            pltpu.VMEM((frames + 2 * PAD, width), F32),
            pltpu.VMEM((frames + 2 * PAD, width), F32),
            pltpu.VMEM((frames, width), F32),
            pltpu.VMEM((frames, width), BF),
        ],
        compiler_params=pltpu.CompilerParams(vmem_limit_bytes=VMEM_BYTES),
        cost_estimate=pl.CostEstimate(
            flops=6 * frames * width * width,
            bytes_accessed=6 * width * width + 34 * frames * width,
            transcendentals=0,
        ),
        name="convolution_backward",
    )(
        dz,
        conv,
        edges[0],
        edges[1],
        g,
        g_edges[0],
        g_edges[1],
        moments,
        totals,
        lin,
        sig,
        x2,
        dx3,
        array,
        vectors,
        columns,
        *order,
    )


def proj_back_kernel(extra, dq_ref, dkv_ref, dx2_ref, x1_ref, wp_ref, vec_ref, *refs):
    dx1_ref, ef_ref, sums_ref, acc_ref = refs[extra:]
    step = pl.program_id(0)

    @pl.when(step == 0)
    def _():
        dq = heads_of(dq_ref, 0, DH)
        acc_ref[...] = dot_nt(dq, square(wp_ref))
        sums_ref[2:3, :] = jnp.sum(dq.astype(F32), axis=0, keepdims=True)
        sums_ref[3:8, :] = jnp.zeros((5, dq.shape[1]), F32)

    @pl.when(step == 1)
    def _():
        acc_ref[...] += dot_nt(heads_of(dkv_ref, 0, DH), square(wp_ref))

    @pl.when(step == 2)
    def _():
        dn = acc_ref[...] + dot_nt(heads_of(dkv_ref, DH, 2 * DH), square(wp_ref))
        normed, inv_std = norm_stats(x1_ref[...])
        dx1 = dx2_ref[...] + norm_back(dn, normed, inv_std, vec_ref[1:2, :])
        dx1_ref[...] = dx1
        ef_ref[0] = (0.5 * dx1).astype(BF)
        sums_ref[0:1, :] = jnp.sum(dn * normed, axis=0, keepdims=True)
        sums_ref[1:2, :] = jnp.sum(dn, axis=0, keepdims=True)


def proj_back_call(dq, dkv, dx2, x1, proj, vectors, order):
    frames, width = x1.shape
    fixed = lambda *shape: pl.BlockSpec(shape, lambda j: (0,) * len(shape))
    array, block = proj.blocks(lambda j: j, 3)
    whole = fixed(frames, width)
    return pl.pallas_call(
        functools.partial(proj_back_kernel, len(order)),
        grid=(3,),
        in_specs=[fixed(*dq.shape), fixed(*dkv.shape), whole, whole, block, fixed(*vectors.shape)]
        + [pl.BlockSpec(memory_space=pl.ANY)] * len(order),
        out_specs=[whole, fixed(1, frames, width), fixed(8, width)],
        out_shape=[
            jax.ShapeDtypeStruct((frames, width), F32),
            jax.ShapeDtypeStruct((1, frames, width), BF),
            jax.ShapeDtypeStruct((8, width), F32),
        ],
        scratch_shapes=[pltpu.VMEM((frames, width), F32)],
        compiler_params=pltpu.CompilerParams(vmem_limit_bytes=VMEM_BYTES),
        cost_estimate=pl.CostEstimate(flops=1024, bytes_accessed=1024, transcendentals=0),
        name="projections_backward",
    )(dq, dkv, dx2, x1, array, vectors, *order)


def last_kernel(extra, core_ref, dx1_ref, ef_ref, x_ref, w1_ref, w2_ref, d_ref, vec_ref, *refs):
    gin_ref, sums_ref, first_ref, second_ref, own_ref, acc_ref, da_ref = refs[extra:]
    step = pl.program_id(0)

    @pl.when(step == 0)
    def _():
        acc_ref[...] = jnp.zeros_like(acc_ref)

    acc_ref[...] += backward_slab(ef_ref[0], w1_ref, w2_ref, d_ref.at[0], da_ref)
    for at, ref in enumerate((first_ref, second_ref)):

        @pl.when(step == at)
        def _():
            ref[0] = da_ref[...]

    @pl.when(step >= 2)
    def _():
        own_ref[0] = da_ref[...]

    @pl.when(step == 3)
    def _():
        normed, inv_std = norm_stats(x_ref[...].astype(F32))
        dn = acc_ref[...]
        dx = dx1_ref[...] + norm_back(dn, normed, inv_std, vec_ref[0:1, :])
        gin_ref[...] = dx.astype(BF)
        sums_ref[0:1, :] = jnp.sum(dn * normed, axis=0, keepdims=True)
        sums_ref[1:2, :] = jnp.sum(dn, axis=0, keepdims=True)
        sums_ref[2:8, :] = jnp.zeros((6, dn.shape[1]), F32)


def last_call(core, dx1, ef, x, gathered, rows, slope, vectors, order):
    frames, width = x.shape
    fixed = lambda *shape: pl.BlockSpec(shape, lambda j, c: (0,) * len(shape))
    slabs, slab_blocks = slab_specs(gathered, rows, lambda j: j)
    whole = fixed(frames, width)
    return pl.pallas_call(
        functools.partial(last_kernel, len(order)),
        grid_spec=pltpu.PrefetchScalarGridSpec(
            num_scalar_prefetch=1,
            grid=(4,),
            in_specs=[whole, fixed(1, frames, width), whole]
            + slab_blocks
            + [pl.BlockSpec((1, frames, width), lambda j, c: (j, 0, 0)), fixed(*vectors.shape)]
            + [pl.BlockSpec(memory_space=pl.ANY)] * len(order),
            out_specs=[
                whole,
                fixed(8, width),
                fixed(1, frames, width),
                fixed(1, frames, width),
                pl.BlockSpec((1, frames, width), lambda j, c: (jnp.clip(j - 2, 0, 1), 0, 0)),
            ],
            scratch_shapes=[pltpu.VMEM((frames, width), F32), pltpu.VMEM((frames, width), BF)],
        ),
        out_shape=[
            jax.ShapeDtypeStruct((frames, width), BF),
            jax.ShapeDtypeStruct((8, width), F32),
            jax.ShapeDtypeStruct((1, frames, width), BF),
            jax.ShapeDtypeStruct((1, frames, width), BF),
            jax.ShapeDtypeStruct((2, frames, width), BF),
        ],
        compiler_params=pltpu.CompilerParams(vmem_limit_bytes=VMEM_BYTES),
        cost_estimate=pl.CostEstimate(flops=1024, bytes_accessed=1024, transcendentals=0),
        name="last_part",
    )(core, dx1, ef, x, *slabs, slope, vectors, *order)


def fill_window(kv_ref, parts):
    for column, refs in ((0, parts[:3]), (DH, parts[3:])):
        at = 0
        for ref in refs:
            kv_ref[at : at + ref.shape[0], column : column + DH] = ref[...]
            at += ref.shape[0]
    kv_ref[at:, :] = jnp.zeros((kv_ref.shape[0] - at, kv_ref.shape[1]), kv_ref.dtype)


def attn_fwd_kernel(
    origin,
    low_ref,
    high_ref,
    c2_ref,
    q_ref,
    *refs,
):
    lo_ref, hi_ref, o_ref, lse_ref, kv_ref = refs[6:]
    block = pl.program_id(0)

    @pl.when(block == 0)
    def _():
        fill_window(kv_ref, refs[:6])

    rows = q_ref.shape[0]
    q = q_ref[...]
    c1 = LOG2E * DH**-0.5
    c2 = c2_ref[0]
    at = lax.broadcasted_iota(jnp.int32, (1, rows), 1) + (origin + block * rows)
    q_pos = at.astype(F32)
    lo_q, hi_q = lo_ref[...], hi_ref[...]
    first = low_ref[block]
    steps = (high_ref[block] - first + (BK - 1)) // BK

    def step(t, carry):
        top, total, mixed = carry
        start = pl.multiple_of(first + t * BK, 128)
        k = kv_ref[pl.ds(start, BK), :DH]
        v = kv_ref[pl.ds(start, BK), DH:]
        k_pos = (lax.broadcasted_iota(jnp.int32, (BK, 1), 0) + start).astype(F32)
        scores = dot_nt(k, q) * c1 - jnp.abs(k_pos - q_pos) * c2
        scores = jnp.where((k_pos >= lo_q) & (k_pos < hi_q), scores, MASKED)
        new_top = jnp.maximum(top, jnp.max(scores, axis=0, keepdims=True))
        expo = jnp.exp2(scores - new_top)
        keep = jnp.exp2(top - new_top)
        total = total * keep + jnp.sum(expo, axis=0, keepdims=True)
        mixed = mixed * keep + dot_tn(v, expo.astype(BF))
        return new_top, total, mixed

    top, total, mixed = lax.fori_loop(
        0,
        steps,
        step,
        (
            jnp.full((1, rows), MASKED, F32),
            jnp.zeros((1, rows), F32),
            jnp.zeros((DH, rows), F32),
        ),
    )
    o_ref[...] = (mixed / total).T.astype(BF)
    lse_ref[...] = top + jnp.log2(total)


def attn_fwd(q, kv, low, high, c2, lo_q, hi_q, origin):
    frames = q.shape[0]
    window = sum(v.shape[0] for v in kv[:3]) + BK
    parts = [pl.BlockSpec(v.shape, lambda i, *_: (0, 0)) for v in kv]
    blocks = frames // BQ
    pairs = frames * 1024 * DH
    grid_spec = pltpu.PrefetchScalarGridSpec(
        num_scalar_prefetch=3,
        grid=(blocks,),
        in_specs=[
            pl.BlockSpec((BQ, DH), lambda i, *_: (i, 0)),
            *parts,
            pl.BlockSpec((1, BQ), lambda i, *_: (0, i)),
            pl.BlockSpec((1, BQ), lambda i, *_: (0, i)),
        ],
        out_specs=[
            pl.BlockSpec((BQ, DH), lambda i, *_: (i, 0)),
            pl.BlockSpec((1, BQ), lambda i, *_: (0, i)),
        ],
        scratch_shapes=[pltpu.VMEM((window, 2 * DH), BF)],
    )

    def kernel(*refs):
        attn_fwd_kernel(origin, *refs)

    return pl.pallas_call(
        kernel,
        grid_spec=grid_spec,
        out_shape=[
            jax.ShapeDtypeStruct((frames, DH), BF),
            jax.ShapeDtypeStruct((1, frames), F32),
        ],
        compiler_params=pltpu.CompilerParams(vmem_limit_bytes=VMEM_BYTES),
        cost_estimate=pl.CostEstimate(
            flops=4 * pairs, bytes_accessed=4 * window * DH, transcendentals=frames * 1024
        ),
        name="attention_forward",
    )(low, high, c2, q, *kv, lo_q, hi_q)


def attn_bwd_kernel(
    origin,
    extra,
    low_ref,
    high_ref,
    c2_ref,
    q_ref,
    o_ref,
    do_ref,
    lse_ref,
    lo_ref,
    hi_ref,
    *refs,
):
    dq_ref, prev_ref, own_ref, next_ref, dk_acc, dv_acc, kv_ref = refs[6 + extra :]
    block = pl.program_id(0)
    rows = q_ref.shape[0]
    frames = own_ref.shape[0]
    scale = DH**-0.5
    c1 = LOG2E * scale

    @pl.when(block == 0)
    def _():
        fill_window(kv_ref, refs[:6])
        dk_acc[...] = jnp.zeros_like(dk_acc)
        dv_acc[...] = jnp.zeros_like(dv_acc)

    q = q_ref[...]
    do = do_ref[...]
    c2 = c2_ref[0]
    delta = jnp.sum((o_ref[...].astype(F32) * do.astype(F32)).T, axis=0, keepdims=True)
    lse = lse_ref[...]
    at = lax.broadcasted_iota(jnp.int32, (1, rows), 1) + (origin + block * rows)
    q_pos = at.astype(F32)
    lo_q, hi_q = lo_ref[...], hi_ref[...]
    first = low_ref[block]
    steps = (high_ref[block] - first + (BK - 1)) // BK

    def step(t, dq):
        start = pl.multiple_of(first + t * BK, 128)
        here = pl.ds(start, BK)
        k = kv_ref[here, :DH]
        v = kv_ref[here, DH:]
        k_pos = (lax.broadcasted_iota(jnp.int32, (BK, 1), 0) + start).astype(F32)
        scores = dot_nt(k, q) * c1 - jnp.abs(k_pos - q_pos) * c2 - lse
        scores = jnp.where((k_pos >= lo_q) & (k_pos < hi_q), scores, MASKED)
        probs = jnp.exp2(scores)
        grads = (probs * (dot_nt(v, do) - delta)).astype(BF)
        dv_acc[here, :] += dot_nn(probs.astype(BF), do)
        dk_acc[here, :] += dot_nn(grads, q)
        return dq + dot_tn(k, grads)

    dq = lax.fori_loop(0, steps, step, jnp.zeros((DH, rows), F32))
    dq_ref[...] = (dq * scale).T.astype(BF)

    @pl.when(block == pl.num_programs(0) - 1)
    def _():
        prev_ref[:, :DH] = (dk_acc[:origin, :] * scale).astype(BF)
        prev_ref[:, DH:] = dv_acc[:origin, :].astype(BF)
        own_ref[:, :DH] = dk_acc[origin : origin + frames, :] * scale
        own_ref[:, DH:] = dv_acc[origin : origin + frames, :]
        next_ref[:, :DH] = (dk_acc[origin + frames : 2 * origin + frames, :] * scale).astype(BF)
        next_ref[:, DH:] = dv_acc[origin + frames : 2 * origin + frames, :].astype(BF)


def attn_bwd(q, o, do, lse, kv, low, high, c2, lo_q, hi_q, origin, order=()):
    frames = q.shape[0]
    blocks = frames // BQ
    pairs = frames * 1024 * DH
    window = sum(v.shape[0] for v in kv[:3]) + BK
    parts = [pl.BlockSpec(v.shape, lambda i, *_: (0, 0)) for v in kv]
    tile = pl.BlockSpec((BQ, DH), lambda i, *_: (i, 0))
    row = pl.BlockSpec((1, BQ), lambda i, *_: (0, i))
    grid_spec = pltpu.PrefetchScalarGridSpec(
        num_scalar_prefetch=3,
        grid=(blocks,),
        in_specs=[
            tile,
            tile,
            tile,
            row,
            row,
            row,
            *parts,
        ]
        + [pl.BlockSpec(memory_space=pl.ANY)] * len(order),
        out_specs=[
            tile,
            pl.BlockSpec((origin, 2 * DH), lambda i, *_: (0, 0)),
            pl.BlockSpec((frames, 2 * DH), lambda i, *_: (0, 0)),
            pl.BlockSpec((origin, 2 * DH), lambda i, *_: (0, 0)),
        ],
        scratch_shapes=[
            pltpu.VMEM((window, DH), F32),
            pltpu.VMEM((window, DH), F32),
            pltpu.VMEM((window, 2 * DH), BF),
        ],
    )

    def kernel(*refs):
        attn_bwd_kernel(origin, len(order), *refs)

    return pl.pallas_call(
        kernel,
        grid_spec=grid_spec,
        out_shape=[
            jax.ShapeDtypeStruct((frames, DH), BF),
            jax.ShapeDtypeStruct((origin, 2 * DH), BF),
            jax.ShapeDtypeStruct((frames, 2 * DH), F32),
            jax.ShapeDtypeStruct((origin, 2 * DH), BF),
        ],
        compiler_params=pltpu.CompilerParams(vmem_limit_bytes=VMEM_BYTES),
        cost_estimate=pl.CostEstimate(
            flops=80 * pairs, bytes_accessed=8 * window * DH, transcendentals=frames * 1024
        ),
        name="attention_backward",
    )(low, high, c2, q, o, do, lse, lo_q, hi_q, *kv, *order)


def pass_on_kernel(extra, *refs):
    count = (len(refs) - extra) // 2
    for a, b in zip(refs[:count], refs[count + extra :]):
        b[...] = a[...]


def pass_on(arrays, order):
    return pl.pallas_call(
        functools.partial(pass_on_kernel, len(order)),
        in_specs=[pl.BlockSpec(v.shape, lambda n=v.ndim: (0,) * n) for v in arrays]
        + [pl.BlockSpec(memory_space=pl.ANY)] * len(order),
        out_specs=[pl.BlockSpec(v.shape, lambda n=v.ndim: (0,) * n) for v in arrays],
        out_shape=[jax.ShapeDtypeStruct(v.shape, v.dtype) for v in arrays],
        compiler_params=pltpu.CompilerParams(vmem_limit_bytes=VMEM_BYTES // 3),
        cost_estimate=pl.CostEstimate(flops=1, bytes_accessed=1024, transcendentals=0),
        name="pass_on",
    )(*arrays, *order)


def join_kernel(extra, own_ref, before_ref, after_ref, *refs):
    out_ref = refs[extra]
    span = before_ref.shape[0]
    rows = own_ref.shape[0]
    out_ref[:span, :] = (own_ref[:span, :] + before_ref[...].astype(F32)).astype(BF)
    if rows > 2 * span:
        out_ref[span : rows - span, :] = own_ref[span : rows - span, :].astype(BF)
    out_ref[rows - span :, :] = (own_ref[rows - span :, :] + after_ref[...].astype(F32)).astype(BF)


def join_edges(own, before, after, order=()):
    return pl.pallas_call(
        functools.partial(join_kernel, len(order)),
        in_specs=[pl.BlockSpec(v.shape, lambda: (0, 0)) for v in (own, before, after)]
        + [pl.BlockSpec(memory_space=pl.ANY)] * len(order),
        out_specs=pl.BlockSpec(own.shape, lambda: (0, 0)),
        out_shape=jax.ShapeDtypeStruct(own.shape, BF),
        compiler_params=pltpu.CompilerParams(vmem_limit_bytes=VMEM_BYTES // 2),
        cost_estimate=pl.CostEstimate(
            flops=own.size, bytes_accessed=8 * own.size, transcendentals=0
        ),
        name="join_edges",
    )(own, before, after, *order)


def stack_kernel(extra, places, *refs):
    out_ref = refs[-1]
    for at, (source, row) in enumerate(places):
        out_ref[at : at + 1, :] = refs[source][row : row + 1, :]


def stack_rows(arrays, places, order=()):
    width = arrays[0].shape[1]
    return pl.pallas_call(
        functools.partial(stack_kernel, len(order), places),
        in_specs=[pl.BlockSpec(v.shape, lambda: (0, 0)) for v in arrays]
        + [pl.BlockSpec(memory_space=pl.ANY)] * len(order),
        out_specs=pl.BlockSpec((len(places), width), lambda: (0, 0)),
        out_shape=jax.ShapeDtypeStruct((len(places), width), F32),
        name="stack_rows",
    )(*arrays, *order)


def halve_kernel(extra, sel_ref, kept_a, kept_b, got_a, got_b, *refs):
    send_ref, keep_ref = refs[extra:]
    send_ref[...] = (kept_a[0].astype(F32) + got_a[0].astype(F32)).astype(BF)
    keep_ref[...] = (kept_b[0].astype(F32) + got_b[0].astype(F32)).astype(BF)


def halve(kept, got, mine, order=()):
    count, _, rows, columns = kept.shape
    step = rows
    while step % 32 == 0 and step * columns > 512 * 1024:
        step //= 2
    block = (1, 1, step, columns)
    other = pl.BlockSpec(block, lambda i, j, m: (i, 1 - m[0], j, 0))
    own = pl.BlockSpec(block, lambda i, j, m: (i, m[0], j, 0))
    out = pl.BlockSpec((1, step, columns), lambda i, j, m: (i, j, 0))
    return pl.pallas_call(
        functools.partial(halve_kernel, len(order)),
        grid_spec=pltpu.PrefetchScalarGridSpec(
            num_scalar_prefetch=1,
            grid=(count, rows // step),
            in_specs=[other, own, other, own]
            + [pl.BlockSpec(memory_space=pl.ANY)] * len(order),
            out_specs=[out, out],
        ),
        out_shape=[jax.ShapeDtypeStruct((count, rows, columns), BF)] * 2,
        compiler_params=pltpu.CompilerParams(vmem_limit_bytes=VMEM_BYTES // 3),
        cost_estimate=pl.CostEstimate(flops=1024, bytes_accessed=1024, transcendentals=0),
        name="halve",
    )(mine.astype(jnp.int32)[None], kept, kept, got, got, *order)


def finish_kernel(extra, turned, kept_ref, got_ref, *refs):
    total = kept_ref[...].astype(F32) + got_ref[...].astype(F32)
    refs[extra][...] = total.T if turned else total


def finish(kept, got, turned=False, order=()):
    rows, columns = kept.shape
    fixed = pl.BlockSpec((rows, columns), lambda: (0, 0))
    shape = (columns, rows) if turned else (rows, columns)
    if turned and rows % 128:
        return finish(kept, got, False, order).T
    return pl.pallas_call(
        functools.partial(finish_kernel, len(order), turned),
        in_specs=[fixed, fixed] + [pl.BlockSpec(memory_space=pl.ANY)] * len(order),
        out_specs=pl.BlockSpec(shape, lambda: (0, 0)),
        out_shape=jax.ShapeDtypeStruct(shape, F32),
        compiler_params=pltpu.CompilerParams(vmem_limit_bytes=VMEM_BYTES // 3),
        name="finish",
    )(kept, got, *order)


class Sum:
    def __init__(self, kept, send, axis, bit):
        self.kept = kept
        self.send = send
        self.got = xor_send(send, axis, bit)

    def step(self, shape, axis, bit=1, order=()):
        mine = (lax.axis_index(axis) // bit) % 2
        send, kept = halve(self.kept.reshape(shape), self.got.reshape(shape), mine, order)
        return Sum(kept, send, axis, bit)

    def finish(self, shape, turned=False, order=()):
        return finish(self.kept.reshape(shape), self.got.reshape(shape), turned, order)


def slab_grad_kernel(split, extra, pair, sel_ref, la_ref, lb_ref, ra_ref, rb_ref, *refs):
    if pair:
        rb_ref = [jnp.where(pl.program_id(0) == 0, rb_ref[0], refs[0][0])]
        refs = refs[1:]
    out_ref = refs[extra]
    if split is None:
        out = dot_tn(la_ref[0], ra_ref[0]) + dot_tn(lb_ref[0], rb_ref[0])
    else:
        zs, rows = split
        take = [pl.ds(pl.multiple_of((z * 2 + sel_ref[0]) * rows, rows), rows) for z in range(zs)]
        left = [jnp.concatenate([ref[0, :, t] for t in take], axis=1) for ref in (la_ref, lb_ref)]
        out = dot_tn(left[0], ra_ref[0]) + dot_tn(left[1], rb_ref[0])
    out_ref[0] = out.astype(BF)


def slab_grad(left, right, x, y, order=()):
    left_a, left_b, left_at = left
    right_a, right_b, right_at = right
    pair = isinstance(right_b, tuple)
    _, frames, width = left_a.shape
    hidden = right_a.shape[2]
    zs = lax.axis_size("z")
    rows = width // (2 * zs)
    half = width // 2
    if x is None:
        split = None
        sel = y
        left_block = pl.BlockSpec((1, frames, half), lambda i, s: (left_at, 0, i))
        right = [
            pl.BlockSpec((1, frames, hidden), lambda i, s: (s[0], 0, 0)),
            pl.BlockSpec((1, frames, hidden), lambda i, s: (s[0] + right_at, 0, 0)),
        ]
    else:
        sel = x
        right = [
            pl.BlockSpec((1, frames, hidden), lambda i, s: (i, 0, 0)),
            pl.BlockSpec((1, frames, hidden), lambda i, s: (i + right_at, 0, 0)),
        ]
        if pair:
            right[1:] = [pl.BlockSpec((1, frames, hidden), lambda i, s: (0, 0, 0))] * 2
        if rows % 128 == 0:
            split = (zs, rows)
            left_block = pl.BlockSpec((1, frames, width), lambda i, s: (left_at, 0, 0))
        else:
            split = None
            left_block = pl.BlockSpec((1, frames, half), lambda i, s: (0, 0, 0))
            left_a, left_b = (
                pick(l[left_at].reshape(frames, zs, 2, rows), x, 2).reshape(1, frames, half)
                for l in (left_a, left_b)
            )
    return pl.pallas_call(
        functools.partial(slab_grad_kernel, split, len(order), pair),
        grid_spec=pltpu.PrefetchScalarGridSpec(
            num_scalar_prefetch=1,
            grid=(2,),
            in_specs=[left_block, left_block]
            + right
            + [pl.BlockSpec(memory_space=pl.ANY)] * len(order),
            out_specs=pl.BlockSpec((1, half, hidden), lambda i, s: (i, 0, 0)),
        ),
        out_shape=jax.ShapeDtypeStruct((2, half, hidden), BF),
        compiler_params=pltpu.CompilerParams(vmem_limit_bytes=VMEM_BYTES),
        cost_estimate=pl.CostEstimate(flops=1024, bytes_accessed=1024, transcendentals=0),
        name="slab_grad",
    )(sel.astype(jnp.int32)[None], left_a, left_b, right_a, *(right_b if pair else (right_b,)), *order)


def slab_sum(left, right, first, order=(), kept_order=()):
    place = lax.axis_index(first)
    picks = lambda i: (i, None) if first == "x" else (None, i)
    away = slab_grad(left, right, *picks(1 - place), order)
    return Sum(slab_grad(left, right, *picks(place), (away,) + tuple(kept_order)), away, first, 1)


def slab_second(total, first, order=()):
    zs = lax.axis_size("z")
    _, half, hidden = total.kept.shape
    if first == "x":
        return total.step((1, 2, half, hidden), "y", 1, order)
    return total.step((zs, 2, half // zs, hidden), "x", 1, order)


def z_steps(total, rows, columns, bits=None, order=()):
    zs = lax.axis_size("z")
    for bit in z_bits() if bits is None else bits:
        total = total.step((zs // (2 * bit), 2, rows, columns), "z", bit, order)
    return total


def z_bits():
    bits = []
    while 1 << len(bits) < lax.axis_size("z"):
        bits.append(1 << len(bits))
    return bits


def right_of(ref):
    if len(ref.shape) == 2:
        return ref[...]
    return jnp.concatenate([heads_of(ref, at, at + DH) for at in range(0, ref.shape[2], DH)], axis=1)


def row_grad_kernel(pairs, rows, core_ref, *refs):
    send_ref, keep_ref = refs[-2:]
    at = 0
    for i in range(pairs):
        whole = dot_tn(refs[2 * i][...], right_of(refs[2 * i + 1])).astype(BF)
        columns = whole.shape[1]
        parts = [whole[k * rows : (k + 1) * rows] for k in range(whole.shape[0] // rows)]
        even = jnp.concatenate(parts[0::2], axis=0)
        odd = jnp.concatenate(parts[1::2], axis=0)
        first = core_ref[0] == 0
        keep_ref[:, at : at + columns] = jnp.where(first, even, odd)
        send_ref[:, at : at + columns] = jnp.where(first, odd, even)
        at += columns


def row_grad(core, pairs):
    frames, width = pairs[0][0].shape
    zs = lax.axis_size("z")
    rows = width // (8 * zs)
    columns = sum(right.size // frames for _, right in pairs)
    if rows % 16:
        whole = jnp.concatenate(
            [dot_tn(left, right_of(right)).astype(BF) for left, right in pairs], axis=1
        )
        whole = whole.reshape(4 * zs, 2, rows, columns)
        flat = lambda v: v.reshape(width // 2, columns)
        return flat(pick(whole, 1 - core[0], 1)), flat(pick(whole, core[0], 1))
    tile = 256
    specs, args = [], []
    for left, right in pairs:
        specs += [
            pl.BlockSpec((frames, tile), lambda i, c: (0, i)),
            pl.BlockSpec(right.shape, lambda i, c, n=right.ndim: (0,) * n),
        ]
        args += [left, right]
    out = pl.BlockSpec((tile // 2, columns), lambda i, c: (i, 0))
    return pl.pallas_call(
        functools.partial(row_grad_kernel, len(pairs), rows),
        grid_spec=pltpu.PrefetchScalarGridSpec(
            num_scalar_prefetch=1, grid=(width // tile,), in_specs=specs, out_specs=[out, out]
        ),
        out_shape=[jax.ShapeDtypeStruct((width // 2, columns), BF)] * 2,
        compiler_params=pltpu.CompilerParams(vmem_limit_bytes=VMEM_BYTES),
        cost_estimate=pl.CostEstimate(flops=1024, bytes_accessed=1024, transcendentals=0),
        name="row_grad",
    )(core, *args)


def body(
    block_in,
    out_grad,
    utt_ends,
    valid_ends,
    ffn1_in,
    ffn1_out,
    att_qkv,
    att_out,
    content_bias,
    conv_in,
    conv_out,
    ffn2_in,
    ffn2_out,
    conv_depth,
    norm_gain,
    norm_bias,
):
    zs = lax.axis_size("z")
    devices = 8 * zs
    frames, width = block_in.shape
    heads = width // DH
    z, x, y, c = (lax.axis_index(axis) for axis in DEV)
    place = ((z * 2 + x) * 2 + y) * 2 + c
    head = (x * 2 + y) * 2 + c

    small = jnp.concatenate([norm_gain, norm_bias, conv_depth, content_bias[None]], axis=0)
    small = jnp.broadcast_to(small[None], (devices,) + small.shape)
    small = lax.all_to_all(small, DEV, split_axis=0, concat_axis=0, tiled=True)
    small = small.transpose(1, 0, 2).reshape(small.shape[1], width).astype(F32)
    gains, shifts, taps, q_bias = small[:6], small[6:12], small[12 : 12 + KSIZE], small[12 + KSIZE]

    rows, few = ffn1_in.shape[0], att_qkv.shape[0]
    blocks = lambda w: [w[:, i : i + width] for i in range(0, w.shape[1], width)]

    def gather(*parts):
        mine = jnp.concatenate(parts, axis=0)
        return lax.all_gather(mine, DEV, axis=0, tiled=True).reshape(devices, -1, width)

    w_first = gather(pack_ffn(ffn1_in, ffn1_out), *blocks(att_qkv))
    w_mid = gather(att_out, *blocks(conv_in), conv_out)
    w_second = gather(pack_ffn(ffn2_in, ffn2_out, order=(small,)))
    w_proj = Rows(w_first, 2 * rows, few)
    w_conv = Rows(w_mid, 0, few)
    w_cout = Rows(w_mid, 3 * few, few)
    core = c.astype(jnp.int32)[None]

    all_frames = frames * devices
    first_frame = place * frames
    span = 4 * frames
    group = 8 * frames
    origin = span
    group_first = z * group
    starts = jnp.concatenate([jnp.zeros((1,), jnp.int32), utt_ends[:-1]])
    valid_count = jnp.sum((valid_ends - starts).astype(F32))

    def segments(positions):
        seg = jnp.sum((utt_ends[None, :] <= positions[:, None]).astype(jnp.int32), axis=1)
        valid_seg = jnp.sum((valid_ends[None, :] <= positions[:, None]).astype(jnp.int32), axis=1)
        valid = seg == valid_seg
        return jnp.where(positions < 0, -1, jnp.where(positions >= all_frames, -2, seg)), valid

    ext_seg, ext_valid = segments(
        first_frame - REACH + jnp.arange(frames + 2 * REACH, dtype=jnp.int32)
    )
    own_seg = ext_seg[REACH : REACH + frames]
    ext_valid = ext_valid.astype(F32)
    edge_valid = jnp.concatenate([ext_valid[:REACH], ext_valid[-REACH:]])
    edge_valid = jnp.concatenate([edge_valid, jnp.zeros((frames - 2 * REACH,), F32)])
    columns = jnp.stack(
        [(ext_seg[m : m + frames] == own_seg).astype(F32) for m in range(KSIZE)]
        + [ext_valid[REACH : REACH + frames], edge_valid, jnp.zeros((frames,), F32)],
        axis=1,
    )
    group_pos = group_first + jnp.arange(group, dtype=jnp.int32)
    ended = utt_ends[None, :] <= group_pos[:, None]
    group_seg = jnp.sum(ended.astype(jnp.int32), axis=1)
    group_lo = jnp.max(jnp.where(ended, utt_ends[None, :], 0), axis=1)
    slots = jnp.arange(utt_ends.shape[0], dtype=jnp.int32)
    group_hi = jnp.sum(
        jnp.where(group_seg[:, None] == slots[None, :], valid_ends[None, :], 0), axis=1
    )
    window_first = group_first - origin
    lo_q = group_lo - window_first
    hi_q = group_hi - window_first
    low = (lo_q[::BQ] // 128) * 128
    high = hi_q[BQ - 1 :: BQ]
    lo_q = lo_q.astype(F32)[None, :]
    hi_q = hi_q.astype(F32)[None, :]
    c2 = (32.0 * jnp.exp2(-head.astype(F32)) * (LOG2E / span))[None]

    def vectors(*rows):
        rows = jnp.stack(rows)
        return jnp.concatenate([rows, jnp.zeros((-len(rows) % 8, width), F32)], axis=0)

    count_row = jnp.broadcast_to(valid_count, (width,))

    x1, n2, pack1, s1, d1, q_heads, k_heads, v_heads = first_call(
        core,
        block_in,
        w_first,
        rows,
        w_proj,
        vectors(gains[0], shifts[0], gains[1], shifts[1], q_bias),
    )
    pack1_sib = xor_send(pack1, "c", 1)

    def to_heads(cells):
        got = lax.all_to_all(cells, LAYER, split_axis=0, concat_axis=0, tiled=True)
        return got.reshape(group, cells.shape[2])

    def to_frames(cells):
        cells = cells.reshape(heads, frames, cells.shape[1])
        return lax.all_to_all(cells, LAYER, split_axis=0, concat_axis=0, tiled=True)

    up = [(i, i + 1) for i in range(zs - 1)]
    down = [(i + 1, i) for i in range(zs - 1)]

    def with_edges(cells):
        return lax.ppermute(cells[-span:], "z", up), cells, lax.ppermute(cells[:span], "z", down)

    kv = with_edges(to_heads(k_heads)) + with_edges(to_heads(v_heads))
    q_own = to_heads(q_heads)
    o_own, lse = attn_fwd(q_own, kv, low, high, c2, lo_q, hi_q, origin)
    mixed, x2, n3, lin, sig, gated = gate_call(
        to_frames(o_own), x1, w_conv, vectors(gains[2], shifts[2]), columns
    )
    g_edges = neighbour_rows(gated)
    tap_rows = [taps[m] for m in range(KSIZE)]
    conv, moments = conv_call(gated, *g_edges, vectors(*tap_rows), columns, devices)
    spread = lambda cells: lax.all_to_all(cells, DEV, split_axis=0, concat_axis=0, tiled=True)
    moments = spread(moments)

    final_out, swished, dx3, ew, dz, sums_c, totals, pack2, s2, da2 = second_call(
        core,
        x2,
        conv,
        moments,
        w_cout,
        w_second,
        rows,
        vectors(gains[3], shifts[3], gains[4], shifts[4], gains[5], shifts[5], count_row),
        out_grad,
    )
    totals = spread(totals)
    edges = neighbour_rows(jnp.concatenate([dz[-REACH:], conv[-REACH:]]), jnp.concatenate([dz[:REACH], conv[:REACH]]))
    pack2_sib = xor_send(pack2, "c", 1)
    hidden = pack2.shape[2]
    f2i = slab_sum((pack2, pack2_sib, 0), (da2, pack2_sib, 4), "x")
    f2o = slab_sum((pack2, pack2_sib, 3), (s2, pack2_sib, 1), "y")

    point_grad, dx2, ey, mixed_grad, sums_b = back_call(
        dz,
        conv,
        edges,
        gated,
        g_edges,
        moments,
        totals,
        lin,
        sig,
        x2,
        dx3,
        w_conv,
        vectors(*tap_rows, gains[3], gains[2], gains[2], count_row),
        columns,
        order=(f2i.send, f2o.send),
    )
    do_own = to_heads(mixed_grad)
    send, kept = row_grad(core, [(mixed, ey), (n3, point_grad), (swished, ew)])
    mid = Sum(kept, send, "c", 1)
    dq, dkv_prev, dkv, dkv_next = attn_bwd(
        q_own,
        o_own,
        do_own,
        lse,
        kv,
        low,
        high,
        c2,
        lo_q,
        hi_q,
        origin,
        order=(f2i.kept, f2o.kept, kept),
    )
    dq = to_frames(dq)
    f2i = slab_second(f2i, "x")
    f2o = slab_second(f2o, "y", order=(f2i.send,))
    dkv = join_edges(
        dkv,
        lax.ppermute(dkv_next, "z", up),
        lax.ppermute(dkv_prev, "z", down),
        order=(f2i.send, f2o.send),
    )
    dkv = to_frames(dkv)

    low_z, high_z = z_bits()[:1], z_bits()[1:]
    send, kept = row_grad(core, [(n2, dq), (n2, dkv)])
    qkv = Sum(kept, send, "c", 1)
    mid = mid.step((zs, 2, 2 * few, 4 * width), "x", order=(qkv.send,))
    dx1, ef1, sums_p = proj_back_call(
        dq, dkv, dx2, x1, w_proj, vectors(gains[0], gains[1]), (mid.send,)
    )
    ef1_sib = xor_send(ef1, "c", 1)
    f2i = z_steps(f2i, rows, hidden, low_z, order=(ef1,))
    f2o = z_steps(f2o, rows, hidden, low_z, order=(f2i.send,))
    qkv = z_steps(qkv, 4 * few, 3 * width, low_z, order=(f2o.send,))
    f1o_left, f1o_right = (ef1, ef1_sib, 0), (s1, pack1_sib, 1)
    f1o_away = slab_grad(f1o_left, f1o_right, None, 1 - y, (qkv.send,))
    grad_input, sums_a, da_first, da_second, da1 = last_call(
        core,
        dx1,
        ef1,
        block_in,
        w_first,
        rows,
        d1,
        vectors(gains[0]),
        order=(f1o_away,),
    )
    da_sib = (xor_send(da_first, "c", 1), xor_send(da_second, "c", 1))
    f2i = z_steps(f2i, rows, hidden, high_z, order=(da1,))
    f2o = z_steps(f2o, rows, hidden, high_z, order=(f2i.send,))
    f1i = slab_sum((pack1, pack1_sib, 0), (da1, da_sib, 0), "x", order=(f2o.send,))
    f1o = Sum(slab_grad(f1o_left, f1o_right, None, y, (f1i.kept,)), f1o_away, "y", 1)
    mid = mid.step((zs, 2, few, 4 * width), "y", order=(f1o.kept,))
    f1o = slab_second(f1o, "y", order=(mid.send,))
    qkv = qkv.step((zs, 2, few, 3 * width), "y", order=(f1o.send,))
    mid = z_steps(mid, few, 4 * width, low_z, order=(qkv.send,))
    f1i = slab_second(f1i, "x", order=(mid.send,))
    qkv = z_steps(qkv, 2 * few, 3 * width, high_z, order=(f1i.send,))
    f1o = z_steps(f1o, rows, hidden, low_z, order=(qkv.send,))
    f1i = z_steps(f1i, rows, hidden, low_z, order=(f1o.send,))
    mid = z_steps(mid, few, 4 * width, high_z, order=(f1i.send,))
    qkv = qkv.step((1, 2, few, 3 * width), "x", order=(mid.send,))
    f1o = z_steps(f1o, rows, hidden, high_z, order=(qkv.send,))
    f1i = z_steps(f1i, rows, hidden, high_z, order=(f1o.send,))
    grad_f2i = f2i.finish((rows, hidden), order=(f1i.send,))
    grad_f2o = f2o.finish((rows, hidden), True, order=(f1i.send,))
    mid = mid.finish((few, 4 * width), order=(f1i.send,))
    out_att, out_cin, out_cout = mid[:, :width], mid[:, width : 3 * width], mid[:, 3 * width :]
    out_qkv = qkv.finish((few, 3 * width), order=(f1i.send,))
    grad_f1o = f1o.finish((rows, hidden), True, order=(f1i.send,))
    grad_f1i = f1i.finish((rows, hidden))

    a, b, c, p = 0, 1, 2, 3
    places = [(a, 0), (p, 0), (b, 0), (c, 4), (c, 2), (c, 0)]
    places += [(a, 1), (p, 1), (b, 1), (c, 5), (c, 3), (c, 1)]
    places += [(b, 2 + m) for m in range(KSIZE)] + [(p, 2)]
    rows = stack_rows([sums_a, sums_b, sums_c, sums_p], places, order=(f1o.kept,))
    rows = rows.reshape(rows.shape[0], devices, width // devices).transpose(1, 0, 2)
    rows = jnp.sum(lax.all_to_all(rows, DEV, split_axis=0, concat_axis=0, tiled=True), axis=0)

    return (
        final_out,
        grad_input,
        grad_f1i,
        grad_f1o,
        out_qkv,
        out_att,
        rows[12 + KSIZE],
        out_cin,
        out_cout,
        grad_f2i,
        grad_f2o,
        rows[12 : 12 + KSIZE],
        rows[:6],
        rows[6:12],
    )


def solution(mesh):
    seq, heads = mesh.shape["seq"], mesh.shape["head"]
    grid = Mesh(mesh.devices.reshape(seq // 2, 2, heads // 2, 2), DEV)
    both = P(DEV, None)
    inward = P(("z", "x"), ("y", "c"))
    outward = P(("y", "c"), ("z", "x"))
    columns = P(None, DEV)
    return jax.shard_map(
        body,
        mesh=grid,
        in_specs=(
            both,
            both,
            P(),
            P(),
            inward,
            outward,
            both,
            both,
            P(DEV),
            both,
            both,
            inward,
            outward,
            columns,
            columns,
            columns,
        ),
        out_specs=(
            both,
            both,
            inward,
            outward,
            both,
            both,
            P(DEV),
            both,
            both,
            inward,
            outward,
            columns,
            columns,
            columns,
        ),
        check_vma=False,
    )
```

time: 1110 us -> 829 us (0.75)
  waiting for transfers between devices: 473 us -> 329 us
  Pallas kernels: 113 us -> 253 us
  local copies, waits for them, and re-layouts: 171 us -> 49.5 us
  other arithmetic: 116 us -> 10.3 us
  matrix products: 101 us -> 0 us
  blocking collectives: 0 us -> 38.2 us
  starting transfers between devices: 101 us -> 125 us
    pallas_call x4 -> x47, Pallas kernels: 59.6 us -> 204 us  [the longest x8 43.7 us: slab_grad(): pl.pallas_call(functools.partial(slab_grad_kernel, split, len(order), pai...]
    all_gather x4 -> x3, waiting for transfers between devices: 280 us -> 174 us  [gather(): lax.all_gather(mine, DEV, axis=0, tiled=True).reshape(devices, -1, width)]
    dot_general x36 -> x0, matrix products: 101 us -> none  [the longest x28 66.4 us: dot_tn(): lax.dot_general(a, b, (((0,), (0,)), ((), ())), preferred_element_type=F32)]
    ppermute x30 -> x31, waiting for transfers between devices: 143 us -> 87 us  [xor_send(): return lax.ppermute(cells, axis, [(i, i ^ bit) for i in range(count)])]
    all_gather x2 -> x0, local copies, waits for them, and re-layouts: 43.4 us -> none  [gather_ffn(): lax.all_gather(both, WIDE, axis=0, tiled=True).reshape(4, width, 2 * width)]
    all_to_all x0 -> x2, blocking collectives: none -> 38.2 us  [the longest x1 23.6 us: to_frames(): return lax.all_to_all(cells, LAYER, split_axis=0, concat_axis=0, tiled=True)]
    add x22 -> x0, other arithmetic: 36.1 us -> none  [the longest x20 33.9 us: halve(): return keep.astype(F32) + xor_send(send, axis, bit).astype(F32)]
    concatenate x11 -> x7, other arithmetic: 36.3 us -> 4.16 us  [the longest x2 2.67 us: gather(): mine = jnp.concatenate(parts, axis=0)]
  transfers between devices with their start and end apart: 52 -> 53, of which waited for: 21 -> 23; matrix products, arithmetic and copies ran while one was open for 30% -> 4% of each run, Pallas kernels for 8% -> 25%
where the time goes in v2:
time: 829 us; the launch traced here: 820 us
  waiting for transfers between devices  329 us (40%)
  Pallas kernels  253 us (31%)
  starting transfers between devices  125 us (15%)
  local copies, waits for them, and re-layouts  49.5 us (6%)
  blocking collectives  38.2 us (5%)
  between operations  15 us (2%)
  other arithmetic  10.3 us (1%)
    all_gather x3, waiting for transfers between devices, gather(): lax.all_gather(mine, DEV, axis=0, tiled=True).reshape(devices, -1, width)  174 us
    ppermute x31, waiting for transfers between devices, xor_send(): return lax.ppermute(cells, axis, [(i, i ^ bit) for i in range(count)])  87 us
    ppermute x31, starting transfers between devices, xor_send(): return lax.ppermute(cells, axis, [(i, i ^ bit) for i in range(count)])  53.1 us
    pallas_call x8, Pallas kernels, slab_grad(): pl.pallas_call(functools.partial(slab_grad_kernel, split, len(order), pai...  43.7 us
    all_to_all x4, waiting for transfers between devices, to_heads(): got = lax.all_to_all(cells, LAYER, split_axis=0, concat_axis=0, tiled=True)  36.3 us
    pallas_call x1, Pallas kernels, second_call(): pl.pallas_call(second_kernel, grid_spec=pltpu.PrefetchScalarGridSpec(num_...  31.1 us
    unnamed x148, local copies, waits for them, and re-layouts  28.8 us
    pallas_call x1, Pallas kernels, attn_bwd(): pl.pallas_call(kernel, grid_spec=grid_spec, out_shape=[jax.ShapeDtypeStru...  26.7 us
  transfers between devices with their start and end apart: 53, of which 23 were waited for; matrix products, arithmetic and copies ran while one was open for 4% of the time, Pallas kernels for 25%

profile of v2, /device:TPU:0, one launch (start us, length us, event | category | flops | bytes accessed | tf_op | source)
XLA Modules:
  0.0 819.7 jit_solution(11663658581391880452)
XLA Ops:
  13.3 14.5 %all_to_all.55 = bf16[32,2,288]{2,1,0:T(2,128)(2,1)S(1)} all-to-all(bf16[32,2,288]{2,1,0:T(2,128)(2,1)S(1)} %reshape.409), channel_id=1, replica_groups=mesh['z'=4,'x'=2,'y'=2,'c'=2] {'z','x','y','c'}, dimensions={0} | all-to-all | bytes 73728 | tf_op jit(solution)/shard_map/all_to_all | solution.py:1335
  33.0 126.6 %all-gather.4.cloned.1.call-done = bf16[11264,1024]{1,0:T(8,128)(2,1)} async-done(((bf16[352,1024]{1,0:T(8,128)(2,1)}), bf16[11264,1024]{1,0:T(8,128)(2,1)}) %all-gather.4.cloned.1.call-update) | async-done | bytes 23068688 | tf_op jit(solution)/shard_map/all_gather | solution.py:1344
  159.7 20.5 %first_part.1 = (f32[384,1024]{1,0:T(8,128)}, bf16[384,1024]{1,0:T(8,128)(2,1)}, bf16[3,384,1024]{2,1,0:T(8,128)(2,1)}, bf16[2,384,1024]{2,1,0:T(8,128)(2,1)}, b...) custom-call(s32[1]{0:T(128)} %bitcast.core_ref, ...), custom_call_target="tpu_custom_call" | custom-call | flops 8858370048 | bytes 38797312 | tf_op jit(solution)/shard_map/first_part/pallas_call | solution.py:231
  186.0 14.9 %all-to-all-done.2 = bf16[8,384,128]{2,1,0:T(8,128)(2,1)S(1)} async-done(((bf16[8,384,128]{2,1,0:T(8,128)(2,1)}), bf16[8,384,128]{2,1,0:T(8,128)(2,1)S(1)}, u32[]{:S(2)}, u32[]{:S(2)}) %all-to-all-start.2) | async-done | bytes 786464 | tf_op jit(solution)/shard_map/all_to_all | solution.py:1415
  226.7 12.7 %all-to-all-done.1 = bf16[8,384,128]{2,1,0:T(8,128)(2,1)S(1)} async-done(((bf16[8,384,128]{2,1,0:T(8,128)(2,1)}), bf16[8,384,128]{2,1,0:T(8,128)(2,1)S(1)}, u32[]{:S(2)}, u32[]{:S(2)}) %all-to-all-start.1) | async-done | bytes 786464 | tf_op jit(solution)/shard_map/all_to_all | solution.py:1415
  239.4 10.6 %collective-permute-done.3.refs_9_.refs_14_ = bf16[1536,128]{1,0:T(8,128)(2,1)} collective-permute-done((bf16[1536,128]{1,0:T(8,128)(2,1)S(1)}, bf16[1536,128]{1,0:T(8,128)(2,1)}, u32[]{:S(2)}, u32[]{:S(2)}) %collective-permute-start.3) | collective-permute-done | bytes 393248 | tf_op jit(solution)/shard_map/ppermute | solution.py:1426
  250.1 22.4 %attention_forward.1 = (bf16[3072,128]{1,0:T(8,128)(2,1)}, f32[1,3072]{1,0:T(1,128)}) custom-call(s32[12]{0:T(128)} %fusion.8.refs_0_, s32[12]{0:T(128)} %slice.235.refs_1_, f32[1]{0:T(128)} %bitcast.1.refs_2_, bf16[3072,128]{1,0:T(8,128)(2,1)} %bitcast.179, bf16[1536,128]{1,0:T(8,128)(2,1)} %collective-permute-done.refs_4_.refs_9_, ...), custom_call_target="tpu_custom_call" | custom-call | flops 1610612736 | bytes 3407872 | tf_op jit(solution)/shard_map/attention_forward/pallas_call | solution.py:894
  280.6 13.1 %all-to-all-done.4.mh_ref = bf16[8,384,128]{2,1,0:T(8,128)(2,1)S(1)} async-done(((bf16[8,384,128]{2,1,0:T(8,128)(2,1)}), bf16[8,384,128]{2,1,0:T(8,128)(2,1)S(1)}, u32[]{:S(2)}, u32[]{:S(2)}) %all-to-all-start.4) | async-done | bytes 786464 | tf_op jit(solution)/shard_map/all_to_all | solution.py:1420
  294.6 9.3 %attention_out_and_gate.1 = (bf16[384,1024]{1,0:T(8,128)(2,1)}, f32[384,1024]{1,0:T(8,128)}, bf16[384,1024]{1,0:T(8,128)(2,1)}, f32[384,1024]{1,0:T(8,128)}, f32...) custom-call(bf16[8,384,128]{2,1,0:T(8,128)(2,1)} %copy-done.38, f32[384,1024]{1,0:T(8,128)} %get-tuple-element.107.x1_ref, ...), custom_call_target="tpu_custom_call" | custom-call | flops 2415919104 | bytes 15728640 | tf_op jit(solution)/shard_map/attention_out_and_gate/pallas_call | solution.py:308
  316.0 11.5 %all-to-all-start.5 = ((f32[32,2,1024]{2,1,0:T(2,128)}), f32[32,2,1024]{2,1,0:T(2,128)S(1)}, u32[]{:S(2)}, u32[]{:S(2)}) async-start(f32[32,2,1024]{2,1,0:T(2,128)} %get-tuple-element.111), calls=%async_computation.5 | async-start | bytes 524288 | tf_op jit(solution)/shard_map/all_to_all | solution.py:1437
  330.0 47.7 %all-gather.8.cloned.1.call-done = bf16[8192,1024]{1,0:T(8,128)(2,1)} async-done(((bf16[256,1024]{1,0:T(8,128)(2,1)}), bf16[8192,1024]{1,0:T(8,128)(2,1)}) %all-gather.8.cloned.1.call-update) | async-done | bytes 16777232 | tf_op jit(solution)/shard_map/all_gather | solution.py:1344
  378.5 31.1 %second_part.1 = (bf16[384,1024]{1,0:T(8,128)(2,1)}, bf16[384,1024]{1,0:T(8,128)(2,1)}, f32[384,1024]{1,0:T(8,128)}, bf16[384,1024]{1,0:T(8,128)(2,1)}, f32[384,...) custom-call(s32[1]{0:T(128)} %bitcast.core_ref, ...), custom_call_target="tpu_custom_call" | custom-call | flops 14495514624 | bytes 51380224 | tf_op jit(solution)/shard_map/second_part/pallas_call | solution.py:475
  432.4 15.3 %convolution_backward.1 = (bf16[384,2048]{1,0:T(8,128)(2,1)}, f32[384,1024]{1,0:T(8,128)}, bf16[384,1024]{1,0:T(8,128)(2,1)}, bf16[8,384,128]{2,1,0:T(8,128)(2,1)}, f32[8,1024]{1,0:T(8,128)}) custom-call(f32[384,1024]{1,0:T(8,128)} %get-tuple-element.113.dz_ref, f32[384,1024]{1,0:T(8,128)} %get-tuple-element.110.conv_ref, f32[4,1024]{1,0:T(4,128)} %copy-done.56, ...), custom_call_target="tpu_custom_call" | custom-call | flops 2415919104 | bytes 19660800 | tf_op jit(solution)/shard_map/convolution_backward/pallas_call | solution.py:621
  458.4 9.3 %row_grad.2 = (bf16[512,4096]{1,0:T(8,128)(2,1)}, bf16[512,4096]{1,0:T(8,128)(2,1)}) custom-call(s32[1]{0:T(128)} %bitcast.core_ref, bf16[384,1024]{1,0:T(8,128)(2,1)} %get-tuple-element.123.refs_0_, bf16[384,1024]{1,0:T(8,128)(2,1)} %get-tuple-element.124.refs_1_, bf16[384,1024]{1,0:T(8,128)(2,1)} %get-tuple-element.125.refs_2_, ...), custom_call_target="tpu_custom_call" | custom-call | flops 1024 | bytes 1024 | tf_op jit(solution)/shard_map/row_grad/pallas_call | solution.py:1295
  479.4 26.7 %attention_backward.1 = (bf16[3072,128]{1,0:T(8,128)(2,1)}, bf16[1536,256]{1,0:T(8,128)(2,1)}, f32[3072,256]{1,0:T(8,128)}, bf16[1536,256]{1,0:T(8,128)(2,1)}) custom-call(s32[12]{0:T(128)} %fusion.8.refs_0_, s32[12]{0:T(128)} %slice.235.refs_1_, f32[1]{0:T(128)} %bitcast.1.refs_2_, bf16[3072,128]{1,0:T(8,128)(2,1)} %bitcast.180, ...), custom_call_target="tpu_custom_call" | custom-call | flops 32212254720 | bytes 6815744 | tf_op jit(solution)/shard_map/attention_backward/pallas_call | solution.py:1011
  507.4 9.1 %collective-permute-start.9 = (bf16[1536,256]{1,0:T(8,128)(2,1)}, bf16[1536,256]{1,0:T(8,128)(2,1)}, u32[]{:S(2)}, u32[]{:S(2)}) collective-permute-start(bf16[1536,256]{1,0:T(8,128)(2,1)} %get-tuple-element.132), channel_id=1, source_target_pairs={{0,8},{8,16},{16,24},{1,9},{9,17},{17,25},{2,10},{10,18},{18,26},{... | collective-permute-start | bytes 2359304 | tf_op jit(solution)/shard_map/ppermute | solution.py:1497
  533.9 23.6 %all_to_all.56.refs_3_.dkv_ref = bf16[8,384,256]{2,1,0:T(8,128)(2,1)} all-to-all(bf16[8,384,256]{2,1,0:T(8,128)(2,1)S(1)} %bitcast.108), channel_id=1, replica_groups=mesh['z'=4,'x'=2,'y'=2,'c'=2] {'x','y','c'}, dimensions={0} | all-to-all | bytes 3145728 | tf_op jit(solution)/shard_map/all_to_all | solution.py:1420
  578.5 9.0 %projections_backward.1 = (f32[384,1024]{1,0:T(8,128)}, bf16[1,384,1024]{2,1,0:T(8,128)(2,1)}, f32[8,1024]{1,0:T(8,128)}) custom-call(bf16[8,384,128]{2,1,0:T(8,128)(2,1)} %all-to-all-done.8.refs_1_.dq_ref, bf16[8,384,256]{2,1,0:T(8,128)(2,1)} %all_to_all.56.refs_3_.dkv_ref, f32[384,1024]{1,0:T(8,128)} %get-tuple-element.136.dx2_ref, ...), custom_call_target="tpu_custom_call" | custom-call | flops 1024 | bytes 1024 | tf_op jit(solution)/shard_map/projections_backward/pallas_call | solution.py:722
  610.5 14.6 %last_part.1 = (bf16[384,1024]{1,0:T(8,128)(2,1)}, f32[8,1024]{1,0:T(8,128)}, bf16[1,384,1024]{2,1,0:T(8,128)(2,1)}, bf16[1,384,1024]{2,1,0:T(8,128)(2,1)}, bf16[2,384,1024]{2,1,0:T(8,128)(2,1)}) custom-call(s32[1]{0:T(128)} %bitcast.core_ref, f32[384,1024]{1,0:T(8,128)} %get-tuple-element.141.dx1_ref, ...), custom_call_target="tpu_custom_call" | custom-call | flops 1024 | bytes 1024 | tf_op jit(solution)/shard_map/last_part/pallas_call | solution.py:775
  665.2 10.0 %collective-permute-done.27 = bf16[2,512,1024]{2,1,0:T(8,128)(2,1)S(1)} collective-permute-done((bf16[2,512,1024]{2,1,0:T(8,128)(2,1)}, bf16[2,512,1024]{2,1,0:T(8,128)(2,1)S(1)}, u32[]{:S(2)}, u32[]{:S(2)}) %collective-permute-start.27) | collective-permute-done | bytes 2097184 | tf_op jit(solution)/shard_map/ppermute | solution.py:33
  687.5 10.2 %collective-permute-done.25 = bf16[4,32,4096]{2,1,0:T(8,128)(2,1)S(1)} collective-permute-done((bf16[4,32,4096]{2,1,0:T(8,128)(2,1)S(1)}, bf16[4,32,4096]{2,1,0:T(8,128)(2,1)S(1)}, u32[]{:S(2)}, u32[]{:S(2)}) %collective-permute-start.25) | collective-permute-done | bytes 1048608 | tf_op jit(solution)/shard_map/ppermute | solution.py:33
  702.7 11.8 %collective-permute-done.30 = bf16[4,32,3072]{2,1,0:T(8,128)(2,1)S(1)} collective-permute-done((bf16[4,32,3072]{2,1,0:T(8,128)(2,1)S(1)}, bf16[4,32,3072]{2,1,0:T(8,128)(2,1)S(1)}, u32[]{:S(2)}, u32[]{:S(2)}) %collective-permute-start.30) | collective-permute-done | bytes 786464 | tf_op jit(solution)/shard_map/ppermute | solution.py:33
  720.2 15.9 %collective-permute-done.28 = bf16[1,512,1024]{2,1,0:T(8,128)(2,1)S(1)} collective-permute-done((bf16[1,512,1024]{2,1,0:T(8,128)(2,1)S(1)}, bf16[1,512,1024]{2,1,0:T(8,128)(2,1)S(1)}, u32[]{:S(2)}, u32[]{:S(2)}) %collective-permute-start.28) | collective-permute-done | bytes 1048608 | tf_op jit(solution)/shard_map/ppermute | solution.py:33
  763.5 22.2 %collective-permute-start.37 = (bf16[1,32,3072]{2,1,0:T(8,128)(2,1)}, bf16[1,32,3072]{2,1,0:T(8,128)(2,1)S(1)}, u32[]{:S(2)}, u32[]{:S(2)}) collective-permute-start(bf16[1,32,3072]{2,1,0:T(8,128)(2,1)} %copy-done.35), channel_id=1, source_target_pairs={{0,4},{4,0},{1,5},{5,1},{2,6},{6,2},{3,7},{7,3},{8,12},{12,8},{9,1... | collective-permute-start | bytes 589832 | tf_op jit(solution)/shard_map/ppermute | solution.py:33
  (369 shorter events, 292.0 us)
Async XLA Ops:
  7.2 152.4 %all-gather.4.cloned.1.call-start = ((), (), s32[]{:S(2)}) async-start(), calls=%async_computation.11 | async-start | bytes 23789568 | tf_op jit(solution)/shard_map/all_gather | solution.py:1344
  12.2 268.4 %all-gather.6.cloned.1.call-start = ((), (), s32[]{:S(2)}) async-start(), calls=%async_computation.12 | async-start | bytes 8650752 | tf_op jit(solution)/shard_map/all_gather | solution.py:1344
  13.0 364.7 %all-gather.8.cloned.1.call-start = ((), (), s32[]{:S(2)}) async-start(), calls=%async_computation.13 | async-start | bytes 17301504 | tf_op jit(solution)/shard_map/all_gather | solution.py:1344
  205.2 34.2 %collective-permute-start = (bf16[1536,128]{1,0:T(8,128)(2,1)S(1)}, bf16[1536,128]{1,0:T(8,128)(2,1)}, u32[]{:S(2)}, u32[]{:S(2)}) collective-permute-start(bf16[1536,128]{1,0:T(8,128)(2,1)S(1)} %bitcast.185), channel_id=1, source_target_pairs={{0,8},{8,16},{16,24},{1,9},{9,17},{17,25},{2,10},{10,18},{18,26},{... | collective-permute-start | bytes 1179656 | tf_op jit(solution)/shard_map/ppermute | solution.py:1426
  207.3 32.1 %collective-permute-start.1 = (bf16[1536,128]{1,0:T(8,128)(2,1)S(1)}, bf16[1536,128]{1,0:T(8,128)(2,1)}, u32[]{:S(2)}, u32[]{:S(2)}) collective-permute-start(bf16[1536,128]{1,0:T(8,128)(2,1)S(1)} %bitcast.184), channel_id=1, source_target_pairs={{8,0},{16,8},{24,16},{9,1},{17,9},{25,17},{10,2},{18,10},{26,18},{... | collective-permute-start | bytes 1179656 | tf_op jit(solution)/shard_map/ppermute | solution.py:1426
  316.0 61.8 %all-to-all-start.5 = ((f32[32,2,1024]{2,1,0:T(2,128)}), f32[32,2,1024]{2,1,0:T(2,128)S(1)}, u32[]{:S(2)}, u32[]{:S(2)}) async-start(f32[32,2,1024]{2,1,0:T(2,128)} %get-tuple-element.111), calls=%async_computation.5 | async-start | bytes 524288 | tf_op jit(solution)/shard_map/all_to_all | solution.py:1437
  454.9 66.3 %collective-permute-start.11 = (bf16[2,512,1024]{2,1,0:T(8,128)(2,1)}, bf16[2,512,1024]{2,1,0:T(8,128)(2,1)}, u32[]{:S(2)}, u32[]{:S(2)}) collective-permute-start(bf16[2,512,1024]{2,1,0:T(8,128)(2,1)} %slab_grad.8.refs_0_), channel_id=1, source_target_pairs={{0,4},{4,0},{1,5},{5,1},{2,6},{6,2},{3,7},{7,3},{8,12},{12,8},{9,1... | collective-permute-start | bytes 6291464 | tf_op jit(solution)/shard_map/ppermute | solution.py:33
  457.0 67.1 %collective-permute-start.12 = (bf16[2,512,1024]{2,1,0:T(8,128)(2,1)}, bf16[2,512,1024]{2,1,0:T(8,128)(2,1)}, u32[]{:S(2)}, u32[]{:S(2)}) collective-permute-start(bf16[2,512,1024]{2,1,0:T(8,128)(2,1)} %slab_grad.9.refs_1_.refs_0_), channel_id=1, source_target_pairs={{0,2},{2,0},{1,3},{3,1},{4,6},{6,4},{5,7},{7,5},{8,10},{10,8},{9,1... | collective-permute-start | bytes 6291464 | tf_op jit(solution)/shard_map/ppermute | solution.py:33
  520.8 48.0 %collective-permute-start.13 = (bf16[512,4096]{1,0:T(8,128)(2,1)}, bf16[512,4096]{1,0:T(8,128)(2,1)}, u32[]{:S(2)}, u32[]{:S(2)}) collective-permute-start(bf16[512,4096]{1,0:T(8,128)(2,1)} %get-tuple-element.137), channel_id=1, source_target_pairs={{0,1},{1,0},{2,3},{3,2},{4,5},{5,4},{6,7},{7,6},{8,9},{9,8},{10,11... | collective-permute-start | bytes 12582920 | tf_op jit(solution)/shard_map/ppermute | solution.py:33
  565.3 37.2 %collective-permute-start.16 = (bf16[512,3072]{1,0:T(8,128)(2,1)}, bf16[512,3072]{1,0:T(8,128)(2,1)S(1)}, u32[]{:S(2)}, u32[]{:S(2)}) collective-permute-start(bf16[512,3072]{1,0:T(8,128)(2,1)} %get-tuple-element.139.refs_0_), channel_id=1, source_target_pairs={{0,1},{1,0},{2,3},{3,2},{4,5},{5,4},{6,7},{7,6},{8,9},{9,8},{10,11... | collective-permute-start | bytes 9437192 | tf_op jit(solution)/shard_map/ppermute | solution.py:33
  565.3 40.0 %collective-permute-start.15 = (bf16[3,384,1024]{2,1,0:T(8,128)(2,1)}, bf16[3,384,1024]{2,1,0:T(8,128)(2,1)}, u32[]{:S(2)}, u32[]{:S(2)}) collective-permute-start(bf16[3,384,1024]{2,1,0:T(8,128)(2,1)} %get-tuple-element.145.la_ref), channel_id=1, source_target_pairs={{0,1},{1,0},{2,3},{3,2},{4,5},{5,4},{6,7},{7,6},{8,9},{9,8},{10,11... | collective-permute-start | bytes 7077896 | tf_op jit(solution)/shard_map/ppermute | solution.py:33
  591.2 68.2 %collective-permute-start.24 = (bf16[4,64,4096]{2,1,0:T(8,128)(2,1)}, bf16[4,64,4096]{2,1,0:T(8,128)(2,1)}, u32[]{:S(2)}, u32[]{:S(2)}) collective-permute-start(bf16[4,64,4096]{2,1,0:T(8,128)(2,1)} %get-tuple-element.140.refs_0_), channel_id=1, source_target_pairs={{0,4},{4,0},{1,5},{5,1},{2,6},{6,2},{3,7},{7,3},{8,12},{12,8},{9,1... | collective-permute-start | bytes 6291464 | tf_op jit(solution)/shard_map/ppermute | solution.py:33
  626.5 48.7 %collective-permute-start.27 = (bf16[2,512,1024]{2,1,0:T(8,128)(2,1)}, bf16[2,512,1024]{2,1,0:T(8,128)(2,1)S(1)}, u32[]{:S(2)}, u32[]{:S(2)}) collective-permute-start(bf16[2,512,1024]{2,1,0:T(8,128)(2,1)} %slab_grad.12.refs_0_), channel_id=1, source_target_pairs={{0,2},{2,0},{1,3},{3,1},{4,6},{6,4},{5,7},{7,5},{8,10},{10,8},{9,1... | collective-permute-start | bytes 6291464 | tf_op jit(solution)/shard_map/ppermute | solution.py:33
  647.1 50.9 %collective-permute-start.23 = (bf16[2,512,1024]{2,1,0:T(8,128)(2,1)}, bf16[2,512,1024]{2,1,0:T(8,128)(2,1)S(1)}, u32[]{:S(2)}, u32[]{:S(2)}) collective-permute-start(bf16[2,512,1024]{2,1,0:T(8,128)(2,1)} %slab_grad.13.refs_1_), channel_id=1, source_target_pairs={{0,4},{4,0},{1,5},{5,1},{2,6},{6,2},{3,7},{7,3},{8,12},{12,8},{9,1... | collective-permute-start | bytes 6291464 | tf_op jit(solution)/shard_map/ppermute | solution.py:33
  647.8 35.6 %collective-permute-start.26 = (bf16[2,128,3072]{2,1,0:T(8,128)(2,1)}, bf16[2,128,3072]{2,1,0:T(8,128)(2,1)}, u32[]{:S(2)}, u32[]{:S(2)}) collective-permute-start(bf16[2,128,3072]{2,1,0:T(8,128)(2,1)} %get-tuple-element.151.refs_0_), channel_id=1, source_target_pairs={{0,8},{8,0},{16,24},{24,16},{1,9},{9,1},{17,25},{25,17},{2,10},{10... | collective-permute-start | bytes 4718600 | tf_op jit(solution)/shard_map/ppermute | solution.py:33
  663.7 34.0 %collective-permute-start.25 = (bf16[4,32,4096]{2,1,0:T(8,128)(2,1)S(1)}, bf16[4,32,4096]{2,1,0:T(8,128)(2,1)S(1)}, u32[]{:S(2)}, u32[]{:S(2)}) collective-permute-start(bf16[4,32,4096]{2,1,0:T(8,128)(2,1)S(1)} %get-tuple-element.162.refs_0_), channel_id=1, source_target_pairs={{0,2},{2,0},{1,3},{3,1},{4,6},{6,4},{5,7},{7,5},{8,10},{10,8},{9,1... | collective-permute-start | bytes 3145736 | tf_op jit(solution)/shard_map/ppermute | solution.py:33
  675.8 40.7 %collective-permute-start.29 = (bf16[4,128,1024]{2,1,0:T(8,128)(2,1)S(1)}, bf16[4,128,1024]{2,1,0:T(8,128)(2,1)S(1)}, u32[]{:S(2)}, u32[]{:S(2)}) collective-permute-start(bf16[4,128,1024]{2,1,0:T(8,128)(2,1)S(1)} %get-tuple-element.164.refs_0_), channel_id=1, source_target_pairs={{0,4},{4,0},{1,5},{5,1},{2,6},{6,2},{3,7},{7,3},{8,12},{12,8},{9,1... | collective-permute-start | bytes 3145736 | tf_op jit(solution)/shard_map/ppermute | solution.py:33
  699.8 36.3 %collective-permute-start.28 = (bf16[1,512,1024]{2,1,0:T(8,128)(2,1)S(1)}, bf16[1,512,1024]{2,1,0:T(8,128)(2,1)S(1)}, u32[]{:S(2)}, u32[]{:S(2)}) collective-permute-start(bf16[1,512,1024]{2,1,0:T(8,128)(2,1)S(1)} %get-tuple-element.168.refs_0_), channel_id=1, source_target_pairs={{0,2},{2,0},{1,3},{3,1},{4,6},{6,4},{5,7},{7,5},{8,10},{10,8},{9,1... | collective-permute-start | bytes 3145736 | tf_op jit(solution)/shard_map/ppermute | solution.py:33
  700.7 37.5 %collective-permute-start.34 = (bf16[2,32,4096]{2,1,0:T(8,128)(2,1)S(1)}, bf16[2,32,4096]{2,1,0:T(8,128)(2,1)S(1)}, u32[]{:S(2)}, u32[]{:S(2)}) collective-permute-start(bf16[2,32,4096]{2,1,0:T(8,128)(2,1)S(1)} %get-tuple-element.166.refs_0_), channel_id=1, source_target_pairs={{0,8},{8,0},{16,24},{24,16},{1,9},{9,1},{17,25},{25,17},{2,10},{10... | collective-permute-start | bytes 1572872 | tf_op jit(solution)/shard_map/ppermute | solution.py:33
  750.4 35.5 %collective-permute-start.38 = (bf16[1,32,4096]{2,1,0:T(8,128)(2,1)}, bf16[1,32,4096]{2,1,0:T(8,128)(2,1)}, u32[]{:S(2)}, u32[]{:S(2)}) collective-permute-start(bf16[1,32,4096]{2,1,0:T(8,128)(2,1)} %get-tuple-element.178.refs_0_), channel_id=1, source_target_pairs={{0,16},{8,24},{16,0},{24,8},{1,17},{9,25},{17,1},{25,9},{2,18},{10... | collective-permute-start | bytes 786440 | tf_op jit(solution)/shard_map/ppermute | solution.py:33
  753.1 42.7 %collective-permute-start.40 = (bf16[1,128,1024]{2,1,0:T(8,128)(2,1)S(1)}, bf16[1,128,1024]{2,1,0:T(8,128)(2,1)}, u32[]{:S(2)}, u32[]{:S(2)}) collective-permute-start(bf16[1,128,1024]{2,1,0:T(8,128)(2,1)S(1)} %copy-done.32), channel_id=1, source_target_pairs={{0,16},{8,24},{16,0},{24,8},{1,17},{9,25},{17,1},{25,9},{2,18},{10... | collective-permute-start | bytes 786440 | tf_op jit(solution)/shard_map/ppermute | solution.py:33
  753.4 47.9 %collective-permute-start.39 = (bf16[1,128,1024]{2,1,0:T(8,128)(2,1)S(1)}, bf16[1,128,1024]{2,1,0:T(8,128)(2,1)S(1)}, u32[]{:S(2)}, u32[]{:S(2)}) collective-permute-start(bf16[1,128,1024]{2,1,0:T(8,128)(2,1)S(1)} %copy-done.28), channel_id=1, source_target_pairs={{0,16},{8,24},{16,0},{24,8},{1,17},{9,25},{17,1},{25,9},{2,18},{10... | collective-permute-start | bytes 786440 | tf_op jit(solution)/shard_map/ppermute | solution.py:33
  756.0 50.9 %collective-permute-start.36 = (bf16[1,128,1024]{2,1,0:T(8,128)(2,1)S(1)}, bf16[1,128,1024]{2,1,0:T(8,128)(2,1)S(1)}, u32[]{:S(2)}, u32[]{:S(2)}) collective-permute-start(bf16[1,128,1024]{2,1,0:T(8,128)(2,1)S(1)} %get-tuple-element.180.refs_0_), channel_id=1, source_target_pairs={{0,16},{8,24},{16,0},{24,8},{1,17},{9,25},{17,1},{25,9},{2,18},{10... | collective-permute-start | bytes 786440 | tf_op jit(solution)/shard_map/ppermute | solution.py:33
  763.5 38.6 %collective-permute-start.37 = (bf16[1,32,3072]{2,1,0:T(8,128)(2,1)}, bf16[1,32,3072]{2,1,0:T(8,128)(2,1)S(1)}, u32[]{:S(2)}, u32[]{:S(2)}) collective-permute-start(bf16[1,32,3072]{2,1,0:T(8,128)(2,1)} %copy-done.35), channel_id=1, source_target_pairs={{0,4},{4,0},{1,5},{5,1},{2,6},{6,2},{3,7},{7,3},{8,12},{12,8},{9,1... | collective-permute-start | bytes 589832 | tf_op jit(solution)/shard_map/ppermute | solution.py:33
  (101 other events, 1335.4 us)
Sparse Core Ops, SparseCore 0:
  12.3 147.2 all-gather.3
  163.1 90.6 all-gather.5
  257.2 120.4 all-gather.7

commit v3 on v2

--- a/solution.py
+++ b/solution.py
@@ -17,11 +17,17 @@
 LOG2E = math.log2(math.e)
 DEV = ("z", "x", "y", "c")
 LAYER = ("x", "y", "c")
-BQ = 256
+BQ = 512
 BK = 512
 BF = jnp.bfloat16
 F32 = jnp.float32
 VMEM_BYTES = 56 * 1024 * 1024
+
+
+def takes(microseconds):
+    return pl.CostEstimate(
+        flops=1024, bytes_accessed=1024 + int(microseconds * 3.7e6), transcendentals=0
+    )
 
 
 def pick(cells, index, dim):
@@ -266,19 +272,8 @@
     )(core, x, *slabs, proj_array, vectors)
 
 
-def gate_kernel(
-    mh_ref,
-    x1_ref,
-    w_ref,
-    vec_ref,
-    cols_ref,
-    mixed_ref,
-    x2_ref,
-    n3_ref,
-    lin_ref,
-    sig_ref,
-    g_ref,
-):
+def gate_kernel(extra, mh_ref, x1_ref, w_ref, vec_ref, cols_ref, *refs):
+    mixed_ref, x2_ref, n3_ref, lin_ref, sig_ref, g_ref = refs[extra:]
     step = pl.program_id(0)
 
     @pl.when(step == 0)
@@ -301,12 +296,12 @@
         g_ref[...] = (lin_ref[...] * sig * cols_ref[:, KSIZE : KSIZE + 1]).astype(BF)
 
 
-def gate_call(mixed_heads, x1, weights, vectors, columns):
+def gate_call(mixed_heads, x1, weights, vectors, columns, order=()):
     frames, width = x1.shape
     fixed = lambda *shape: pl.BlockSpec(shape, lambda j: (0,) * len(shape))
     array, block = weights.blocks(lambda j: j, 3)
     return pl.pallas_call(
-        gate_kernel,
+        functools.partial(gate_kernel, len(order)),
         grid=(3,),
         in_specs=[
             fixed(*mixed_heads.shape),
@@ -314,7 +309,8 @@
             block,
             fixed(*vectors.shape),
             fixed(*columns.shape),
-        ],
+        ]
+        + [pl.BlockSpec(memory_space=pl.ANY)] * len(order),
         out_specs=[fixed(frames, width)] * 6,
         out_shape=[jax.ShapeDtypeStruct((frames, width), t) for t in (BF, F32, BF, F32, F32, BF)],
         compiler_params=pltpu.CompilerParams(vmem_limit_bytes=VMEM_BYTES),
@@ -324,7 +320,7 @@
             transcendentals=frames * width,
         ),
         name="attention_out_and_gate",
-    )(mixed_heads, x1, array, vectors, columns)
+    )(mixed_heads, x1, array, vectors, columns, *order)
 
 
 PAD = 8
@@ -732,7 +728,7 @@
         ],
         scratch_shapes=[pltpu.VMEM((frames, width), F32)],
         compiler_params=pltpu.CompilerParams(vmem_limit_bytes=VMEM_BYTES),
-        cost_estimate=pl.CostEstimate(flops=1024, bytes_accessed=1024, transcendentals=0),
+        cost_estimate=takes(9),
         name="projections_backward",
     )(dq, dkv, dx2, x1, array, vectors, *order)
 
@@ -798,7 +794,7 @@
             jax.ShapeDtypeStruct((2, frames, width), BF),
         ],
         compiler_params=pltpu.CompilerParams(vmem_limit_bytes=VMEM_BYTES),
-        cost_estimate=pl.CostEstimate(flops=1024, bytes_accessed=1024, transcendentals=0),
+        cost_estimate=takes(15),
         name="last_part",
     )(core, dx1, ef, x, *slabs, slope, vectors, *order)
 
@@ -1069,20 +1065,30 @@
     )(own, before, after, *order)
 
 
-def stack_kernel(extra, places, *refs):
-    out_ref = refs[-1]
+def stack_kernel(extra, places, arrays, *refs):
+    out_ref = refs[arrays + extra]
+    rows_ref = refs[arrays + extra + 1]
     for at, (source, row) in enumerate(places):
-        out_ref[at : at + 1, :] = refs[source][row : row + 1, :]
-
-
-def stack_rows(arrays, places, order=()):
+        rows_ref[at : at + 1, :] = refs[source][row : row + 1, :]
+    share = out_ref.shape[2]
+    rows = rows_ref[...]
+    for i in range(out_ref.shape[0]):
+        out_ref[i] = rows[:, i * share : (i + 1) * share]
+
+
+def stack_rows(arrays, places, devices, order=()):
     width = arrays[0].shape[1]
-    return pl.pallas_call(
-        functools.partial(stack_kernel, len(order), places),
+    share = width // devices
+    if share % 32:
+        rows = jnp.stack([arrays[source][row] for source, row in places])
+        return rows.reshape(len(places), devices, share).transpose(1, 0, 2)
+    return pl.pallas_call(
+        functools.partial(stack_kernel, len(order), places, len(arrays)),
         in_specs=[pl.BlockSpec(v.shape, lambda: (0, 0)) for v in arrays]
         + [pl.BlockSpec(memory_space=pl.ANY)] * len(order),
-        out_specs=pl.BlockSpec((len(places), width), lambda: (0, 0)),
-        out_shape=jax.ShapeDtypeStruct((len(places), width), F32),
+        out_specs=pl.BlockSpec((devices, len(places), share), lambda: (0, 0, 0)),
+        out_shape=jax.ShapeDtypeStruct((devices, len(places), share), F32),
+        scratch_shapes=[pltpu.VMEM((len(places), width), F32)],
         name="stack_rows",
     )(*arrays, *order)
 
@@ -1139,6 +1145,91 @@
     )(kept, got, *order)
 
 
+def halve_both_kernel(extra, sel_ref, *refs):
+    send_ref, keep_ref = refs[8 + extra :]
+    for i in (0, 1):
+        kept_a, kept_b, got_a, got_b = refs[4 * i : 4 * i + 4]
+        rows = kept_a.shape[2]
+        here = slice(i * rows, (i + 1) * rows)
+        send_ref[0, here, :] = (kept_a[0, 0].astype(F32) + got_a[0, 0].astype(F32)).astype(BF)
+        keep_ref[0, here, :] = (kept_b[0, 0].astype(F32) + got_b[0, 0].astype(F32)).astype(BF)
+
+
+def halve_both(first, second, shape, mine, order=()):
+    count, _, rows, columns = shape
+    block = (1, 1, rows, columns)
+    other = pl.BlockSpec(block, lambda i, m: (i, 1 - m[0], 0, 0))
+    own = pl.BlockSpec(block, lambda i, m: (i, m[0], 0, 0))
+    out = pl.BlockSpec((1, 2 * rows, columns), lambda i, m: (i, 0, 0))
+    arrays = []
+    for part in (first, second):
+        kept, got = part.kept.reshape(shape), part.got.reshape(shape)
+        arrays += [kept, kept, got, got]
+    return pl.pallas_call(
+        functools.partial(halve_both_kernel, len(order)),
+        grid_spec=pltpu.PrefetchScalarGridSpec(
+            num_scalar_prefetch=1,
+            grid=(count,),
+            in_specs=[other, own, other, own] * 2
+            + [pl.BlockSpec(memory_space=pl.ANY)] * len(order),
+            out_specs=[out, out],
+        ),
+        out_shape=[jax.ShapeDtypeStruct((count, 2 * rows, columns), BF)] * 2,
+        compiler_params=pltpu.CompilerParams(vmem_limit_bytes=VMEM_BYTES // 3),
+        cost_estimate=pl.CostEstimate(flops=1024, bytes_accessed=1024, transcendentals=0),
+        name="halve_both",
+    )(mine.astype(jnp.int32)[None], *arrays, *order)
+
+
+def finish_both_kernel(extra, kept_ref, got_ref, *refs):
+    first_ref, second_ref = refs[extra:]
+    rows = first_ref.shape[0]
+    total = kept_ref[...].astype(F32) + got_ref[...].astype(F32)
+    first_ref[...] = total[:rows]
+    second_ref[...] = total[rows:].T
+
+
+def finish_both(total, rows, columns, order=()):
+    kept, got = total.kept.reshape(2 * rows, columns), total.got.reshape(2 * rows, columns)
+    if rows % 128:
+        both = kept.astype(F32) + got.astype(F32)
+        return both[:rows], both[rows:].T
+    fixed = lambda *shape: pl.BlockSpec(shape, lambda: (0, 0))
+    return pl.pallas_call(
+        functools.partial(finish_both_kernel, len(order)),
+        in_specs=[fixed(2 * rows, columns)] * 2
+        + [pl.BlockSpec(memory_space=pl.ANY)] * len(order),
+        out_specs=[fixed(rows, columns), fixed(columns, rows)],
+        out_shape=[
+            jax.ShapeDtypeStruct((rows, columns), F32),
+            jax.ShapeDtypeStruct((columns, rows), F32),
+        ],
+        compiler_params=pltpu.CompilerParams(vmem_limit_bytes=VMEM_BYTES // 3),
+        cost_estimate=pl.CostEstimate(flops=1024, bytes_accessed=1024, transcendentals=0),
+        name="finish_both",
+    )(kept, got, *order)
+
+
+def total_kernel(extra, parts_ref, *refs):
+    total = jnp.sum(parts_ref[...], axis=0)
+    at = 0
+    for ref in refs[extra:]:
+        ref[...] = total[at : at + ref.shape[0]]
+        at += ref.shape[0]
+
+
+def total_of(parts, counts, order=()):
+    columns = parts.shape[2]
+    return pl.pallas_call(
+        functools.partial(total_kernel, len(order)),
+        in_specs=[pl.BlockSpec(parts.shape, lambda: (0, 0, 0))]
+        + [pl.BlockSpec(memory_space=pl.ANY)] * len(order),
+        out_specs=[pl.BlockSpec((n, columns), lambda: (0, 0)) for n in counts],
+        out_shape=[jax.ShapeDtypeStruct((n, columns), F32) for n in counts],
+        name="total_of",
+    )(parts, *order)
+
+
 class Sum:
     def __init__(self, kept, send, axis, bit):
         self.kept = kept
@@ -1169,7 +1260,7 @@
     out_ref[0] = out.astype(BF)
 
 
-def slab_grad(left, right, x, y, order=()):
+def slab_grad(left, right, x, y, order=(), lasting=0):
     left_a, left_b, left_at = left
     right_a, right_b, right_at = right
     pair = isinstance(right_b, tuple)
@@ -1216,7 +1307,7 @@
         ),
         out_shape=jax.ShapeDtypeStruct((2, half, hidden), BF),
         compiler_params=pltpu.CompilerParams(vmem_limit_bytes=VMEM_BYTES),
-        cost_estimate=pl.CostEstimate(flops=1024, bytes_accessed=1024, transcendentals=0),
+        cost_estimate=takes(lasting),
         name="slab_grad",
     )(sel.astype(jnp.int32)[None], left_a, left_b, right_a, *(right_b if pair else (right_b,)), *order)
 
@@ -1241,6 +1332,13 @@
     for bit in z_bits() if bits is None else bits:
         total = total.step((zs // (2 * bit), 2, rows, columns), "z", bit, order)
     return total
+
+
+def z_both(first, second, rows, columns, order=()):
+    zs = lax.axis_size("z")
+    mine = lax.axis_index("z") % 2
+    send, kept = halve_both(first, second, (zs // 2, 2, rows, columns), mine, order)
+    return Sum(kept, send, "z", 1)
 
 
 def z_bits():
@@ -1271,7 +1369,7 @@
         at += columns
 
 
-def row_grad(core, pairs):
+def row_grad(core, pairs, order=()):
     frames, width = pairs[0][0].shape
     zs = lax.axis_size("z")
     rows = width // (8 * zs)
@@ -1291,6 +1389,7 @@
             pl.BlockSpec(right.shape, lambda i, c, n=right.ndim: (0,) * n),
         ]
         args += [left, right]
+    specs += [pl.BlockSpec(memory_space=pl.ANY)] * len(order)
     out = pl.BlockSpec((tile // 2, columns), lambda i, c: (i, 0))
     return pl.pallas_call(
         functools.partial(row_grad_kernel, len(pairs), rows),
@@ -1299,9 +1398,9 @@
         ),
         out_shape=[jax.ShapeDtypeStruct((width // 2, columns), BF)] * 2,
         compiler_params=pltpu.CompilerParams(vmem_limit_bytes=VMEM_BYTES),
-        cost_estimate=pl.CostEstimate(flops=1024, bytes_accessed=1024, transcendentals=0),
+        cost_estimate=takes(10),
         name="row_grad",
-    )(core, *args)
+    )(core, *args, *order)
 
 
 def body(
@@ -1429,7 +1528,7 @@
     q_own = to_heads(q_heads)
     o_own, lse = attn_fwd(q_own, kv, low, high, c2, lo_q, hi_q, origin)
     mixed, x2, n3, lin, sig, gated = gate_call(
-        to_frames(o_own), x1, w_conv, vectors(gains[2], shifts[2]), columns
+        to_frames(o_own), x1, w_conv, vectors(gains[2], shifts[2]), columns, (pack1_sib,)
     )
     g_edges = neighbour_rows(gated)
     tap_rows = [taps[m] for m in range(KSIZE)]
@@ -1501,18 +1600,14 @@
     dkv = to_frames(dkv)
 
     low_z, high_z = z_bits()[:1], z_bits()[1:]
-    send, kept = row_grad(core, [(n2, dq), (n2, dkv)])
+    dx1, ef1, sums_p = proj_back_call(dq, dkv, dx2, x1, w_proj, vectors(gains[0], gains[1]), ())
+    ef1_sib = xor_send(ef1, "c", 1)
+    send, kept = row_grad(core, [(n2, dq), (n2, dkv)], order=(ef1,))
     qkv = Sum(kept, send, "c", 1)
-    mid = mid.step((zs, 2, 2 * few, 4 * width), "x", order=(qkv.send,))
-    dx1, ef1, sums_p = proj_back_call(
-        dq, dkv, dx2, x1, w_proj, vectors(gains[0], gains[1]), (mid.send,)
-    )
-    ef1_sib = xor_send(ef1, "c", 1)
-    f2i = z_steps(f2i, rows, hidden, low_z, order=(ef1,))
-    f2o = z_steps(f2o, rows, hidden, low_z, order=(f2i.send,))
-    qkv = z_steps(qkv, 4 * few, 3 * width, low_z, order=(f2o.send,))
     f1o_left, f1o_right = (ef1, ef1_sib, 0), (s1, pack1_sib, 1)
     f1o_away = slab_grad(f1o_left, f1o_right, None, 1 - y, (qkv.send,))
+    mid = mid.step((zs, 2, 2 * few, 4 * width), "x", order=(f1o_away,))
+    f2 = z_both(f2i, f2o, rows, hidden, order=(mid.send,))
     grad_input, sums_a, da_first, da_second, da1 = last_call(
         core,
         dx1,
@@ -1522,40 +1617,40 @@
         rows,
         d1,
         vectors(gains[0]),
-        order=(f1o_away,),
+        order=(f2.send,),
     )
     da_sib = (xor_send(da_first, "c", 1), xor_send(da_second, "c", 1))
-    f2i = z_steps(f2i, rows, hidden, high_z, order=(da1,))
-    f2o = z_steps(f2o, rows, hidden, high_z, order=(f2i.send,))
-    f1i = slab_sum((pack1, pack1_sib, 0), (da1, da_sib, 0), "x", order=(f2o.send,))
-    f1o = Sum(slab_grad(f1o_left, f1o_right, None, y, (f1i.kept,)), f1o_away, "y", 1)
-    mid = mid.step((zs, 2, few, 4 * width), "y", order=(f1o.kept,))
-    f1o = slab_second(f1o, "y", order=(mid.send,))
-    qkv = qkv.step((zs, 2, few, 3 * width), "y", order=(f1o.send,))
+    f2 = z_steps(f2, 2 * rows, hidden, high_z, order=(da1,))
+    f1o = Sum(slab_grad(f1o_left, f1o_right, None, y, (f2.send,), 10), f1o_away, "y", 1)
+    f1i = slab_sum((pack1, pack1_sib, 0), (da1, da_sib, 0), "x", order=(f1o.kept,))
+    grad_f2i, grad_f2o = finish_both(f2, rows, hidden, order=(f1i.kept,))
+    qkv = z_steps(qkv, 4 * few, 3 * width, low_z, order=(grad_f2i,))
+    f1o = slab_second(f1o, "y", order=(qkv.send,))
+    mid = mid.step((zs, 2, few, 4 * width), "y", order=(f1o.send,))
+    qkv = qkv.step((zs, 2, few, 3 * width), "y", order=(mid.send,))
     mid = z_steps(mid, few, 4 * width, low_z, order=(qkv.send,))
     f1i = slab_second(f1i, "x", order=(mid.send,))
-    qkv = z_steps(qkv, 2 * few, 3 * width, high_z, order=(f1i.send,))
-    f1o = z_steps(f1o, rows, hidden, low_z, order=(qkv.send,))
-    f1i = z_steps(f1i, rows, hidden, low_z, order=(f1o.send,))
-    mid = z_steps(mid, few, 4 * width, high_z, order=(f1i.send,))
-    qkv = qkv.step((1, 2, few, 3 * width), "x", order=(mid.send,))
-    f1o = z_steps(f1o, rows, hidden, high_z, order=(qkv.send,))
-    f1i = z_steps(f1i, rows, hidden, high_z, order=(f1o.send,))
-    grad_f2i = f2i.finish((rows, hidden), order=(f1i.send,))
-    grad_f2o = f2o.finish((rows, hidden), True, order=(f1i.send,))
-    mid = mid.finish((few, 4 * width), order=(f1i.send,))
+    f1o = z_steps(f1o, rows, hidden, low_z, order=(f1i.send,))
+    mid = z_steps(mid, few, 4 * width, high_z, order=(f1o.send,))
+    f1o = z_steps(f1o, rows, hidden, high_z, order=(mid.send,))
+    mid = mid.finish((few, 4 * width), order=(f1o.send,))
     out_att, out_cin, out_cout = mid[:, :width], mid[:, width : 3 * width], mid[:, 3 * width :]
-    out_qkv = qkv.finish((few, 3 * width), order=(f1i.send,))
-    grad_f1o = f1o.finish((rows, hidden), True, order=(f1i.send,))
-    grad_f1i = f1i.finish((rows, hidden))
-
+    qkv = z_steps(qkv, 2 * few, 3 * width, high_z, order=(mid,))
+    f1i = z_steps(f1i, rows, hidden, low_z, order=(qkv.send,))
+    f1i = z_steps(f1i, rows, hidden, high_z, order=(f1i.send,))
     a, b, c, p = 0, 1, 2, 3
     places = [(a, 0), (p, 0), (b, 0), (c, 4), (c, 2), (c, 0)]
     places += [(a, 1), (p, 1), (b, 1), (c, 5), (c, 3), (c, 1)]
     places += [(b, 2 + m) for m in range(KSIZE)] + [(p, 2)]
-    rows = stack_rows([sums_a, sums_b, sums_c, sums_p], places, order=(f1o.kept,))
-    rows = rows.reshape(rows.shape[0], devices, width // devices).transpose(1, 0, 2)
-    rows = jnp.sum(lax.all_to_all(rows, DEV, split_axis=0, concat_axis=0, tiled=True), axis=0)
+    sums = stack_rows([sums_a, sums_b, sums_c, sums_p], places, devices, order=(f1i.send,))
+    qkv = qkv.step((1, 2, few, 3 * width), "x", order=(sums,))
+    grad_f1o = f1o.finish((rows, hidden), True, order=(qkv.send,))
+    grad_f1i = f1i.finish((rows, hidden), order=(grad_f1o,))
+    out_qkv = qkv.finish((few, 3 * width), order=(grad_f1i,))
+    sums = lax.all_to_all(sums, DEV, split_axis=0, concat_axis=0, tiled=True)
+    gain_sums, bias_sums, tap_sums, query_sums = total_of(
+        sums, (6, 6, KSIZE, 1), order=(out_qkv,)
+    )
 
     return (
         final_out,
@@ -1564,14 +1659,14 @@
         grad_f1o,
         out_qkv,
         out_att,
-        rows[12 + KSIZE],
+        query_sums[0],
         out_cin,
         out_cout,
         grad_f2i,
         grad_f2o,
-        rows[12 : 12 + KSIZE],
-        rows[:6],
-        rows[6:12],
+        tap_sums,
+        gain_sums,
+        bias_sums,
     )
 
 

time: 829 us -> 807 us (0.973)
  waiting for transfers between devices: 329 us -> 366 us
  starting transfers between devices: 125 us -> 97 us
  blocking collectives: 38.2 us -> 14.5 us
    all_to_all x1 -> x0, blocking collectives: 23.6 us -> none  [to_frames(): return lax.all_to_all(cells, LAYER, split_axis=0, concat_axis=0, tiled=True)]
    ppermute x31 -> x29, starting transfers between devices: 53.1 us -> 30 us  [xor_send(): return lax.ppermute(cells, axis, [(i, i ^ bit) for i in range(count)])]
    all_to_all x2 -> x3, waiting for transfers between devices: 13.1 us -> 27.6 us  [to_frames(): return lax.all_to_all(cells, LAYER, split_axis=0, concat_axis=0, tiled=True)]
    ppermute x31 -> x29, waiting for transfers between devices: 87 us -> 99.2 us  [xor_send(): return lax.ppermute(cells, axis, [(i, i ^ bit) for i in range(count)])]
    pallas_call x20 -> x17, Pallas kernels: 25.3 us -> 21.8 us  [halve(): pl.pallas_call(functools.partial(halve_kernel, len(order)), grid_spec=plt...]
    unnamed x148 -> x124, local copies, waits for them, and re-layouts: 28.8 us -> 25.6 us
  transfers between devices with their start and end apart: 53 -> 52, of which waited for: 23 -> 21; matrix products, arithmetic and copies ran while one was open for 4% -> 4% of each run, Pallas kernels for 25% -> 25%
where the time goes in v3:
time: 807 us; the launch traced here: 796 us
  waiting for transfers between devices  366 us (45%)
  Pallas kernels  251 us (31%)
  starting transfers between devices  97 us (12%)
  local copies, waits for them, and re-layouts  44.8 us (6%)
  between operations  15.1 us (2%)
  blocking collectives  14.5 us (2%)
  other arithmetic  8.59 us (1%)
    all_gather x3, waiting for transfers between devices, gather(): lax.all_gather(mine, DEV, axis=0, tiled=True).reshape(devices, -1, width)  181 us
    ppermute x29, waiting for transfers between devices, xor_send(): return lax.ppermute(cells, axis, [(i, i ^ bit) for i in range(count)])  99.2 us
    pallas_call x8, Pallas kernels, slab_grad(): pl.pallas_call(functools.partial(slab_grad_kernel, split, len(order), pai...  43.8 us
    all_to_all x4, waiting for transfers between devices, to_heads(): got = lax.all_to_all(cells, LAYER, split_axis=0, concat_axis=0, tiled=True)  32.3 us
    pallas_call x1, Pallas kernels, second_call(): pl.pallas_call(second_kernel, grid_spec=pltpu.PrefetchScalarGridSpec(num_...  31.1 us
    ppermute x29, starting transfers between devices, xor_send(): return lax.ppermute(cells, axis, [(i, i ^ bit) for i in range(count)])  30 us
    pallas_call x1, Pallas kernels, attn_bwd(): pl.pallas_call(kernel, grid_spec=grid_spec, out_shape=[jax.ShapeDtypeStru...  27.8 us
    all_to_all x3, waiting for transfers between devices, to_frames(): return lax.all_to_all(cells, LAYER, split_axis=0, concat_axis=0, tiled=True)  27.6 us
  transfers between devices with their start and end apart: 52, of which 21 were waited for; matrix products, arithmetic and copies ran while one was open for 4% of the time, Pallas kernels for 25%

profile of v3, /device:TPU:0, one launch (start us, length us, event | category | flops | bytes accessed | tf_op | source)
XLA Modules:
  0.0 796.5 jit_solution(16948540225483626949)
XLA Ops:
  13.3 14.5 %all_to_all.55 = bf16[32,2,288]{2,1,0:T(2,128)(2,1)S(1)} all-to-all(bf16[32,2,288]{2,1,0:T(2,128)(2,1)S(1)} %reshape.389), channel_id=1, replica_groups=mesh['z'=4,'x'=2,'y'=2,'c'=2] {'z','x','y','c'}, dimensions={0} | all-to-all | bytes 73728 | tf_op jit(solution)/shard_map/all_to_all | solution.py:1434
  33.0 126.6 %all-gather.4.cloned.1.call-done = bf16[11264,1024]{1,0:T(8,128)(2,1)} async-done(((bf16[352,1024]{1,0:T(8,128)(2,1)}), bf16[11264,1024]{1,0:T(8,128)(2,1)}) %all-gather.4.cloned.1.call-update) | async-done | bytes 23068688 | tf_op jit(solution)/shard_map/all_gather | solution.py:1443
  159.7 20.5 %first_part.1 = (f32[384,1024]{1,0:T(8,128)}, bf16[384,1024]{1,0:T(8,128)(2,1)}, bf16[3,384,1024]{2,1,0:T(8,128)(2,1)}, bf16[2,384,1024]{2,1,0:T(8,128)(2,1)}, b...) custom-call(s32[1]{0:T(128)} %bitcast.core_ref, ...), custom_call_target="tpu_custom_call" | custom-call | flops 8858370048 | bytes 38797312 | tf_op jit(solution)/shard_map/first_part/pallas_call | solution.py:237
  187.1 15.2 %all-to-all-done.3 = bf16[8,384,128]{2,1,0:T(8,128)(2,1)} async-done(((bf16[8,384,128]{2,1,0:T(8,128)(2,1)}), bf16[8,384,128]{2,1,0:T(8,128)(2,1)}, u32[]{:S(2)}, u32[]{:S(2)}) %all-to-all-start.3) | async-done | bytes 786464 | tf_op jit(solution)/shard_map/all_to_all | solution.py:1514
  212.4 8.4 %all-to-all-done.2 = bf16[8,384,128]{2,1,0:T(8,128)(2,1)} async-done(((bf16[8,384,128]{2,1,0:T(8,128)(2,1)}), bf16[8,384,128]{2,1,0:T(8,128)(2,1)}, u32[]{:S(2)}, u32[]{:S(2)}) %all-to-all-start.2) | async-done | bytes 786464 | tf_op jit(solution)/shard_map/all_to_all | solution.py:1514
  232.9 8.7 %all-to-all-done.1 = bf16[8,384,128]{2,1,0:T(8,128)(2,1)} async-done(((bf16[8,384,128]{2,1,0:T(8,128)(2,1)}), bf16[8,384,128]{2,1,0:T(8,128)(2,1)}, u32[]{:S(2)}, u32[]{:S(2)}) %all-to-all-start.1) | async-done | bytes 786464 | tf_op jit(solution)/shard_map/all_to_all | solution.py:1514
  243.7 11.8 %collective-permute-done.1.refs_6_.refs_11_ = bf16[1536,128]{1,0:T(8,128)(2,1)} collective-permute-done((bf16[1536,128]{1,0:T(8,128)(2,1)}, bf16[1536,128]{1,0:T(8,128)(2,1)}, u32[]{:S(2)}, u32[]{:S(2)}) %collective-permute-start.1) | collective-permute-done | bytes 393248 | tf_op jit(solution)/shard_map/ppermute | solution.py:1525
  255.5 20.5 %attention_forward.1 = (bf16[3072,128]{1,0:T(8,128)(2,1)}, f32[1,3072]{1,0:T(1,128)}) custom-call(s32[6]{0:T(128)} %fusion.8.refs_0_, s32[6]{0:T(128)} %slice.223.refs_1_, f32[1]{0:T(128)} %bitcast.1.refs_2_, bf16[3072,128]{1,0:T(8,128)(2,1)} %bitcast.6.refs_3_, bf16[1536,128]{1,0:T(8,128)(2,1)} %collective-permute-done.refs_4_.refs_9_, ...), custom_call_target="tpu_custom_call" | custom-call | flops 1610612736 | bytes 3407872 | tf_op jit(solution)/shard_map/attention_forward/pallas_call | solution.py:890
  282.5 11.5 %all-to-all-done.4.mh_ref = bf16[8,384,128]{2,1,0:T(8,128)(2,1)} async-done(((bf16[8,384,128]{2,1,0:T(8,128)(2,1)}), bf16[8,384,128]{2,1,0:T(8,128)(2,1)}, u32[]{:S(2)}, u32[]{:S(2)}) %all-to-all-start.4) | async-done | bytes 786464 | tf_op jit(solution)/shard_map/all_to_all | solution.py:1519
  295.4 9.3 %attention_out_and_gate.1 = (bf16[384,1024]{1,0:T(8,128)(2,1)}, f32[384,1024]{1,0:T(8,128)}, bf16[384,1024]{1,0:T(8,128)(2,1)}, f32[384,1024]{1,0:T(8,128)}, f32...) custom-call(bf16[8,384,128]{2,1,0:T(8,128)(2,1)} %all-to-all-done.4.mh_ref, f32[384,1024]{1,0:T(8,128)} %get-tuple-element.109.x1_ref, ...), custom_call_target="tpu_custom_call" | custom-call | flops 2415919104 | bytes 15728640 | tf_op jit(solution)/shard_map/attention_out_and_gate/pallas_call | solution.py:303
  324.3 54.2 %all-gather.8.cloned.1.call-done = bf16[8192,1024]{1,0:T(8,128)(2,1)} async-done(((bf16[256,1024]{1,0:T(8,128)(2,1)}), bf16[8192,1024]{1,0:T(8,128)(2,1)}) %all-gather.8.cloned.1.call-update) | async-done | bytes 16777232 | tf_op jit(solution)/shard_map/all_gather | solution.py:1443
  379.3 31.1 %second_part.1 = (bf16[384,1024]{1,0:T(8,128)(2,1)}, bf16[384,1024]{1,0:T(8,128)(2,1)}, f32[384,1024]{1,0:T(8,128)}, bf16[384,1024]{1,0:T(8,128)(2,1)}, f32[384,...) custom-call(s32[1]{0:T(128)} %bitcast.core_ref, ...), custom_call_target="tpu_custom_call" | custom-call | flops 14495514624 | bytes 51380224 | tf_op jit(solution)/shard_map/second_part/pallas_call | solution.py:471
  432.4 15.3 %convolution_backward.1 = (bf16[384,2048]{1,0:T(8,128)(2,1)}, f32[384,1024]{1,0:T(8,128)}, bf16[384,1024]{1,0:T(8,128)(2,1)}, bf16[8,384,128]{2,1,0:T(8,128)(2,1)}, f32[8,1024]{1,0:T(8,128)}) custom-call(f32[384,1024]{1,0:T(8,128)} %get-tuple-element.116.dz_ref, f32[384,1024]{1,0:T(8,128)} %get-tuple-element.113.conv_ref, f32[4,1024]{1,0:T(4,128)} %copy-done.43, ...), custom_call_target="tpu_custom_call" | custom-call | flops 2415919104 | bytes 19660800 | tf_op jit(solution)/shard_map/convolution_backward/pallas_call | solution.py:617
  457.7 9.3 %row_grad.2 = (bf16[512,4096]{1,0:T(8,128)(2,1)}, bf16[512,4096]{1,0:T(8,128)(2,1)}) custom-call(s32[1]{0:T(128)} %bitcast.core_ref, bf16[384,1024]{1,0:T(8,128)(2,1)} %get-tuple-element.126.refs_0_, bf16[384,1024]{1,0:T(8,128)(2,1)} %get-tuple-element.127.refs_1_, bf16[384,1024]{1,0:T(8,128)(2,1)} %get-tuple-element.128.refs_2_, ...), custom_call_target="tpu_custom_call" | custom-call | flops 1024 | bytes 37001024 | tf_op jit(solution)/shard_map/row_grad/pallas_call | solution.py:1394
  478.7 27.8 %attention_backward.1 = (bf16[3072,128]{1,0:T(8,128)(2,1)}, bf16[1536,256]{1,0:T(8,128)(2,1)}, f32[3072,256]{1,0:T(8,128)}, bf16[1536,256]{1,0:T(8,128)(2,1)}) custom-call(s32[6]{0:T(128)} %fusion.8.refs_0_, s32[6]{0:T(128)} %slice.223.refs_1_, f32[1]{0:T(128)} %bitcast.1.refs_2_, bf16[3072,128]{1,0:T(8,128)(2,1)} %bitcast.6.refs_3_, ...), custom_call_target="tpu_custom_call" | custom-call | flops 32212254720 | bytes 6815744 | tf_op jit(solution)/shard_map/attention_backward/pallas_call | solution.py:1007
  545.3 16.1 %all-to-all-done.9.dkv_ref.refs_3_ = bf16[8,384,256]{2,1,0:T(8,128)(2,1)S(1)} async-done(((bf16[8,384,256]{2,1,0:T(8,128)(2,1)}), bf16[8,384,256]{2,1,0:T(8,128)(2,1)S(1)}, u32[]{:S(2)}, u32[]{:S(2)}) %all-to-all-start.9) | async-done | bytes 1572896 | tf_op jit(solution)/shard_map/all_to_all | solution.py:1519
  562.5 9.0 %projections_backward.1 = (f32[384,1024]{1,0:T(8,128)}, bf16[1,384,1024]{2,1,0:T(8,128)(2,1)}, f32[8,1024]{1,0:T(8,128)}) custom-call(bf16[8,384,128]{2,1,0:T(8,128)(2,1)} %all-to-all-done.8.dq_ref.refs_1_, bf16[8,384,256]{2,1,0:T(8,128)(2,1)} %copy-done.27, f32[384,1024]{1,0:T(8,128)} %get-tuple-element.139.dx2_ref, f32[384,1024]{1,0:T(8,128)} %get-tuple-element.109.x1_ref, ...), custom_call_target="tpu_custom_call" | custom-call | flops 1024 | bytes 33301024 | tf_op jit(solution)/shard_map/projections_backward/pallas_call | solution.py:718
  571.5 7.7 row_grad.3
  598.0 14.5 %last_part.1 = (bf16[384,1024]{1,0:T(8,128)(2,1)}, f32[8,1024]{1,0:T(8,128)}, bf16[1,384,1024]{2,1,0:T(8,128)(2,1)}, bf16[1,384,1024]{2,1,0:T(8,128)(2,1)}, bf16[2,384,1024]{2,1,0:T(8,128)(2,1)}) custom-call(s32[1]{0:T(128)} %bitcast.core_ref, f32[384,1024]{1,0:T(8,128)} %get-tuple-element.140.dx1_ref, ...), custom_call_target="tpu_custom_call" | custom-call | flops 1024 | bytes 55501024 | tf_op jit(solution)/shard_map/last_part/pallas_call | solution.py:771
  612.5 6.8 collective-permute-done.20
  664.1 28.0 %collective-permute-done.27 = bf16[2,128,3072]{2,1,0:T(8,128)(2,1)S(1)} collective-permute-done((bf16[2,128,3072]{2,1,0:T(8,128)(2,1)S(1)}, bf16[2,128,3072]{2,1,0:T(8,128)(2,1)S(1)}, u32[]{:S(2)}, u32[]{:S(2)}) %collective-permute-start.27) | collective-permute-done | bytes 1572896 | tf_op jit(solution)/shard_map/ppermute | solution.py:39
  698.6 13.5 %collective-permute-done.31 = bf16[4,128,1024]{2,1,0:T(8,128)(2,1)S(1)} collective-permute-done((bf16[4,128,1024]{2,1,0:T(8,128)(2,1)S(1)}, bf16[4,128,1024]{2,1,0:T(8,128)(2,1)S(1)}, u32[]{:S(2)}, u32[]{:S(2)}) %collective-permute-start.31) | collective-permute-done | bytes 1048608 | tf_op jit(solution)/shard_map/ppermute | solution.py:39
  715.8 14.6 %collective-permute-done.33 = bf16[2,128,1024]{2,1,0:T(8,128)(2,1)S(1)} collective-permute-done((bf16[2,128,1024]{2,1,0:T(8,128)(2,1)S(1)}, bf16[2,128,1024]{2,1,0:T(8,128)(2,1)S(1)}, u32[]{:S(2)}, u32[]{:S(2)}) %collective-permute-start.33) | collective-permute-done | bytes 524320 | tf_op jit(solution)/shard_map/ppermute | solution.py:39
  741.4 19.2 %collective-permute-done.34 = bf16[2,128,1024]{2,1,0:T(8,128)(2,1)S(1)} collective-permute-done((bf16[2,128,1024]{2,1,0:T(8,128)(2,1)S(1)}, bf16[2,128,1024]{2,1,0:T(8,128)(2,1)S(1)}, u32[]{:S(2)}, u32[]{:S(2)}) %collective-permute-start.34) | collective-permute-done | bytes 524320 | tf_op jit(solution)/shard_map/ppermute | solution.py:39
  (334 shorter events, 267.3 us)
Async XLA Ops:
  7.2 152.4 %all-gather.4.cloned.1.call-start = ((), (), s32[]{:S(2)}) async-start(), calls=%async_computation.11 | async-start | bytes 23789568 | tf_op jit(solution)/shard_map/all_gather | solution.py:1443
  12.2 270.3 %all-gather.6.cloned.1.call-start = ((), (), s32[]{:S(2)}) async-start(), calls=%async_computation.12 | async-start | bytes 8650752 | tf_op jit(solution)/shard_map/all_gather | solution.py:1443
  13.0 365.5 %all-gather.8.cloned.1.call-start = ((), (), s32[]{:S(2)}) async-start(), calls=%async_computation.13 | async-start | bytes 17301504 | tf_op jit(solution)/shard_map/all_gather | solution.py:1443
  184.8 109.3 %collective-permute-start.4 = (bf16[3,384,1024]{2,1,0:T(8,128)(2,1)}, bf16[3,384,1024]{2,1,0:T(8,128)(2,1)S(1)}, u32[]{:S(2)}, u32[]{:S(2)}) collective-permute-start(bf16[3,384,1024]{2,1,0:T(8,128)(2,1)} %get-tuple-element.110.la_ref), channel_id=1, source_target_pairs={{0,1},{1,0},{2,3},{3,2},{4,5},{5,4},{6,7},{7,6},{8,9},{9,8},{10,11... | collective-permute-start | bytes 7077896 | tf_op jit(solution)/shard_map/ppermute | solution.py:39
  209.0 32.6 %collective-permute-start.2 = (bf16[1536,128]{1,0:T(8,128)(2,1)S(1)}, bf16[1536,128]{1,0:T(8,128)(2,1)}, u32[]{:S(2)}, u32[]{:S(2)}) collective-permute-start(bf16[1536,128]{1,0:T(8,128)(2,1)S(1)} %bitcast.163), channel_id=1, source_target_pairs={{0,8},{8,16},{16,24},{1,9},{9,17},{17,25},{2,10},{10,18},{18,26},{... | collective-permute-start | bytes 1179656 | tf_op jit(solution)/shard_map/ppermute | solution.py:1525
  211.1 30.5 %collective-permute-start.3 = (bf16[1536,128]{1,0:T(8,128)(2,1)S(1)}, bf16[1536,128]{1,0:T(8,128)(2,1)}, u32[]{:S(2)}, u32[]{:S(2)}) collective-permute-start(bf16[1536,128]{1,0:T(8,128)(2,1)S(1)} %bitcast.162), channel_id=1, source_target_pairs={{8,0},{16,8},{24,16},{9,1},{17,9},{25,17},{10,2},{18,10},{26,18},{... | collective-permute-start | bytes 1179656 | tf_op jit(solution)/shard_map/ppermute | solution.py:1525
  316.5 62.1 %all-to-all-start.5 = ((f32[32,2,1024]{2,1,0:T(2,128)}), f32[32,2,1024]{2,1,0:T(2,128)S(1)}, u32[]{:S(2)}, u32[]{:S(2)}) async-start(f32[32,2,1024]{2,1,0:T(2,128)} %get-tuple-element.114), calls=%async_computation.5 | async-start | bytes 524288 | tf_op jit(solution)/shard_map/all_to_all | solution.py:1536
  447.7 30.1 %all-to-all-start.7 = ((bf16[8,384,128]{2,1,0:T(8,128)(2,1)}), bf16[8,384,128]{2,1,0:T(8,128)(2,1)S(1)}, u32[]{:S(2)}, u32[]{:S(2)}) async-start(bf16[8,384,128]{2,1,0:T(8,128)(2,1)} %get-tuple-element.124), calls=%async_computation.7 | async-start | bytes 1572864 | tf_op jit(solution)/shard_map/all_to_all | solution.py:1514
  454.2 64.0 %collective-permute-start.12 = (bf16[2,512,1024]{2,1,0:T(8,128)(2,1)}, bf16[2,512,1024]{2,1,0:T(8,128)(2,1)}, u32[]{:S(2)}, u32[]{:S(2)}) collective-permute-start(bf16[2,512,1024]{2,1,0:T(8,128)(2,1)} %slab_grad.8.refs_0_), channel_id=1, source_target_pairs={{0,4},{4,0},{1,5},{5,1},{2,6},{6,2},{3,7},{7,3},{8,12},{12,8},{9,1... | collective-permute-start | bytes 6291464 | tf_op jit(solution)/shard_map/ppermute | solution.py:39
  456.4 64.8 %collective-permute-start.13 = (bf16[2,512,1024]{2,1,0:T(8,128)(2,1)}, bf16[2,512,1024]{2,1,0:T(8,128)(2,1)}, u32[]{:S(2)}, u32[]{:S(2)}) collective-permute-start(bf16[2,512,1024]{2,1,0:T(8,128)(2,1)} %slab_grad.9.refs_1_.refs_0_), channel_id=1, source_target_pairs={{0,2},{2,0},{1,3},{3,1},{4,6},{6,4},{5,7},{7,5},{8,10},{10,8},{9,1... | collective-permute-start | bytes 6291464 | tf_op jit(solution)/shard_map/ppermute | solution.py:39
  467.1 118.0 %collective-permute-start.16 = (bf16[512,4096]{1,0:T(8,128)(2,1)}, bf16[512,4096]{1,0:T(8,128)(2,1)}, u32[]{:S(2)}, u32[]{:S(2)}) collective-permute-start(bf16[512,4096]{1,0:T(8,128)(2,1)} %get-tuple-element.145), channel_id=1, source_target_pairs={{0,1},{1,0},{2,3},{3,2},{4,5},{5,4},{6,7},{7,6},{8,9},{9,8},{10,11... | collective-permute-start | bytes 12582920 | tf_op jit(solution)/shard_map/ppermute | solution.py:39
  540.9 49.9 %collective-permute-start.14 = (bf16[1,512,1024]{2,1,0:T(8,128)(2,1)}, bf16[1,512,1024]{2,1,0:T(8,128)(2,1)}, u32[]{:S(2)}, u32[]{:S(2)}) collective-permute-start(bf16[1,512,1024]{2,1,0:T(8,128)(2,1)} %get-tuple-element.137.refs_0_), channel_id=1, source_target_pairs={{0,2},{2,0},{1,3},{3,1},{4,6},{6,4},{5,7},{7,5},{8,10},{10,8},{9,1... | collective-permute-start | bytes 3145736 | tf_op jit(solution)/shard_map/ppermute | solution.py:39
  543.0 47.9 %collective-permute-start.15 = (bf16[4,128,1024]{2,1,0:T(8,128)(2,1)}, bf16[4,128,1024]{2,1,0:T(8,128)(2,1)}, u32[]{:S(2)}, u32[]{:S(2)}) collective-permute-start(bf16[4,128,1024]{2,1,0:T(8,128)(2,1)} %get-tuple-element.138.refs_1_), channel_id=1, source_target_pairs={{0,4},{4,0},{1,5},{5,1},{2,6},{6,2},{3,7},{7,3},{8,12},{12,8},{9,1... | collective-permute-start | bytes 3145736 | tf_op jit(solution)/shard_map/ppermute | solution.py:39
  579.2 74.8 %collective-permute-start.24 = (bf16[512,3072]{1,0:T(8,128)(2,1)}, bf16[512,3072]{1,0:T(8,128)(2,1)S(1)}, u32[]{:S(2)}, u32[]{:S(2)}) collective-permute-start(bf16[512,3072]{1,0:T(8,128)(2,1)} %get-tuple-element.148.refs_0_), channel_id=1, source_target_pairs={{0,1},{1,0},{2,3},{3,2},{4,5},{5,4},{6,7},{7,6},{8,9},{9,8},{10,11... | collective-permute-start | bytes 9437192 | tf_op jit(solution)/shard_map/ppermute | solution.py:39
  596.0 59.9 %collective-permute-start.23 = (bf16[2,512,1024]{2,1,0:T(8,128)(2,1)}, bf16[2,512,1024]{2,1,0:T(8,128)(2,1)}, u32[]{:S(2)}, u32[]{:S(2)}) collective-permute-start(bf16[2,512,1024]{2,1,0:T(8,128)(2,1)} %slab_grad.12.refs_0_), channel_id=1, source_target_pairs={{0,2},{2,0},{1,3},{3,1},{4,6},{6,4},{5,7},{7,5},{8,10},{10,8},{9,1... | collective-permute-start | bytes 6291464 | tf_op jit(solution)/shard_map/ppermute | solution.py:39
  597.5 62.0 %collective-permute-start.22 = (bf16[4,64,4096]{2,1,0:T(8,128)(2,1)}, bf16[4,64,4096]{2,1,0:T(8,128)(2,1)}, u32[]{:S(2)}, u32[]{:S(2)}) collective-permute-start(bf16[4,64,4096]{2,1,0:T(8,128)(2,1)} %get-tuple-element.149.refs_8_), channel_id=1, source_target_pairs={{0,4},{4,0},{1,5},{5,1},{2,6},{6,2},{3,7},{7,3},{8,12},{12,8},{9,1... | collective-permute-start | bytes 6291464 | tf_op jit(solution)/shard_map/ppermute | solution.py:39
  638.4 54.5 %collective-permute-start.21 = (bf16[2,512,1024]{2,1,0:T(8,128)(2,1)}, bf16[2,512,1024]{2,1,0:T(8,128)(2,1)}, u32[]{:S(2)}, u32[]{:S(2)}) collective-permute-start(bf16[2,512,1024]{2,1,0:T(8,128)(2,1)} %slab_grad.14.refs_1_), channel_id=1, source_target_pairs={{0,4},{4,0},{1,5},{5,1},{2,6},{6,2},{3,7},{7,3},{8,12},{12,8},{9,1... | collective-permute-start | bytes 6291464 | tf_op jit(solution)/shard_map/ppermute | solution.py:39
  655.8 36.3 %collective-permute-start.27 = (bf16[2,128,3072]{2,1,0:T(8,128)(2,1)S(1)}, bf16[2,128,3072]{2,1,0:T(8,128)(2,1)S(1)}, u32[]{:S(2)}, u32[]{:S(2)}) collective-permute-start(bf16[2,128,3072]{2,1,0:T(8,128)(2,1)S(1)} %get-tuple-element.161.refs_0_), channel_id=1, source_target_pairs={{0,8},{8,0},{16,24},{24,16},{1,9},{9,1},{17,25},{25,17},{2,10},{10... | collective-permute-start | bytes 4718600 | tf_op jit(solution)/shard_map/ppermute | solution.py:39
  662.0 30.5 %collective-permute-start.26 = (bf16[4,32,4096]{2,1,0:T(8,128)(2,1)S(1)}, bf16[4,32,4096]{2,1,0:T(8,128)(2,1)S(1)}, u32[]{:S(2)}, u32[]{:S(2)}) collective-permute-start(bf16[4,32,4096]{2,1,0:T(8,128)(2,1)S(1)} %get-tuple-element.164.refs_0_), channel_id=1, source_target_pairs={{0,2},{2,0},{1,3},{3,1},{4,6},{6,4},{5,7},{7,5},{8,10},{10,8},{9,1... | collective-permute-start | bytes 3145736 | tf_op jit(solution)/shard_map/ppermute | solution.py:39
  663.6 48.5 %collective-permute-start.31 = (bf16[4,128,1024]{2,1,0:T(8,128)(2,1)S(1)}, bf16[4,128,1024]{2,1,0:T(8,128)(2,1)S(1)}, u32[]{:S(2)}, u32[]{:S(2)}) collective-permute-start(bf16[4,128,1024]{2,1,0:T(8,128)(2,1)S(1)} %get-tuple-element.162.refs_0_), channel_id=1, source_target_pairs={{0,4},{4,0},{1,5},{5,1},{2,6},{6,2},{3,7},{7,3},{8,12},{12,8},{9,1... | collective-permute-start | bytes 3145736 | tf_op jit(solution)/shard_map/ppermute | solution.py:39
  696.2 41.3 %collective-permute-start.28 = (bf16[1,512,1024]{2,1,0:T(8,128)(2,1)S(1)}, bf16[1,512,1024]{2,1,0:T(8,128)(2,1)S(1)}, u32[]{:S(2)}, u32[]{:S(2)}) collective-permute-start(bf16[1,512,1024]{2,1,0:T(8,128)(2,1)S(1)} %get-tuple-element.169.refs_0_), channel_id=1, source_target_pairs={{0,2},{2,0},{1,3},{3,1},{4,6},{6,4},{5,7},{7,5},{8,10},{10,8},{9,1... | collective-permute-start | bytes 3145736 | tf_op jit(solution)/shard_map/ppermute | solution.py:39
  698.1 39.3 %collective-permute-start.29 = (bf16[4,32,3072]{2,1,0:T(8,128)(2,1)S(1)}, bf16[4,32,3072]{2,1,0:T(8,128)(2,1)S(1)}, u32[]{:S(2)}, u32[]{:S(2)}) collective-permute-start(bf16[4,32,3072]{2,1,0:T(8,128)(2,1)S(1)} %get-tuple-element.166.refs_0_), channel_id=1, source_target_pairs={{0,2},{2,0},{1,3},{3,1},{4,6},{6,4},{5,7},{7,5},{8,10},{10,8},{9,1... | collective-permute-start | bytes 2359304 | tf_op jit(solution)/shard_map/ppermute | solution.py:39
  738.4 32.6 %collective-permute-start.37 = (bf16[1,64,3072]{2,1,0:T(8,128)(2,1)S(1)}, bf16[1,64,3072]{2,1,0:T(8,128)(2,1)S(1)}, u32[]{:S(2)}, u32[]{:S(2)}) collective-permute-start(bf16[1,64,3072]{2,1,0:T(8,128)(2,1)S(1)} %get-tuple-element.178.refs_0_), channel_id=1, source_target_pairs={{0,16},{8,24},{16,0},{24,8},{1,17},{9,25},{17,1},{25,9},{2,18},{10... | collective-permute-start | bytes 1179656 | tf_op jit(solution)/shard_map/ppermute | solution.py:39
  740.5 37.1 %collective-permute-start.36 = (bf16[1,128,1024]{2,1,0:T(8,128)(2,1)S(1)}, bf16[1,128,1024]{2,1,0:T(8,128)(2,1)S(1)}, u32[]{:S(2)}, u32[]{:S(2)}) collective-permute-start(bf16[1,128,1024]{2,1,0:T(8,128)(2,1)S(1)} %get-tuple-element.177.refs_0_), channel_id=1, source_target_pairs={{0,16},{8,24},{16,0},{24,8},{1,17},{9,25},{17,1},{25,9},{2,18},{10... | collective-permute-start | bytes 786440 | tf_op jit(solution)/shard_map/ppermute | solution.py:39
  (88 other events, 1000.7 us)
Sparse Core Ops, SparseCore 0:
  12.3 147.2 all-gather.3
  163.1 93.8 all-gather.5
  260.4 118.1 all-gather.7

commit v4 on v3

--- a/solution.py
+++ b/solution.py
@@ -1627,7 +1627,7 @@
     qkv = z_steps(qkv, 4 * few, 3 * width, low_z, order=(grad_f2i,))
     f1o = slab_second(f1o, "y", order=(qkv.send,))
     mid = mid.step((zs, 2, few, 4 * width), "y", order=(f1o.send,))
-    qkv = qkv.step((zs, 2, few, 3 * width), "y", order=(mid.send,))
+    qkv = qkv.step((zs // 2, 2, 2 * few, 3 * width), "x", order=(mid.send,))
     mid = z_steps(mid, few, 4 * width, low_z, order=(qkv.send,))
     f1i = slab_second(f1i, "x", order=(mid.send,))
     f1o = z_steps(f1o, rows, hidden, low_z, order=(f1i.send,))
@@ -1635,7 +1635,7 @@
     f1o = z_steps(f1o, rows, hidden, high_z, order=(mid.send,))
     mid = mid.finish((few, 4 * width), order=(f1o.send,))
     out_att, out_cin, out_cout = mid[:, :width], mid[:, width : 3 * width], mid[:, 3 * width :]
-    qkv = z_steps(qkv, 2 * few, 3 * width, high_z, order=(mid,))
+    qkv = qkv.step((zs // 2, 2, few, 3 * width), "y", order=(mid,))
     f1i = z_steps(f1i, rows, hidden, low_z, order=(qkv.send,))
     f1i = z_steps(f1i, rows, hidden, high_z, order=(f1i.send,))
     a, b, c, p = 0, 1, 2, 3
@@ -1643,7 +1643,7 @@
     places += [(a, 1), (p, 1), (b, 1), (c, 5), (c, 3), (c, 1)]
     places += [(b, 2 + m) for m in range(KSIZE)] + [(p, 2)]
     sums = stack_rows([sums_a, sums_b, sums_c, sums_p], places, devices, order=(f1i.send,))
-    qkv = qkv.step((1, 2, few, 3 * width), "x", order=(sums,))
+    qkv = z_steps(qkv, few, 3 * width, high_z, order=(sums,))
     grad_f1o = f1o.finish((rows, hidden), True, order=(qkv.send,))
     grad_f1i = f1i.finish((rows, hidden), order=(grad_f1o,))
     out_qkv = qkv.finish((few, 3 * width), order=(grad_f1i,))

time: 807 us -> 794 us (0.984)
  waiting for transfers between devices: 366 us -> 350 us
    ppermute x29, waiting for transfers between devices: 99.2 us -> 82.5 us  [xor_send(): return lax.ppermute(cells, axis, [(i, i ^ bit) for i in range(count)])]
  transfers between devices with their start and end apart: 52 -> 52, of which waited for: 21 -> 18; matrix products, arithmetic and copies ran while one was open for 4% -> 4% of each run, Pallas kernels for 25% -> 26%
where the time goes in v4:
time: 794 us; the launch traced here: 786 us
  waiting for transfers between devices  350 us (44%)
  Pallas kernels  256 us (32%)
  starting transfers between devices  96 us (12%)
  local copies, waits for them, and re-layouts  44.8 us (6%)
  between operations  15.1 us (2%)
  blocking collectives  14.5 us (2%)
  other arithmetic  8.59 us (1%)
    all_gather x3, waiting for transfers between devices, gather(): lax.all_gather(mine, DEV, axis=0, tiled=True).reshape(devices, -1, width)  178 us
    ppermute x29, waiting for transfers between devices, xor_send(): return lax.ppermute(cells, axis, [(i, i ^ bit) for i in range(count)])  82.5 us
    pallas_call x8, Pallas kernels, slab_grad(): pl.pallas_call(functools.partial(slab_grad_kernel, split, len(order), pai...  43.8 us
    all_to_all x4, waiting for transfers between devices, to_heads(): got = lax.all_to_all(cells, LAYER, split_axis=0, concat_axis=0, tiled=True)  32.3 us
    ppermute x29, starting transfers between devices, xor_send(): return lax.ppermute(cells, axis, [(i, i ^ bit) for i in range(count)])  32.2 us
    pallas_call x1, Pallas kernels, second_call(): pl.pallas_call(second_kernel, grid_spec=pltpu.PrefetchScalarGridSpec(num_...  31.1 us
    pallas_call x1, Pallas kernels, attn_bwd(): pl.pallas_call(kernel, grid_spec=grid_spec, out_shape=[jax.ShapeDtypeStru...  31 us
    all_to_all x3, waiting for transfers between devices, to_frames(): return lax.all_to_all(cells, LAYER, split_axis=0, concat_axis=0, tiled=True)  29.8 us
  transfers between devices with their start and end apart: 52, of which 18 were waited for; matrix products, arithmetic and copies ran while one was open for 4% of the time, Pallas kernels for 26%

profile of v4, /device:TPU:0, one launch (start us, length us, event | category | flops | bytes accessed | tf_op | source)
XLA Modules:
  0.0 785.6 jit_solution(7223071759766759007)
XLA Ops:
  13.3 14.5 %all_to_all.55 = bf16[32,2,288]{2,1,0:T(2,128)(2,1)S(1)} all-to-all(bf16[32,2,288]{2,1,0:T(2,128)(2,1)S(1)} %reshape.389), channel_id=1, replica_groups=mesh['z'=4,'x'=2,'y'=2,'c'=2] {'z','x','y','c'}, dimensions={0} | all-to-all | bytes 73728 | tf_op jit(solution)/shard_map/all_to_all | solution.py:1434
  33.0 126.6 %all-gather.4.cloned.1.call-done = bf16[11264,1024]{1,0:T(8,128)(2,1)} async-done(((bf16[352,1024]{1,0:T(8,128)(2,1)}), bf16[11264,1024]{1,0:T(8,128)(2,1)}) %all-gather.4.cloned.1.call-update) | async-done | bytes 23068688 | tf_op jit(solution)/shard_map/all_gather | solution.py:1443
  159.7 20.5 %first_part.1 = (f32[384,1024]{1,0:T(8,128)}, bf16[384,1024]{1,0:T(8,128)(2,1)}, bf16[3,384,1024]{2,1,0:T(8,128)(2,1)}, bf16[2,384,1024]{2,1,0:T(8,128)(2,1)}, b...) custom-call(s32[1]{0:T(128)} %bitcast.core_ref, ...), custom_call_target="tpu_custom_call" | custom-call | flops 8858370048 | bytes 38797312 | tf_op jit(solution)/shard_map/first_part/pallas_call | solution.py:237
  187.1 15.2 %all-to-all-done.3 = bf16[8,384,128]{2,1,0:T(8,128)(2,1)} async-done(((bf16[8,384,128]{2,1,0:T(8,128)(2,1)}), bf16[8,384,128]{2,1,0:T(8,128)(2,1)}, u32[]{:S(2)}, u32[]{:S(2)}) %all-to-all-start.3) | async-done | bytes 786464 | tf_op jit(solution)/shard_map/all_to_all | solution.py:1514
  212.4 8.4 %all-to-all-done.2 = bf16[8,384,128]{2,1,0:T(8,128)(2,1)} async-done(((bf16[8,384,128]{2,1,0:T(8,128)(2,1)}), bf16[8,384,128]{2,1,0:T(8,128)(2,1)}, u32[]{:S(2)}, u32[]{:S(2)}) %all-to-all-start.2) | async-done | bytes 786464 | tf_op jit(solution)/shard_map/all_to_all | solution.py:1514
  232.9 8.7 %all-to-all-done.1 = bf16[8,384,128]{2,1,0:T(8,128)(2,1)} async-done(((bf16[8,384,128]{2,1,0:T(8,128)(2,1)}), bf16[8,384,128]{2,1,0:T(8,128)(2,1)}, u32[]{:S(2)}, u32[]{:S(2)}) %all-to-all-start.1) | async-done | bytes 786464 | tf_op jit(solution)/shard_map/all_to_all | solution.py:1514
  243.7 11.8 %collective-permute-done.1.refs_6_.refs_11_ = bf16[1536,128]{1,0:T(8,128)(2,1)} collective-permute-done((bf16[1536,128]{1,0:T(8,128)(2,1)}, bf16[1536,128]{1,0:T(8,128)(2,1)}, u32[]{:S(2)}, u32[]{:S(2)}) %collective-permute-start.1) | collective-permute-done | bytes 393248 | tf_op jit(solution)/shard_map/ppermute | solution.py:1525
  255.5 23.0 %attention_forward.1 = (bf16[3072,128]{1,0:T(8,128)(2,1)}, f32[1,3072]{1,0:T(1,128)}) custom-call(s32[6]{0:T(128)} %fusion.8.refs_0_, s32[6]{0:T(128)} %slice.223.refs_1_, f32[1]{0:T(128)} %bitcast.1.refs_2_, bf16[3072,128]{1,0:T(8,128)(2,1)} %bitcast.6.refs_3_, bf16[1536,128]{1,0:T(8,128)(2,1)} %collective-permute-done.refs_4_.refs_9_, ...), custom_call_target="tpu_custom_call" | custom-call | flops 1610612736 | bytes 3407872 | tf_op jit(solution)/shard_map/attention_forward/pallas_call | solution.py:890
  285.1 13.8 %all-to-all-done.4.mh_ref = bf16[8,384,128]{2,1,0:T(8,128)(2,1)} async-done(((bf16[8,384,128]{2,1,0:T(8,128)(2,1)}), bf16[8,384,128]{2,1,0:T(8,128)(2,1)}, u32[]{:S(2)}, u32[]{:S(2)}) %all-to-all-start.4) | async-done | bytes 786464 | tf_op jit(solution)/shard_map/all_to_all | solution.py:1519
  300.2 9.3 %attention_out_and_gate.1 = (bf16[384,1024]{1,0:T(8,128)(2,1)}, f32[384,1024]{1,0:T(8,128)}, bf16[384,1024]{1,0:T(8,128)(2,1)}, f32[384,1024]{1,0:T(8,128)}, f32...) custom-call(bf16[8,384,128]{2,1,0:T(8,128)(2,1)} %all-to-all-done.4.mh_ref, f32[384,1024]{1,0:T(8,128)} %get-tuple-element.109.x1_ref, ...), custom_call_target="tpu_custom_call" | custom-call | flops 2415919104 | bytes 15728640 | tf_op jit(solution)/shard_map/attention_out_and_gate/pallas_call | solution.py:303
  328.4 51.3 %all-gather.8.cloned.1.call-done = bf16[8192,1024]{1,0:T(8,128)(2,1)} async-done(((bf16[256,1024]{1,0:T(8,128)(2,1)}), bf16[8192,1024]{1,0:T(8,128)(2,1)}) %all-gather.8.cloned.1.call-update) | async-done | bytes 16777232 | tf_op jit(solution)/shard_map/all_gather | solution.py:1443
  380.5 31.1 %second_part.1 = (bf16[384,1024]{1,0:T(8,128)(2,1)}, bf16[384,1024]{1,0:T(8,128)(2,1)}, f32[384,1024]{1,0:T(8,128)}, bf16[384,1024]{1,0:T(8,128)(2,1)}, f32[384,...) custom-call(s32[1]{0:T(128)} %bitcast.core_ref, ...), custom_call_target="tpu_custom_call" | custom-call | flops 14495514624 | bytes 51380224 | tf_op jit(solution)/shard_map/second_part/pallas_call | solution.py:471
  433.6 15.3 %convolution_backward.1 = (bf16[384,2048]{1,0:T(8,128)(2,1)}, f32[384,1024]{1,0:T(8,128)}, bf16[384,1024]{1,0:T(8,128)(2,1)}, bf16[8,384,128]{2,1,0:T(8,128)(2,1)}, f32[8,1024]{1,0:T(8,128)}) custom-call(f32[384,1024]{1,0:T(8,128)} %get-tuple-element.116.dz_ref, f32[384,1024]{1,0:T(8,128)} %get-tuple-element.113.conv_ref, f32[4,1024]{1,0:T(4,128)} %copy-done.43, ...), custom_call_target="tpu_custom_call" | custom-call | flops 2415919104 | bytes 19660800 | tf_op jit(solution)/shard_map/convolution_backward/pallas_call | solution.py:617
  458.9 9.3 %row_grad.2 = (bf16[512,4096]{1,0:T(8,128)(2,1)}, bf16[512,4096]{1,0:T(8,128)(2,1)}) custom-call(s32[1]{0:T(128)} %bitcast.core_ref, bf16[384,1024]{1,0:T(8,128)(2,1)} %get-tuple-element.126.refs_0_, bf16[384,1024]{1,0:T(8,128)(2,1)} %get-tuple-element.127.refs_1_, bf16[384,1024]{1,0:T(8,128)(2,1)} %get-tuple-element.128.refs_2_, ...), custom_call_target="tpu_custom_call" | custom-call | flops 1024 | bytes 37001024 | tf_op jit(solution)/shard_map/row_grad/pallas_call | solution.py:1394
  479.9 31.0 %attention_backward.1 = (bf16[3072,128]{1,0:T(8,128)(2,1)}, bf16[1536,256]{1,0:T(8,128)(2,1)}, f32[3072,256]{1,0:T(8,128)}, bf16[1536,256]{1,0:T(8,128)(2,1)}) custom-call(s32[6]{0:T(128)} %fusion.8.refs_0_, s32[6]{0:T(128)} %slice.223.refs_1_, f32[1]{0:T(128)} %bitcast.1.refs_2_, bf16[3072,128]{1,0:T(8,128)(2,1)} %bitcast.6.refs_3_, ...), custom_call_target="tpu_custom_call" | custom-call | flops 32212254720 | bytes 6815744 | tf_op jit(solution)/shard_map/attention_backward/pallas_call | solution.py:1007
  547.6 16.1 %all-to-all-done.9.dkv_ref.refs_3_ = bf16[8,384,256]{2,1,0:T(8,128)(2,1)S(1)} async-done(((bf16[8,384,256]{2,1,0:T(8,128)(2,1)}), bf16[8,384,256]{2,1,0:T(8,128)(2,1)S(1)}, u32[]{:S(2)}, u32[]{:S(2)}) %all-to-all-start.9) | async-done | bytes 1572896 | tf_op jit(solution)/shard_map/all_to_all | solution.py:1519
  564.9 9.0 %projections_backward.1 = (f32[384,1024]{1,0:T(8,128)}, bf16[1,384,1024]{2,1,0:T(8,128)(2,1)}, f32[8,1024]{1,0:T(8,128)}) custom-call(bf16[8,384,128]{2,1,0:T(8,128)(2,1)} %all-to-all-done.8.dq_ref.refs_1_, bf16[8,384,256]{2,1,0:T(8,128)(2,1)} %copy-done.27, f32[384,1024]{1,0:T(8,128)} %get-tuple-element.139.dx2_ref, f32[384,1024]{1,0:T(8,128)} %get-tuple-element.109.x1_ref, ...), custom_call_target="tpu_custom_call" | custom-call | flops 1024 | bytes 33301024 | tf_op jit(solution)/shard_map/projections_backward/pallas_call | solution.py:718
  573.8 7.7 row_grad.3
  600.3 14.5 %last_part.1 = (bf16[384,1024]{1,0:T(8,128)(2,1)}, f32[8,1024]{1,0:T(8,128)}, bf16[1,384,1024]{2,1,0:T(8,128)(2,1)}, bf16[1,384,1024]{2,1,0:T(8,128)(2,1)}, bf16[2,384,1024]{2,1,0:T(8,128)(2,1)}) custom-call(s32[1]{0:T(128)} %bitcast.core_ref, f32[384,1024]{1,0:T(8,128)} %get-tuple-element.140.dx1_ref, ...), custom_call_target="tpu_custom_call" | custom-call | flops 1024 | bytes 55501024 | tf_op jit(solution)/shard_map/last_part/pallas_call | solution.py:771
  614.8 6.8 collective-permute-done.20
  666.4 28.0 %collective-permute-done.27 = bf16[2,128,3072]{2,1,0:T(8,128)(2,1)S(1)} collective-permute-done((bf16[2,128,3072]{2,1,0:T(8,128)(2,1)S(1)}, bf16[2,128,3072]{2,1,0:T(8,128)(2,1)S(1)}, u32[]{:S(2)}, u32[]{:S(2)}) %collective-permute-start.27) | collective-permute-done | bytes 1572896 | tf_op jit(solution)/shard_map/ppermute | solution.py:39
  700.9 15.1 %collective-permute-done.31 = bf16[4,128,1024]{2,1,0:T(8,128)(2,1)S(1)} collective-permute-done((bf16[4,128,1024]{2,1,0:T(8,128)(2,1)S(1)}, bf16[4,128,1024]{2,1,0:T(8,128)(2,1)S(1)}, u32[]{:S(2)}, u32[]{:S(2)}) %collective-permute-start.31) | collective-permute-done | bytes 1048608 | tf_op jit(solution)/shard_map/ppermute | solution.py:39
  719.7 13.0 %collective-permute-done.33 = bf16[2,128,1024]{2,1,0:T(8,128)(2,1)S(1)} collective-permute-done((bf16[2,128,1024]{2,1,0:T(8,128)(2,1)S(1)}, bf16[2,128,1024]{2,1,0:T(8,128)(2,1)S(1)}, u32[]{:S(2)}, u32[]{:S(2)}) %collective-permute-start.33) | collective-permute-done | bytes 524320 | tf_op jit(solution)/shard_map/ppermute | solution.py:39
  737.3 14.2 %collective-permute-done.34 = bf16[2,128,1024]{2,1,0:T(8,128)(2,1)S(1)} collective-permute-done((bf16[2,128,1024]{2,1,0:T(8,128)(2,1)S(1)}, bf16[2,128,1024]{2,1,0:T(8,128)(2,1)S(1)}, u32[]{:S(2)}, u32[]{:S(2)}) %collective-permute-start.34) | collective-permute-done | bytes 524320 | tf_op jit(solution)/shard_map/ppermute | solution.py:39
  (334 shorter events, 256.3 us)
Async XLA Ops:
  7.2 152.4 %all-gather.4.cloned.1.call-start = ((), (), s32[]{:S(2)}) async-start(), calls=%async_computation.11 | async-start | bytes 23789568 | tf_op jit(solution)/shard_map/all_gather | solution.py:1443
  12.2 272.9 %all-gather.6.cloned.1.call-start = ((), (), s32[]{:S(2)}) async-start(), calls=%async_computation.12 | async-start | bytes 8650752 | tf_op jit(solution)/shard_map/all_gather | solution.py:1443
  13.0 366.7 %all-gather.8.cloned.1.call-start = ((), (), s32[]{:S(2)}) async-start(), calls=%async_computation.13 | async-start | bytes 17301504 | tf_op jit(solution)/shard_map/all_gather | solution.py:1443
  184.8 114.1 %collective-permute-start.4 = (bf16[3,384,1024]{2,1,0:T(8,128)(2,1)}, bf16[3,384,1024]{2,1,0:T(8,128)(2,1)S(1)}, u32[]{:S(2)}, u32[]{:S(2)}) collective-permute-start(bf16[3,384,1024]{2,1,0:T(8,128)(2,1)} %get-tuple-element.110.la_ref), channel_id=1, source_target_pairs={{0,1},{1,0},{2,3},{3,2},{4,5},{5,4},{6,7},{7,6},{8,9},{9,8},{10,11... | collective-permute-start | bytes 7077896 | tf_op jit(solution)/shard_map/ppermute | solution.py:39
  209.0 32.6 %collective-permute-start.2 = (bf16[1536,128]{1,0:T(8,128)(2,1)S(1)}, bf16[1536,128]{1,0:T(8,128)(2,1)}, u32[]{:S(2)}, u32[]{:S(2)}) collective-permute-start(bf16[1536,128]{1,0:T(8,128)(2,1)S(1)} %bitcast.163), channel_id=1, source_target_pairs={{0,8},{8,16},{16,24},{1,9},{9,17},{17,25},{2,10},{10,18},{18,26},{... | collective-permute-start | bytes 1179656 | tf_op jit(solution)/shard_map/ppermute | solution.py:1525
  211.1 30.5 %collective-permute-start.3 = (bf16[1536,128]{1,0:T(8,128)(2,1)S(1)}, bf16[1536,128]{1,0:T(8,128)(2,1)}, u32[]{:S(2)}, u32[]{:S(2)}) collective-permute-start(bf16[1536,128]{1,0:T(8,128)(2,1)S(1)} %bitcast.162), channel_id=1, source_target_pairs={{8,0},{16,8},{24,16},{9,1},{17,9},{25,17},{10,2},{18,10},{26,18},{... | collective-permute-start | bytes 1179656 | tf_op jit(solution)/shard_map/ppermute | solution.py:1525
  321.3 58.5 %all-to-all-start.5 = ((f32[32,2,1024]{2,1,0:T(2,128)}), f32[32,2,1024]{2,1,0:T(2,128)S(1)}, u32[]{:S(2)}, u32[]{:S(2)}) async-start(f32[32,2,1024]{2,1,0:T(2,128)} %get-tuple-element.114), calls=%async_computation.5 | async-start | bytes 524288 | tf_op jit(solution)/shard_map/all_to_all | solution.py:1536
  448.9 30.1 %all-to-all-start.7 = ((bf16[8,384,128]{2,1,0:T(8,128)(2,1)}), bf16[8,384,128]{2,1,0:T(8,128)(2,1)S(1)}, u32[]{:S(2)}, u32[]{:S(2)}) async-start(bf16[8,384,128]{2,1,0:T(8,128)(2,1)} %get-tuple-element.124), calls=%async_computation.7 | async-start | bytes 1572864 | tf_op jit(solution)/shard_map/all_to_all | solution.py:1514
  455.4 65.1 %collective-permute-start.12 = (bf16[2,512,1024]{2,1,0:T(8,128)(2,1)}, bf16[2,512,1024]{2,1,0:T(8,128)(2,1)}, u32[]{:S(2)}, u32[]{:S(2)}) collective-permute-start(bf16[2,512,1024]{2,1,0:T(8,128)(2,1)} %slab_grad.8.refs_0_), channel_id=1, source_target_pairs={{0,4},{4,0},{1,5},{5,1},{2,6},{6,2},{3,7},{7,3},{8,12},{12,8},{9,1... | collective-permute-start | bytes 6291464 | tf_op jit(solution)/shard_map/ppermute | solution.py:39
  457.7 65.8 %collective-permute-start.13 = (bf16[2,512,1024]{2,1,0:T(8,128)(2,1)}, bf16[2,512,1024]{2,1,0:T(8,128)(2,1)}, u32[]{:S(2)}, u32[]{:S(2)}) collective-permute-start(bf16[2,512,1024]{2,1,0:T(8,128)(2,1)} %slab_grad.9.refs_1_.refs_0_), channel_id=1, source_target_pairs={{0,2},{2,0},{1,3},{3,1},{4,6},{6,4},{5,7},{7,5},{8,10},{10,8},{9,1... | collective-permute-start | bytes 6291464 | tf_op jit(solution)/shard_map/ppermute | solution.py:39
  468.3 119.1 %collective-permute-start.16 = (bf16[512,4096]{1,0:T(8,128)(2,1)}, bf16[512,4096]{1,0:T(8,128)(2,1)}, u32[]{:S(2)}, u32[]{:S(2)}) collective-permute-start(bf16[512,4096]{1,0:T(8,128)(2,1)} %get-tuple-element.145), channel_id=1, source_target_pairs={{0,1},{1,0},{2,3},{3,2},{4,5},{5,4},{6,7},{7,6},{8,9},{9,8},{10,11... | collective-permute-start | bytes 12582920 | tf_op jit(solution)/shard_map/ppermute | solution.py:39
  543.2 49.9 %collective-permute-start.14 = (bf16[1,512,1024]{2,1,0:T(8,128)(2,1)}, bf16[1,512,1024]{2,1,0:T(8,128)(2,1)}, u32[]{:S(2)}, u32[]{:S(2)}) collective-permute-start(bf16[1,512,1024]{2,1,0:T(8,128)(2,1)} %get-tuple-element.137.refs_0_), channel_id=1, source_target_pairs={{0,2},{2,0},{1,3},{3,1},{4,6},{6,4},{5,7},{7,5},{8,10},{10,8},{9,1... | collective-permute-start | bytes 3145736 | tf_op jit(solution)/shard_map/ppermute | solution.py:39
  545.3 47.9 %collective-permute-start.15 = (bf16[4,128,1024]{2,1,0:T(8,128)(2,1)}, bf16[4,128,1024]{2,1,0:T(8,128)(2,1)}, u32[]{:S(2)}, u32[]{:S(2)}) collective-permute-start(bf16[4,128,1024]{2,1,0:T(8,128)(2,1)} %get-tuple-element.138.refs_1_), channel_id=1, source_target_pairs={{0,4},{4,0},{1,5},{5,1},{2,6},{6,2},{3,7},{7,3},{8,12},{12,8},{9,1... | collective-permute-start | bytes 3145736 | tf_op jit(solution)/shard_map/ppermute | solution.py:39
  581.5 74.8 %collective-permute-start.24 = (bf16[512,3072]{1,0:T(8,128)(2,1)}, bf16[512,3072]{1,0:T(8,128)(2,1)S(1)}, u32[]{:S(2)}, u32[]{:S(2)}) collective-permute-start(bf16[512,3072]{1,0:T(8,128)(2,1)} %get-tuple-element.148.refs_0_), channel_id=1, source_target_pairs={{0,1},{1,0},{2,3},{3,2},{4,5},{5,4},{6,7},{7,6},{8,9},{9,8},{10,11... | collective-permute-start | bytes 9437192 | tf_op jit(solution)/shard_map/ppermute | solution.py:39
  598.3 59.9 %collective-permute-start.23 = (bf16[2,512,1024]{2,1,0:T(8,128)(2,1)}, bf16[2,512,1024]{2,1,0:T(8,128)(2,1)}, u32[]{:S(2)}, u32[]{:S(2)}) collective-permute-start(bf16[2,512,1024]{2,1,0:T(8,128)(2,1)} %slab_grad.12.refs_0_), channel_id=1, source_target_pairs={{0,2},{2,0},{1,3},{3,1},{4,6},{6,4},{5,7},{7,5},{8,10},{10,8},{9,1... | collective-permute-start | bytes 6291464 | tf_op jit(solution)/shard_map/ppermute | solution.py:39
  599.8 62.0 %collective-permute-start.22 = (bf16[4,64,4096]{2,1,0:T(8,128)(2,1)}, bf16[4,64,4096]{2,1,0:T(8,128)(2,1)}, u32[]{:S(2)}, u32[]{:S(2)}) collective-permute-start(bf16[4,64,4096]{2,1,0:T(8,128)(2,1)} %get-tuple-element.149.refs_8_), channel_id=1, source_target_pairs={{0,4},{4,0},{1,5},{5,1},{2,6},{6,2},{3,7},{7,3},{8,12},{12,8},{9,1... | collective-permute-start | bytes 6291464 | tf_op jit(solution)/shard_map/ppermute | solution.py:39
  626.8 26.8 %collective-permute-start.25 = (bf16[1,256,1024]{2,1,0:T(8,128)(2,1)S(1)}, bf16[1,256,1024]{2,1,0:T(8,128)(2,1)S(1)}, u32[]{:S(2)}, u32[]{:S(2)}) collective-permute-start(bf16[1,256,1024]{2,1,0:T(8,128)(2,1)S(1)} %get-tuple-element.156.refs_0_), channel_id=1, source_target_pairs={{0,16},{8,24},{16,0},{24,8},{1,17},{9,25},{17,1},{25,9},{2,18},{10... | collective-permute-start | bytes 1572872 | tf_op jit(solution)/shard_map/ppermute | solution.py:39
  640.7 54.5 %collective-permute-start.21 = (bf16[2,512,1024]{2,1,0:T(8,128)(2,1)}, bf16[2,512,1024]{2,1,0:T(8,128)(2,1)}, u32[]{:S(2)}, u32[]{:S(2)}) collective-permute-start(bf16[2,512,1024]{2,1,0:T(8,128)(2,1)} %slab_grad.14.refs_1_), channel_id=1, source_target_pairs={{0,4},{4,0},{1,5},{5,1},{2,6},{6,2},{3,7},{7,3},{8,12},{12,8},{9,1... | collective-permute-start | bytes 6291464 | tf_op jit(solution)/shard_map/ppermute | solution.py:39
  658.1 36.3 %collective-permute-start.27 = (bf16[2,128,3072]{2,1,0:T(8,128)(2,1)S(1)}, bf16[2,128,3072]{2,1,0:T(8,128)(2,1)S(1)}, u32[]{:S(2)}, u32[]{:S(2)}) collective-permute-start(bf16[2,128,3072]{2,1,0:T(8,128)(2,1)S(1)} %get-tuple-element.161.refs_0_), channel_id=1, source_target_pairs={{0,8},{8,0},{16,24},{24,16},{1,9},{9,1},{17,25},{25,17},{2,10},{10... | collective-permute-start | bytes 4718600 | tf_op jit(solution)/shard_map/ppermute | solution.py:39
  664.3 30.5 %collective-permute-start.26 = (bf16[4,32,4096]{2,1,0:T(8,128)(2,1)S(1)}, bf16[4,32,4096]{2,1,0:T(8,128)(2,1)S(1)}, u32[]{:S(2)}, u32[]{:S(2)}) collective-permute-start(bf16[4,32,4096]{2,1,0:T(8,128)(2,1)S(1)} %get-tuple-element.164.refs_0_), channel_id=1, source_target_pairs={{0,2},{2,0},{1,3},{3,1},{4,6},{6,4},{5,7},{7,5},{8,10},{10,8},{9,1... | collective-permute-start | bytes 3145736 | tf_op jit(solution)/shard_map/ppermute | solution.py:39
  665.9 50.1 %collective-permute-start.31 = (bf16[4,128,1024]{2,1,0:T(8,128)(2,1)S(1)}, bf16[4,128,1024]{2,1,0:T(8,128)(2,1)S(1)}, u32[]{:S(2)}, u32[]{:S(2)}) collective-permute-start(bf16[4,128,1024]{2,1,0:T(8,128)(2,1)S(1)} %get-tuple-element.162.refs_0_), channel_id=1, source_target_pairs={{0,4},{4,0},{1,5},{5,1},{2,6},{6,2},{3,7},{7,3},{8,12},{12,8},{9,1... | collective-permute-start | bytes 3145736 | tf_op jit(solution)/shard_map/ppermute | solution.py:39
  698.5 34.7 %collective-permute-start.28 = (bf16[1,512,1024]{2,1,0:T(8,128)(2,1)S(1)}, bf16[1,512,1024]{2,1,0:T(8,128)(2,1)S(1)}, u32[]{:S(2)}, u32[]{:S(2)}) collective-permute-start(bf16[1,512,1024]{2,1,0:T(8,128)(2,1)S(1)} %get-tuple-element.169.refs_0_), channel_id=1, source_target_pairs={{0,2},{2,0},{1,3},{3,1},{4,6},{6,4},{5,7},{7,5},{8,10},{10,8},{9,1... | collective-permute-start | bytes 3145736 | tf_op jit(solution)/shard_map/ppermute | solution.py:39
  700.3 32.6 %collective-permute-start.29 = (bf16[2,64,3072]{2,1,0:T(8,128)(2,1)S(1)}, bf16[2,64,3072]{2,1,0:T(8,128)(2,1)S(1)}, u32[]{:S(2)}, u32[]{:S(2)}) collective-permute-start(bf16[2,64,3072]{2,1,0:T(8,128)(2,1)S(1)} %get-tuple-element.166.refs_0_), channel_id=1, source_target_pairs={{0,4},{4,0},{1,5},{5,1},{2,6},{6,2},{3,7},{7,3},{8,12},{12,8},{9,1... | collective-permute-start | bytes 2359304 | tf_op jit(solution)/shard_map/ppermute | solution.py:39
  735.7 29.3 %collective-permute-start.36 = (bf16[1,128,1024]{2,1,0:T(8,128)(2,1)S(1)}, bf16[1,128,1024]{2,1,0:T(8,128)(2,1)S(1)}, u32[]{:S(2)}, u32[]{:S(2)}) collective-permute-start(bf16[1,128,1024]{2,1,0:T(8,128)(2,1)S(1)} %get-tuple-element.177.refs_0_), channel_id=1, source_target_pairs={{0,16},{8,24},{16,0},{24,8},{1,17},{9,25},{17,1},{25,9},{2,18},{10... | collective-permute-start | bytes 786440 | tf_op jit(solution)/shard_map/ppermute | solution.py:39
  (88 other events, 1001.0 us)
Sparse Core Ops, SparseCore 0:
  12.3 147.2 all-gather.3
  163.1 93.8 all-gather.5
  260.4 119.2 all-gather.7

commit v5 on v4

--- a/solution.py
+++ b/solution.py
@@ -1632,12 +1632,12 @@
     f1i = slab_second(f1i, "x", order=(mid.send,))
     f1o = z_steps(f1o, rows, hidden, low_z, order=(f1i.send,))
     mid = z_steps(mid, few, 4 * width, high_z, order=(f1o.send,))
-    f1o = z_steps(f1o, rows, hidden, high_z, order=(mid.send,))
+    f1i = z_steps(f1i, rows, hidden, low_z, order=(mid.send,))
+    f1o = z_steps(f1o, rows, hidden, high_z, order=(f1i.send,))
     mid = mid.finish((few, 4 * width), order=(f1o.send,))
     out_att, out_cin, out_cout = mid[:, :width], mid[:, width : 3 * width], mid[:, 3 * width :]
     qkv = qkv.step((zs // 2, 2, few, 3 * width), "y", order=(mid,))
-    f1i = z_steps(f1i, rows, hidden, low_z, order=(qkv.send,))
-    f1i = z_steps(f1i, rows, hidden, high_z, order=(f1i.send,))
+    f1i = z_steps(f1i, rows, hidden, high_z, order=(qkv.send,))
     a, b, c, p = 0, 1, 2, 3
     places = [(a, 0), (p, 0), (b, 0), (c, 4), (c, 2), (c, 0)]
     places += [(a, 1), (p, 1), (b, 1), (c, 5), (c, 3), (c, 1)]

time: 794 us -> 791 us (level)
    ppermute x29, starting transfers between devices: 32.2 us -> 23.9 us  [xor_send(): return lax.ppermute(cells, axis, [(i, i ^ bit) for i in range(count)])]
  transfers between devices with their start and end apart: 52 -> 52, of which waited for: 18 -> 20; matrix products, arithmetic and copies ran while one was open for 4% -> 4% of each run, Pallas kernels for 26% -> 25%
where the time goes in v5:
time: 791 us; the launch traced here: 778 us
  waiting for transfers between devices  350 us (44%)
  Pallas kernels  249 us (31%)
  starting transfers between devices  96.3 us (12%)
  local copies, waits for them, and re-layouts  45.5 us (6%)
  between operations  15.1 us (2%)
  blocking collectives  14.5 us (2%)
  other arithmetic  8.59 us (1%)
    all_gather x3, waiting for transfers between devices, gather(): lax.all_gather(mine, DEV, axis=0, tiled=True).reshape(devices, -1, width)  179 us
    ppermute x29, waiting for transfers between devices, xor_send(): return lax.ppermute(cells, axis, [(i, i ^ bit) for i in range(count)])  87.4 us
    pallas_call x8, Pallas kernels, slab_grad(): pl.pallas_call(functools.partial(slab_grad_kernel, split, len(order), pai...  43.8 us
    all_to_all x4, waiting for transfers between devices, to_heads(): got = lax.all_to_all(cells, LAYER, split_axis=0, concat_axis=0, tiled=True)  32.3 us
    pallas_call x1, Pallas kernels, second_call(): pl.pallas_call(second_kernel, grid_spec=pltpu.PrefetchScalarGridSpec(num_...  31.1 us
    all_to_all x3, waiting for transfers between devices, to_frames(): return lax.all_to_all(cells, LAYER, split_axis=0, concat_axis=0, tiled=True)  26.7 us
    pallas_call x1, Pallas kernels, attn_bwd(): pl.pallas_call(kernel, grid_spec=grid_spec, out_shape=[jax.ShapeDtypeStru...  26.7 us
    unnamed x124, local copies, waits for them, and re-layouts  26.2 us
  transfers between devices with their start and end apart: 52, of which 20 were waited for; matrix products, arithmetic and copies ran while one was open for 4% of the time, Pallas kernels for 25%

profile of v5, /device:TPU:0, one launch (start us, length us, event | category | flops | bytes accessed | tf_op | source)
XLA Modules:
  0.0 778.5 jit_solution(5801693580708154953)
XLA Ops:
  13.3 14.5 %all_to_all.55 = bf16[32,2,288]{2,1,0:T(2,128)(2,1)S(1)} all-to-all(bf16[32,2,288]{2,1,0:T(2,128)(2,1)S(1)} %reshape.389), channel_id=1, replica_groups=mesh['z'=4,'x'=2,'y'=2,'c'=2] {'z','x','y','c'}, dimensions={0} | all-to-all | bytes 73728 | tf_op jit(solution)/shard_map/all_to_all | solution.py:1434
  33.0 126.6 %all-gather.4.cloned.1.call-done = bf16[11264,1024]{1,0:T(8,128)(2,1)} async-done(((bf16[352,1024]{1,0:T(8,128)(2,1)}), bf16[11264,1024]{1,0:T(8,128)(2,1)}) %all-gather.4.cloned.1.call-update) | async-done | bytes 23068688 | tf_op jit(solution)/shard_map/all_gather | solution.py:1443
  159.7 20.5 %first_part.1 = (f32[384,1024]{1,0:T(8,128)}, bf16[384,1024]{1,0:T(8,128)(2,1)}, bf16[3,384,1024]{2,1,0:T(8,128)(2,1)}, bf16[2,384,1024]{2,1,0:T(8,128)(2,1)}, b...) custom-call(s32[1]{0:T(128)} %bitcast.core_ref, ...), custom_call_target="tpu_custom_call" | custom-call | flops 8858370048 | bytes 38797312 | tf_op jit(solution)/shard_map/first_part/pallas_call | solution.py:237
  187.1 15.2 %all-to-all-done.3 = bf16[8,384,128]{2,1,0:T(8,128)(2,1)} async-done(((bf16[8,384,128]{2,1,0:T(8,128)(2,1)}), bf16[8,384,128]{2,1,0:T(8,128)(2,1)}, u32[]{:S(2)}, u32[]{:S(2)}) %all-to-all-start.3) | async-done | bytes 786464 | tf_op jit(solution)/shard_map/all_to_all | solution.py:1514
  212.4 8.4 %all-to-all-done.2 = bf16[8,384,128]{2,1,0:T(8,128)(2,1)} async-done(((bf16[8,384,128]{2,1,0:T(8,128)(2,1)}), bf16[8,384,128]{2,1,0:T(8,128)(2,1)}, u32[]{:S(2)}, u32[]{:S(2)}) %all-to-all-start.2) | async-done | bytes 786464 | tf_op jit(solution)/shard_map/all_to_all | solution.py:1514
  232.9 8.7 %all-to-all-done.1 = bf16[8,384,128]{2,1,0:T(8,128)(2,1)} async-done(((bf16[8,384,128]{2,1,0:T(8,128)(2,1)}), bf16[8,384,128]{2,1,0:T(8,128)(2,1)}, u32[]{:S(2)}, u32[]{:S(2)}) %all-to-all-start.1) | async-done | bytes 786464 | tf_op jit(solution)/shard_map/all_to_all | solution.py:1514
  243.7 11.8 %collective-permute-done.1.refs_6_.refs_11_ = bf16[1536,128]{1,0:T(8,128)(2,1)} collective-permute-done((bf16[1536,128]{1,0:T(8,128)(2,1)}, bf16[1536,128]{1,0:T(8,128)(2,1)}, u32[]{:S(2)}, u32[]{:S(2)}) %collective-permute-start.1) | collective-permute-done | bytes 393248 | tf_op jit(solution)/shard_map/ppermute | solution.py:1525
  255.5 19.6 %attention_forward.1 = (bf16[3072,128]{1,0:T(8,128)(2,1)}, f32[1,3072]{1,0:T(1,128)}) custom-call(s32[6]{0:T(128)} %fusion.8.refs_0_, s32[6]{0:T(128)} %slice.223.refs_1_, f32[1]{0:T(128)} %bitcast.1.refs_2_, bf16[3072,128]{1,0:T(8,128)(2,1)} %bitcast.6.refs_3_, bf16[1536,128]{1,0:T(8,128)(2,1)} %collective-permute-done.refs_4_.refs_9_, ...), custom_call_target="tpu_custom_call" | custom-call | flops 1610612736 | bytes 3407872 | tf_op jit(solution)/shard_map/attention_forward/pallas_call | solution.py:890
  281.7 10.7 %all-to-all-done.4.mh_ref = bf16[8,384,128]{2,1,0:T(8,128)(2,1)} async-done(((bf16[8,384,128]{2,1,0:T(8,128)(2,1)}), bf16[8,384,128]{2,1,0:T(8,128)(2,1)}, u32[]{:S(2)}, u32[]{:S(2)}) %all-to-all-start.4) | async-done | bytes 786464 | tf_op jit(solution)/shard_map/all_to_all | solution.py:1519
  293.7 9.3 %attention_out_and_gate.1 = (bf16[384,1024]{1,0:T(8,128)(2,1)}, f32[384,1024]{1,0:T(8,128)}, bf16[384,1024]{1,0:T(8,128)(2,1)}, f32[384,1024]{1,0:T(8,128)}, f32...) custom-call(bf16[8,384,128]{2,1,0:T(8,128)(2,1)} %all-to-all-done.4.mh_ref, f32[384,1024]{1,0:T(8,128)} %get-tuple-element.109.x1_ref, ...), custom_call_target="tpu_custom_call" | custom-call | flops 2415919104 | bytes 15728640 | tf_op jit(solution)/shard_map/attention_out_and_gate/pallas_call | solution.py:303
  314.8 8.7 %all-to-all-start.5 = ((f32[32,2,1024]{2,1,0:T(2,128)}), f32[32,2,1024]{2,1,0:T(2,128)S(1)}, u32[]{:S(2)}, u32[]{:S(2)}) async-start(f32[32,2,1024]{2,1,0:T(2,128)} %get-tuple-element.114), calls=%async_computation.5 | async-start | bytes 524288 | tf_op jit(solution)/shard_map/all_to_all | solution.py:1536
  326.0 52.5 %all-gather.8.cloned.1.call-done = bf16[8192,1024]{1,0:T(8,128)(2,1)} async-done(((bf16[256,1024]{1,0:T(8,128)(2,1)}), bf16[8192,1024]{1,0:T(8,128)(2,1)}) %all-gather.8.cloned.1.call-update) | async-done | bytes 16777232 | tf_op jit(solution)/shard_map/all_gather | solution.py:1443
  379.1 31.1 %second_part.1 = (bf16[384,1024]{1,0:T(8,128)(2,1)}, bf16[384,1024]{1,0:T(8,128)(2,1)}, f32[384,1024]{1,0:T(8,128)}, bf16[384,1024]{1,0:T(8,128)(2,1)}, f32[384,...) custom-call(s32[1]{0:T(128)} %bitcast.core_ref, ...), custom_call_target="tpu_custom_call" | custom-call | flops 14495514624 | bytes 51380224 | tf_op jit(solution)/shard_map/second_part/pallas_call | solution.py:471
  432.2 15.3 %convolution_backward.1 = (bf16[384,2048]{1,0:T(8,128)(2,1)}, f32[384,1024]{1,0:T(8,128)}, bf16[384,1024]{1,0:T(8,128)(2,1)}, bf16[8,384,128]{2,1,0:T(8,128)(2,1)}, f32[8,1024]{1,0:T(8,128)}) custom-call(f32[384,1024]{1,0:T(8,128)} %get-tuple-element.116.dz_ref, f32[384,1024]{1,0:T(8,128)} %get-tuple-element.113.conv_ref, f32[4,1024]{1,0:T(4,128)} %copy-done.43, ...), custom_call_target="tpu_custom_call" | custom-call | flops 2415919104 | bytes 19660800 | tf_op jit(solution)/shard_map/convolution_backward/pallas_call | solution.py:617
  457.5 9.3 %row_grad.2 = (bf16[512,4096]{1,0:T(8,128)(2,1)}, bf16[512,4096]{1,0:T(8,128)(2,1)}) custom-call(s32[1]{0:T(128)} %bitcast.core_ref, bf16[384,1024]{1,0:T(8,128)(2,1)} %get-tuple-element.126.refs_0_, bf16[384,1024]{1,0:T(8,128)(2,1)} %get-tuple-element.127.refs_1_, bf16[384,1024]{1,0:T(8,128)(2,1)} %get-tuple-element.128.refs_2_, ...), custom_call_target="tpu_custom_call" | custom-call | flops 1024 | bytes 37001024 | tf_op jit(solution)/shard_map/row_grad/pallas_call | solution.py:1394
  478.5 26.7 %attention_backward.1 = (bf16[3072,128]{1,0:T(8,128)(2,1)}, bf16[1536,256]{1,0:T(8,128)(2,1)}, f32[3072,256]{1,0:T(8,128)}, bf16[1536,256]{1,0:T(8,128)(2,1)}) custom-call(s32[6]{0:T(128)} %fusion.8.refs_0_, s32[6]{0:T(128)} %slice.223.refs_1_, f32[1]{0:T(128)} %bitcast.1.refs_2_, bf16[3072,128]{1,0:T(8,128)(2,1)} %bitcast.6.refs_3_, ...), custom_call_target="tpu_custom_call" | custom-call | flops 32212254720 | bytes 6815744 | tf_op jit(solution)/shard_map/attention_backward/pallas_call | solution.py:1007
  505.2 8.3 %collective-permute-start.10 = (bf16[1536,256]{1,0:T(8,128)(2,1)}, bf16[1536,256]{1,0:T(8,128)(2,1)S(1)}, u32[]{:S(2)}, u32[]{:S(2)}) collective-permute-start(bf16[1536,256]{1,0:T(8,128)(2,1)} %get-tuple-element.135), channel_id=1, source_target_pairs={{0,8},{8,16},{16,24},{1,9},{9,17},{17,25},{2,10},{10,18},{18,26},{... | collective-permute-start | bytes 2359304 | tf_op jit(solution)/shard_map/ppermute | solution.py:1596
  546.2 16.1 %all-to-all-done.9.dkv_ref.refs_3_ = bf16[8,384,256]{2,1,0:T(8,128)(2,1)S(1)} async-done(((bf16[8,384,256]{2,1,0:T(8,128)(2,1)}), bf16[8,384,256]{2,1,0:T(8,128)(2,1)S(1)}, u32[]{:S(2)}, u32[]{:S(2)}) %all-to-all-start.9) | async-done | bytes 1572896 | tf_op jit(solution)/shard_map/all_to_all | solution.py:1519
  563.4 9.0 %projections_backward.1 = (f32[384,1024]{1,0:T(8,128)}, bf16[1,384,1024]{2,1,0:T(8,128)(2,1)}, f32[8,1024]{1,0:T(8,128)}) custom-call(bf16[8,384,128]{2,1,0:T(8,128)(2,1)} %all-to-all-done.8.dq_ref.refs_1_, bf16[8,384,256]{2,1,0:T(8,128)(2,1)} %copy-done.27, f32[384,1024]{1,0:T(8,128)} %get-tuple-element.139.dx2_ref, f32[384,1024]{1,0:T(8,128)} %get-tuple-element.109.x1_ref, ...), custom_call_target="tpu_custom_call" | custom-call | flops 1024 | bytes 33301024 | tf_op jit(solution)/shard_map/projections_backward/pallas_call | solution.py:718
  597.0 14.5 %last_part.1 = (bf16[384,1024]{1,0:T(8,128)(2,1)}, f32[8,1024]{1,0:T(8,128)}, bf16[1,384,1024]{2,1,0:T(8,128)(2,1)}, bf16[1,384,1024]{2,1,0:T(8,128)(2,1)}, bf16[2,384,1024]{2,1,0:T(8,128)(2,1)}) custom-call(s32[1]{0:T(128)} %bitcast.core_ref, f32[384,1024]{1,0:T(8,128)} %get-tuple-element.140.dx1_ref, ...), custom_call_target="tpu_custom_call" | custom-call | flops 1024 | bytes 55501024 | tf_op jit(solution)/shard_map/last_part/pallas_call | solution.py:771
  664.0 28.2 %collective-permute-done.27 = bf16[2,128,3072]{2,1,0:T(8,128)(2,1)S(1)} collective-permute-done((bf16[2,128,3072]{2,1,0:T(8,128)(2,1)S(1)}, bf16[2,128,3072]{2,1,0:T(8,128)(2,1)S(1)}, u32[]{:S(2)}, u32[]{:S(2)}) %collective-permute-start.27) | collective-permute-done | bytes 1572896 | tf_op jit(solution)/shard_map/ppermute | solution.py:39
  698.6 14.0 %collective-permute-done.30 = bf16[4,128,1024]{2,1,0:T(8,128)(2,1)S(1)} collective-permute-done((bf16[4,128,1024]{2,1,0:T(8,128)(2,1)S(1)}, bf16[4,128,1024]{2,1,0:T(8,128)(2,1)S(1)}, u32[]{:S(2)}, u32[]{:S(2)}) %collective-permute-start.30) | collective-permute-done | bytes 1048608 | tf_op jit(solution)/shard_map/ppermute | solution.py:39
  721.6 13.2 %collective-permute-done.34 = bf16[2,128,1024]{2,1,0:T(8,128)(2,1)S(1)} collective-permute-done((bf16[2,128,1024]{2,1,0:T(8,128)(2,1)S(1)}, bf16[2,128,1024]{2,1,0:T(8,128)(2,1)S(1)}, u32[]{:S(2)}, u32[]{:S(2)}) %collective-permute-start.34) | collective-permute-done | bytes 524320 | tf_op jit(solution)/shard_map/ppermute | solution.py:39
  736.9 8.6 %collective-permute-done.31 = bf16[2,128,1024]{2,1,0:T(8,128)(2,1)S(1)} collective-permute-done((bf16[2,128,1024]{2,1,0:T(8,128)(2,1)S(1)}, bf16[2,128,1024]{2,1,0:T(8,128)(2,1)S(1)}, u32[]{:S(2)}, u32[]{:S(2)}) %collective-permute-start.31) | collective-permute-done | bytes 524320 | tf_op jit(solution)/shard_map/ppermute | solution.py:39
  (334 shorter events, 262.7 us)
Async XLA Ops:
  7.2 152.4 %all-gather.4.cloned.1.call-start = ((), (), s32[]{:S(2)}) async-start(), calls=%async_computation.11 | async-start | bytes 23789568 | tf_op jit(solution)/shard_map/all_gather | solution.py:1443
  12.2 269.5 %all-gather.6.cloned.1.call-start = ((), (), s32[]{:S(2)}) async-start(), calls=%async_computation.12 | async-start | bytes 8650752 | tf_op jit(solution)/shard_map/all_gather | solution.py:1443
  13.0 365.4 %all-gather.8.cloned.1.call-start = ((), (), s32[]{:S(2)}) async-start(), calls=%async_computation.13 | async-start | bytes 17301504 | tf_op jit(solution)/shard_map/all_gather | solution.py:1443
  184.8 107.6 %collective-permute-start.4 = (bf16[3,384,1024]{2,1,0:T(8,128)(2,1)}, bf16[3,384,1024]{2,1,0:T(8,128)(2,1)S(1)}, u32[]{:S(2)}, u32[]{:S(2)}) collective-permute-start(bf16[3,384,1024]{2,1,0:T(8,128)(2,1)} %get-tuple-element.110.la_ref), channel_id=1, source_target_pairs={{0,1},{1,0},{2,3},{3,2},{4,5},{5,4},{6,7},{7,6},{8,9},{9,8},{10,11... | collective-permute-start | bytes 7077896 | tf_op jit(solution)/shard_map/ppermute | solution.py:39
  209.0 32.6 %collective-permute-start.2 = (bf16[1536,128]{1,0:T(8,128)(2,1)S(1)}, bf16[1536,128]{1,0:T(8,128)(2,1)}, u32[]{:S(2)}, u32[]{:S(2)}) collective-permute-start(bf16[1536,128]{1,0:T(8,128)(2,1)S(1)} %bitcast.163), channel_id=1, source_target_pairs={{0,8},{8,16},{16,24},{1,9},{9,17},{17,25},{2,10},{10,18},{18,26},{... | collective-permute-start | bytes 1179656 | tf_op jit(solution)/shard_map/ppermute | solution.py:1525
  211.1 30.5 %collective-permute-start.3 = (bf16[1536,128]{1,0:T(8,128)(2,1)S(1)}, bf16[1536,128]{1,0:T(8,128)(2,1)}, u32[]{:S(2)}, u32[]{:S(2)}) collective-permute-start(bf16[1536,128]{1,0:T(8,128)(2,1)S(1)} %bitcast.162), channel_id=1, source_target_pairs={{8,0},{16,8},{24,16},{9,1},{17,9},{25,17},{10,2},{18,10},{26,18},{... | collective-permute-start | bytes 1179656 | tf_op jit(solution)/shard_map/ppermute | solution.py:1525
  229.1 26.4 %collective-permute-start.1 = (bf16[1536,128]{1,0:T(8,128)(2,1)}, bf16[1536,128]{1,0:T(8,128)(2,1)}, u32[]{:S(2)}, u32[]{:S(2)}) collective-permute-start(bf16[1536,128]{1,0:T(8,128)(2,1)} %bitcast.9), channel_id=1, source_target_pairs={{8,0},{16,8},{24,16},{9,1},{17,9},{25,17},{10,2},{18,10},{26,18},{... | collective-permute-start | bytes 1179656 | tf_op jit(solution)/shard_map/ppermute | solution.py:1525
  314.8 63.7 %all-to-all-start.5 = ((f32[32,2,1024]{2,1,0:T(2,128)}), f32[32,2,1024]{2,1,0:T(2,128)S(1)}, u32[]{:S(2)}, u32[]{:S(2)}) async-start(f32[32,2,1024]{2,1,0:T(2,128)} %get-tuple-element.114), calls=%async_computation.5 | async-start | bytes 524288 | tf_op jit(solution)/shard_map/all_to_all | solution.py:1536
  447.5 30.1 %all-to-all-start.7 = ((bf16[8,384,128]{2,1,0:T(8,128)(2,1)}), bf16[8,384,128]{2,1,0:T(8,128)(2,1)S(1)}, u32[]{:S(2)}, u32[]{:S(2)}) async-start(bf16[8,384,128]{2,1,0:T(8,128)(2,1)} %get-tuple-element.124), calls=%async_computation.7 | async-start | bytes 1572864 | tf_op jit(solution)/shard_map/all_to_all | solution.py:1514
  454.0 65.1 %collective-permute-start.12 = (bf16[2,512,1024]{2,1,0:T(8,128)(2,1)}, bf16[2,512,1024]{2,1,0:T(8,128)(2,1)}, u32[]{:S(2)}, u32[]{:S(2)}) collective-permute-start(bf16[2,512,1024]{2,1,0:T(8,128)(2,1)} %slab_grad.8.refs_0_), channel_id=1, source_target_pairs={{0,4},{4,0},{1,5},{5,1},{2,6},{6,2},{3,7},{7,3},{8,12},{12,8},{9,1... | collective-permute-start | bytes 6291464 | tf_op jit(solution)/shard_map/ppermute | solution.py:39
  456.2 65.8 %collective-permute-start.13 = (bf16[2,512,1024]{2,1,0:T(8,128)(2,1)}, bf16[2,512,1024]{2,1,0:T(8,128)(2,1)}, u32[]{:S(2)}, u32[]{:S(2)}) collective-permute-start(bf16[2,512,1024]{2,1,0:T(8,128)(2,1)} %slab_grad.9.refs_1_.refs_0_), channel_id=1, source_target_pairs={{0,2},{2,0},{1,3},{3,1},{4,6},{6,4},{5,7},{7,5},{8,10},{10,8},{9,1... | collective-permute-start | bytes 6291464 | tf_op jit(solution)/shard_map/ppermute | solution.py:39
  466.9 119.1 %collective-permute-start.16 = (bf16[512,4096]{1,0:T(8,128)(2,1)}, bf16[512,4096]{1,0:T(8,128)(2,1)}, u32[]{:S(2)}, u32[]{:S(2)}) collective-permute-start(bf16[512,4096]{1,0:T(8,128)(2,1)} %get-tuple-element.145), channel_id=1, source_target_pairs={{0,1},{1,0},{2,3},{3,2},{4,5},{5,4},{6,7},{7,6},{8,9},{9,8},{10,11... | collective-permute-start | bytes 12582920 | tf_op jit(solution)/shard_map/ppermute | solution.py:39
  505.2 26.0 %collective-permute-start.10 = (bf16[1536,256]{1,0:T(8,128)(2,1)}, bf16[1536,256]{1,0:T(8,128)(2,1)S(1)}, u32[]{:S(2)}, u32[]{:S(2)}) collective-permute-start(bf16[1536,256]{1,0:T(8,128)(2,1)} %get-tuple-element.135), channel_id=1, source_target_pairs={{0,8},{8,16},{16,24},{1,9},{9,17},{17,25},{2,10},{10,18},{18,26},{... | collective-permute-start | bytes 2359304 | tf_op jit(solution)/shard_map/ppermute | solution.py:1596
  541.8 49.9 %collective-permute-start.14 = (bf16[1,512,1024]{2,1,0:T(8,128)(2,1)}, bf16[1,512,1024]{2,1,0:T(8,128)(2,1)}, u32[]{:S(2)}, u32[]{:S(2)}) collective-permute-start(bf16[1,512,1024]{2,1,0:T(8,128)(2,1)} %get-tuple-element.137.refs_0_), channel_id=1, source_target_pairs={{0,2},{2,0},{1,3},{3,1},{4,6},{6,4},{5,7},{7,5},{8,10},{10,8},{9,1... | collective-permute-start | bytes 3145736 | tf_op jit(solution)/shard_map/ppermute | solution.py:39
  543.9 47.9 %collective-permute-start.15 = (bf16[4,128,1024]{2,1,0:T(8,128)(2,1)}, bf16[4,128,1024]{2,1,0:T(8,128)(2,1)}, u32[]{:S(2)}, u32[]{:S(2)}) collective-permute-start(bf16[4,128,1024]{2,1,0:T(8,128)(2,1)} %get-tuple-element.138.refs_1_), channel_id=1, source_target_pairs={{0,4},{4,0},{1,5},{5,1},{2,6},{6,2},{3,7},{7,3},{8,12},{12,8},{9,1... | collective-permute-start | bytes 3145736 | tf_op jit(solution)/shard_map/ppermute | solution.py:39
  580.1 73.8 %collective-permute-start.24 = (bf16[512,3072]{1,0:T(8,128)(2,1)}, bf16[512,3072]{1,0:T(8,128)(2,1)S(1)}, u32[]{:S(2)}, u32[]{:S(2)}) collective-permute-start(bf16[512,3072]{1,0:T(8,128)(2,1)} %get-tuple-element.148.refs_0_), channel_id=1, source_target_pairs={{0,1},{1,0},{2,3},{3,2},{4,5},{5,4},{6,7},{7,6},{8,9},{9,8},{10,11... | collective-permute-start | bytes 9437192 | tf_op jit(solution)/shard_map/ppermute | solution.py:39
  594.9 60.8 %collective-permute-start.23 = (bf16[2,512,1024]{2,1,0:T(8,128)(2,1)}, bf16[2,512,1024]{2,1,0:T(8,128)(2,1)}, u32[]{:S(2)}, u32[]{:S(2)}) collective-permute-start(bf16[2,512,1024]{2,1,0:T(8,128)(2,1)} %slab_grad.12.refs_0_), channel_id=1, source_target_pairs={{0,2},{2,0},{1,3},{3,1},{4,6},{6,4},{5,7},{7,5},{8,10},{10,8},{9,1... | collective-permute-start | bytes 6291464 | tf_op jit(solution)/shard_map/ppermute | solution.py:39
  596.4 62.9 %collective-permute-start.22 = (bf16[4,64,4096]{2,1,0:T(8,128)(2,1)}, bf16[4,64,4096]{2,1,0:T(8,128)(2,1)}, u32[]{:S(2)}, u32[]{:S(2)}) collective-permute-start(bf16[4,64,4096]{2,1,0:T(8,128)(2,1)} %get-tuple-element.149.refs_8_), channel_id=1, source_target_pairs={{0,4},{4,0},{1,5},{5,1},{2,6},{6,2},{3,7},{7,3},{8,12},{12,8},{9,1... | collective-permute-start | bytes 6291464 | tf_op jit(solution)/shard_map/ppermute | solution.py:39
  624.8 26.3 %collective-permute-start.25 = (bf16[1,256,1024]{2,1,0:T(8,128)(2,1)S(1)}, bf16[1,256,1024]{2,1,0:T(8,128)(2,1)S(1)}, u32[]{:S(2)}, u32[]{:S(2)}) collective-permute-start(bf16[1,256,1024]{2,1,0:T(8,128)(2,1)S(1)} %get-tuple-element.156.refs_0_), channel_id=1, source_target_pairs={{0,16},{8,24},{16,0},{24,8},{1,17},{9,25},{17,1},{25,9},{2,18},{10... | collective-permute-start | bytes 1572872 | tf_op jit(solution)/shard_map/ppermute | solution.py:39
  636.5 56.3 %collective-permute-start.21 = (bf16[2,512,1024]{2,1,0:T(8,128)(2,1)}, bf16[2,512,1024]{2,1,0:T(8,128)(2,1)}, u32[]{:S(2)}, u32[]{:S(2)}) collective-permute-start(bf16[2,512,1024]{2,1,0:T(8,128)(2,1)} %slab_grad.14.refs_1_), channel_id=1, source_target_pairs={{0,4},{4,0},{1,5},{5,1},{2,6},{6,2},{3,7},{7,3},{8,12},{12,8},{9,1... | collective-permute-start | bytes 6291464 | tf_op jit(solution)/shard_map/ppermute | solution.py:39
  655.7 36.4 %collective-permute-start.27 = (bf16[2,128,3072]{2,1,0:T(8,128)(2,1)S(1)}, bf16[2,128,3072]{2,1,0:T(8,128)(2,1)S(1)}, u32[]{:S(2)}, u32[]{:S(2)}) collective-permute-start(bf16[2,128,3072]{2,1,0:T(8,128)(2,1)S(1)} %get-tuple-element.161.refs_0_), channel_id=1, source_target_pairs={{0,8},{8,0},{16,24},{24,16},{1,9},{9,1},{17,25},{25,17},{2,10},{10... | collective-permute-start | bytes 4718600 | tf_op jit(solution)/shard_map/ppermute | solution.py:39
  661.9 30.6 %collective-permute-start.26 = (bf16[4,32,4096]{2,1,0:T(8,128)(2,1)S(1)}, bf16[4,32,4096]{2,1,0:T(8,128)(2,1)S(1)}, u32[]{:S(2)}, u32[]{:S(2)}) collective-permute-start(bf16[4,32,4096]{2,1,0:T(8,128)(2,1)S(1)} %get-tuple-element.164.refs_0_), channel_id=1, source_target_pairs={{0,2},{2,0},{1,3},{3,1},{4,6},{6,4},{5,7},{7,5},{8,10},{10,8},{9,1... | collective-permute-start | bytes 3145736 | tf_op jit(solution)/shard_map/ppermute | solution.py:39
  663.4 49.2 %collective-permute-start.30 = (bf16[4,128,1024]{2,1,0:T(8,128)(2,1)S(1)}, bf16[4,128,1024]{2,1,0:T(8,128)(2,1)S(1)}, u32[]{:S(2)}, u32[]{:S(2)}) collective-permute-start(bf16[4,128,1024]{2,1,0:T(8,128)(2,1)S(1)} %get-tuple-element.162.refs_0_), channel_id=1, source_target_pairs={{0,4},{4,0},{1,5},{5,1},{2,6},{6,2},{3,7},{7,3},{8,12},{12,8},{9,1... | collective-permute-start | bytes 3145736 | tf_op jit(solution)/shard_map/ppermute | solution.py:39
  698.1 37.0 %collective-permute-start.32 = (bf16[2,64,3072]{2,1,0:T(8,128)(2,1)S(1)}, bf16[2,64,3072]{2,1,0:T(8,128)(2,1)S(1)}, u32[]{:S(2)}, u32[]{:S(2)}) collective-permute-start(bf16[2,64,3072]{2,1,0:T(8,128)(2,1)S(1)} %get-tuple-element.166.refs_0_), channel_id=1, source_target_pairs={{0,4},{4,0},{1,5},{5,1},{2,6},{6,2},{3,7},{7,3},{8,12},{12,8},{9,1... | collective-permute-start | bytes 2359304 | tf_op jit(solution)/shard_map/ppermute | solution.py:39
  (88 other events, 1003.9 us)
Sparse Core Ops, SparseCore 0:
  12.3 147.2 all-gather.3
  163.1 93.8 all-gather.5
  260.4 117.9 all-gather.7

commit v6 on v5

--- a/solution.py
+++ b/solution.py
@@ -18,7 +18,7 @@
 DEV = ("z", "x", "y", "c")
 LAYER = ("x", "y", "c")
 BQ = 512
-BK = 512
+BK = 1024
 BF = jnp.bfloat16
 F32 = jnp.float32
 VMEM_BYTES = 56 * 1024 * 1024

time: 791 us -> 794 us (level)
  transfers between devices with their start and end apart: 52 -> 52, of which waited for: 20 -> 19; matrix products, arithmetic and copies ran while one was open for 4% -> 4% of each run, Pallas kernels for 25% -> 26%
where the time goes in v6:
time: 794 us; the launch traced here: 783 us
  waiting for transfers between devices  350 us (44%)
  Pallas kernels  252 us (32%)
  starting transfers between devices  97.3 us (12%)
  local copies, waits for them, and re-layouts  45.5 us (6%)
  between operations  15.3 us (2%)
  blocking collectives  14.5 us (2%)
  other arithmetic  8.59 us (1%)
    all_gather x3, waiting for transfers between devices, gather(): lax.all_gather(mine, DEV, axis=0, tiled=True).reshape(devices, -1, width)  177 us
    ppermute x29, waiting for transfers between devices, xor_send(): return lax.ppermute(cells, axis, [(i, i ^ bit) for i in range(count)])  84.5 us
    pallas_call x8, Pallas kernels, slab_grad(): pl.pallas_call(functools.partial(slab_grad_kernel, split, len(order), pai...  43.8 us
    all_to_all x4, waiting for transfers between devices, to_heads(): got = lax.all_to_all(cells, LAYER, split_axis=0, concat_axis=0, tiled=True)  32.4 us
    pallas_call x1, Pallas kernels, second_call(): pl.pallas_call(second_kernel, grid_spec=pltpu.PrefetchScalarGridSpec(num_...  31.1 us
    pallas_call x1, Pallas kernels, attn_bwd(): pl.pallas_call(kernel, grid_spec=grid_spec, out_shape=[jax.ShapeDtypeStru...  28.5 us
    all_to_all x3, waiting for transfers between devices, to_frames(): return lax.all_to_all(cells, LAYER, split_axis=0, concat_axis=0, tiled=True)  28.2 us
    unnamed x124, local copies, waits for them, and re-layouts  26.3 us
  transfers between devices with their start and end apart: 52, of which 19 were waited for; matrix products, arithmetic and copies ran while one was open for 4% of the time, Pallas kernels for 26%

profile of v6, /device:TPU:0, one launch (start us, length us, event | category | flops | bytes accessed | tf_op | source)
XLA Modules:
  0.0 783.4 jit_solution(6434215073119568676)
XLA Ops:
  13.3 14.5 %all_to_all.55 = bf16[32,2,288]{2,1,0:T(2,128)(2,1)S(1)} all-to-all(bf16[32,2,288]{2,1,0:T(2,128)(2,1)S(1)} %reshape.389), channel_id=1, replica_groups=mesh['z'=4,'x'=2,'y'=2,'c'=2] {'z','x','y','c'}, dimensions={0} | all-to-all | bytes 73728 | tf_op jit(solution)/shard_map/all_to_all | solution.py:1434
  33.0 126.6 %all-gather.4.cloned.1.call-done = bf16[11264,1024]{1,0:T(8,128)(2,1)} async-done(((bf16[352,1024]{1,0:T(8,128)(2,1)}), bf16[11264,1024]{1,0:T(8,128)(2,1)}) %all-gather.4.cloned.1.call-update) | async-done | bytes 23068688 | tf_op jit(solution)/shard_map/all_gather | solution.py:1443
  159.7 20.5 %first_part.1 = (f32[384,1024]{1,0:T(8,128)}, bf16[384,1024]{1,0:T(8,128)(2,1)}, bf16[3,384,1024]{2,1,0:T(8,128)(2,1)}, bf16[2,384,1024]{2,1,0:T(8,128)(2,1)}, b...) custom-call(s32[1]{0:T(128)} %bitcast.core_ref, ...), custom_call_target="tpu_custom_call" | custom-call | flops 8858370048 | bytes 38797312 | tf_op jit(solution)/shard_map/first_part/pallas_call | solution.py:237
  187.1 15.3 %all-to-all-done.3 = bf16[8,384,128]{2,1,0:T(8,128)(2,1)} async-done(((bf16[8,384,128]{2,1,0:T(8,128)(2,1)}), bf16[8,384,128]{2,1,0:T(8,128)(2,1)}, u32[]{:S(2)}, u32[]{:S(2)}) %all-to-all-start.3) | async-done | bytes 786464 | tf_op jit(solution)/shard_map/all_to_all | solution.py:1514
  212.4 8.4 %all-to-all-done.2 = bf16[8,384,128]{2,1,0:T(8,128)(2,1)} async-done(((bf16[8,384,128]{2,1,0:T(8,128)(2,1)}), bf16[8,384,128]{2,1,0:T(8,128)(2,1)}, u32[]{:S(2)}, u32[]{:S(2)}) %all-to-all-start.2) | async-done | bytes 786464 | tf_op jit(solution)/shard_map/all_to_all | solution.py:1514
  232.9 8.7 %all-to-all-done.1 = bf16[8,384,128]{2,1,0:T(8,128)(2,1)} async-done(((bf16[8,384,128]{2,1,0:T(8,128)(2,1)}), bf16[8,384,128]{2,1,0:T(8,128)(2,1)}, u32[]{:S(2)}, u32[]{:S(2)}) %all-to-all-start.1) | async-done | bytes 786464 | tf_op jit(solution)/shard_map/all_to_all | solution.py:1514
  243.7 11.8 %collective-permute-done.1.refs_6_.refs_11_ = bf16[1536,128]{1,0:T(8,128)(2,1)} collective-permute-done((bf16[1536,128]{1,0:T(8,128)(2,1)}, bf16[1536,128]{1,0:T(8,128)(2,1)}, u32[]{:S(2)}, u32[]{:S(2)}) %collective-permute-start.1) | collective-permute-done | bytes 393248 | tf_op jit(solution)/shard_map/ppermute | solution.py:1525
  255.5 21.1 %attention_forward.1 = (bf16[3072,128]{1,0:T(8,128)(2,1)}, f32[1,3072]{1,0:T(1,128)}) custom-call(s32[6]{0:T(128)} %fusion.8.refs_0_, s32[6]{0:T(128)} %slice.223.refs_1_, f32[1]{0:T(128)} %bitcast.1.refs_2_, bf16[3072,128]{1,0:T(8,128)(2,1)} %bitcast.6.refs_3_, bf16[1536,128]{1,0:T(8,128)(2,1)} %collective-permute-done.refs_4_.refs_9_, ...), custom_call_target="tpu_custom_call" | custom-call | flops 1610612736 | bytes 3670016 | tf_op jit(solution)/shard_map/attention_forward/pallas_call | solution.py:890
  283.2 12.1 %all-to-all-done.4.mh_ref = bf16[8,384,128]{2,1,0:T(8,128)(2,1)} async-done(((bf16[8,384,128]{2,1,0:T(8,128)(2,1)}), bf16[8,384,128]{2,1,0:T(8,128)(2,1)}, u32[]{:S(2)}, u32[]{:S(2)}) %all-to-all-start.4) | async-done | bytes 786464 | tf_op jit(solution)/shard_map/all_to_all | solution.py:1519
  296.7 9.3 %attention_out_and_gate.1 = (bf16[384,1024]{1,0:T(8,128)(2,1)}, f32[384,1024]{1,0:T(8,128)}, bf16[384,1024]{1,0:T(8,128)(2,1)}, f32[384,1024]{1,0:T(8,128)}, f32...) custom-call(bf16[8,384,128]{2,1,0:T(8,128)(2,1)} %all-to-all-done.4.mh_ref, f32[384,1024]{1,0:T(8,128)} %get-tuple-element.109.x1_ref, ...), custom_call_target="tpu_custom_call" | custom-call | flops 2415919104 | bytes 15728640 | tf_op jit(solution)/shard_map/attention_out_and_gate/pallas_call | solution.py:303
  317.8 9.3 %all-to-all-start.5 = ((f32[32,2,1024]{2,1,0:T(2,128)}), f32[32,2,1024]{2,1,0:T(2,128)S(1)}, u32[]{:S(2)}, u32[]{:S(2)}) async-start(f32[32,2,1024]{2,1,0:T(2,128)} %get-tuple-element.114), calls=%async_computation.5 | async-start | bytes 524288 | tf_op jit(solution)/shard_map/all_to_all | solution.py:1536
  329.6 50.5 %all-gather.8.cloned.1.call-done = bf16[8192,1024]{1,0:T(8,128)(2,1)} async-done(((bf16[256,1024]{1,0:T(8,128)(2,1)}), bf16[8192,1024]{1,0:T(8,128)(2,1)}) %all-gather.8.cloned.1.call-update) | async-done | bytes 16777232 | tf_op jit(solution)/shard_map/all_gather | solution.py:1443
  380.8 31.1 %second_part.1 = (bf16[384,1024]{1,0:T(8,128)(2,1)}, bf16[384,1024]{1,0:T(8,128)(2,1)}, f32[384,1024]{1,0:T(8,128)}, bf16[384,1024]{1,0:T(8,128)(2,1)}, f32[384,...) custom-call(s32[1]{0:T(128)} %bitcast.core_ref, ...), custom_call_target="tpu_custom_call" | custom-call | flops 14495514624 | bytes 51380224 | tf_op jit(solution)/shard_map/second_part/pallas_call | solution.py:471
  434.1 15.3 %convolution_backward.1 = (bf16[384,2048]{1,0:T(8,128)(2,1)}, f32[384,1024]{1,0:T(8,128)}, bf16[384,1024]{1,0:T(8,128)(2,1)}, bf16[8,384,128]{2,1,0:T(8,128)(2,1)}, f32[8,1024]{1,0:T(8,128)}) custom-call(f32[384,1024]{1,0:T(8,128)} %get-tuple-element.116.dz_ref, f32[384,1024]{1,0:T(8,128)} %get-tuple-element.113.conv_ref, f32[4,1024]{1,0:T(4,128)} %copy-done.43, ...), custom_call_target="tpu_custom_call" | custom-call | flops 2415919104 | bytes 19660800 | tf_op jit(solution)/shard_map/convolution_backward/pallas_call | solution.py:617
  459.2 9.3 %row_grad.2 = (bf16[512,4096]{1,0:T(8,128)(2,1)}, bf16[512,4096]{1,0:T(8,128)(2,1)}) custom-call(s32[1]{0:T(128)} %bitcast.core_ref, bf16[384,1024]{1,0:T(8,128)(2,1)} %get-tuple-element.126.refs_0_, bf16[384,1024]{1,0:T(8,128)(2,1)} %get-tuple-element.127.refs_1_, bf16[384,1024]{1,0:T(8,128)(2,1)} %get-tuple-element.128.refs_2_, ...), custom_call_target="tpu_custom_call" | custom-call | flops 1024 | bytes 37001024 | tf_op jit(solution)/shard_map/row_grad/pallas_call | solution.py:1394
  480.2 28.5 %attention_backward.1 = (bf16[3072,128]{1,0:T(8,128)(2,1)}, bf16[1536,256]{1,0:T(8,128)(2,1)}, f32[3072,256]{1,0:T(8,128)}, bf16[1536,256]{1,0:T(8,128)(2,1)}) custom-call(s32[6]{0:T(128)} %fusion.8.refs_0_, s32[6]{0:T(128)} %slice.223.refs_1_, f32[1]{0:T(128)} %bitcast.1.refs_2_, bf16[3072,128]{1,0:T(8,128)(2,1)} %bitcast.6.refs_3_, ...), custom_call_target="tpu_custom_call" | custom-call | flops 32212254720 | bytes 7340032 | tf_op jit(solution)/shard_map/attention_backward/pallas_call | solution.py:1007
  508.7 8.7 %collective-permute-start.10 = (bf16[1536,256]{1,0:T(8,128)(2,1)}, bf16[1536,256]{1,0:T(8,128)(2,1)S(1)}, u32[]{:S(2)}, u32[]{:S(2)}) collective-permute-start(bf16[1536,256]{1,0:T(8,128)(2,1)} %get-tuple-element.135), channel_id=1, source_target_pairs={{0,8},{8,16},{16,24},{1,9},{9,17},{17,25},{2,10},{10,18},{18,26},{... | collective-permute-start | bytes 2359304 | tf_op jit(solution)/shard_map/ppermute | solution.py:1596
  550.1 16.1 %all-to-all-done.9.dkv_ref.refs_3_ = bf16[8,384,256]{2,1,0:T(8,128)(2,1)S(1)} async-done(((bf16[8,384,256]{2,1,0:T(8,128)(2,1)}), bf16[8,384,256]{2,1,0:T(8,128)(2,1)S(1)}, u32[]{:S(2)}, u32[]{:S(2)}) %all-to-all-start.9) | async-done | bytes 1572896 | tf_op jit(solution)/shard_map/all_to_all | solution.py:1519
  567.4 9.0 %projections_backward.1 = (f32[384,1024]{1,0:T(8,128)}, bf16[1,384,1024]{2,1,0:T(8,128)(2,1)}, f32[8,1024]{1,0:T(8,128)}) custom-call(bf16[8,384,128]{2,1,0:T(8,128)(2,1)} %all-to-all-done.8.dq_ref.refs_1_, bf16[8,384,256]{2,1,0:T(8,128)(2,1)} %copy-done.27, f32[384,1024]{1,0:T(8,128)} %get-tuple-element.139.dx2_ref, f32[384,1024]{1,0:T(8,128)} %get-tuple-element.109.x1_ref, ...), custom_call_target="tpu_custom_call" | custom-call | flops 1024 | bytes 33301024 | tf_op jit(solution)/shard_map/projections_backward/pallas_call | solution.py:718
  600.8 14.5 %last_part.1 = (bf16[384,1024]{1,0:T(8,128)(2,1)}, f32[8,1024]{1,0:T(8,128)}, bf16[1,384,1024]{2,1,0:T(8,128)(2,1)}, bf16[1,384,1024]{2,1,0:T(8,128)(2,1)}, bf16[2,384,1024]{2,1,0:T(8,128)(2,1)}) custom-call(s32[1]{0:T(128)} %bitcast.core_ref, f32[384,1024]{1,0:T(8,128)} %get-tuple-element.140.dx1_ref, ...), custom_call_target="tpu_custom_call" | custom-call | flops 1024 | bytes 55501024 | tf_op jit(solution)/shard_map/last_part/pallas_call | solution.py:771
  615.3 8.3 %collective-permute-done.20 = bf16[2,256,1024]{2,1,0:T(8,128)(2,1)S(1)} collective-permute-done((bf16[2,256,1024]{2,1,0:T(8,128)(2,1)S(1)}, bf16[2,256,1024]{2,1,0:T(8,128)(2,1)S(1)}, u32[]{:S(2)}, u32[]{:S(2)}) %collective-permute-start.20) | collective-permute-done | bytes 1048608 | tf_op jit(solution)/shard_map/ppermute | solution.py:39
  667.8 28.2 %collective-permute-done.27 = bf16[2,128,3072]{2,1,0:T(8,128)(2,1)S(1)} collective-permute-done((bf16[2,128,3072]{2,1,0:T(8,128)(2,1)S(1)}, bf16[2,128,3072]{2,1,0:T(8,128)(2,1)S(1)}, u32[]{:S(2)}, u32[]{:S(2)}) %collective-permute-start.27) | collective-permute-done | bytes 1572896 | tf_op jit(solution)/shard_map/ppermute | solution.py:39
  702.4 14.0 %collective-permute-done.30 = bf16[4,128,1024]{2,1,0:T(8,128)(2,1)S(1)} collective-permute-done((bf16[4,128,1024]{2,1,0:T(8,128)(2,1)S(1)}, bf16[4,128,1024]{2,1,0:T(8,128)(2,1)S(1)}, u32[]{:S(2)}, u32[]{:S(2)}) %collective-permute-start.30) | collective-permute-done | bytes 1048608 | tf_op jit(solution)/shard_map/ppermute | solution.py:39
  725.5 13.3 %collective-permute-done.34 = bf16[2,128,1024]{2,1,0:T(8,128)(2,1)S(1)} collective-permute-done((bf16[2,128,1024]{2,1,0:T(8,128)(2,1)S(1)}, bf16[2,128,1024]{2,1,0:T(8,128)(2,1)S(1)}, u32[]{:S(2)}, u32[]{:S(2)}) %collective-permute-start.34) | collective-permute-done | bytes 524320 | tf_op jit(solution)/shard_map/ppermute | solution.py:39
  (334 shorter events, 263.9 us)
Async XLA Ops:
  7.2 152.4 %all-gather.4.cloned.1.call-start = ((), (), s32[]{:S(2)}) async-start(), calls=%async_computation.11 | async-start | bytes 23789568 | tf_op jit(solution)/shard_map/all_gather | solution.py:1443
  12.2 271.0 %all-gather.6.cloned.1.call-start = ((), (), s32[]{:S(2)}) async-start(), calls=%async_computation.12 | async-start | bytes 8650752 | tf_op jit(solution)/shard_map/all_gather | solution.py:1443
  13.0 367.1 %all-gather.8.cloned.1.call-start = ((), (), s32[]{:S(2)}) async-start(), calls=%async_computation.13 | async-start | bytes 17301504 | tf_op jit(solution)/shard_map/all_gather | solution.py:1443
  184.8 110.5 %collective-permute-start.4 = (bf16[3,384,1024]{2,1,0:T(8,128)(2,1)}, bf16[3,384,1024]{2,1,0:T(8,128)(2,1)S(1)}, u32[]{:S(2)}, u32[]{:S(2)}) collective-permute-start(bf16[3,384,1024]{2,1,0:T(8,128)(2,1)} %get-tuple-element.110.la_ref), channel_id=1, source_target_pairs={{0,1},{1,0},{2,3},{3,2},{4,5},{5,4},{6,7},{7,6},{8,9},{9,8},{10,11... | collective-permute-start | bytes 7077896 | tf_op jit(solution)/shard_map/ppermute | solution.py:39
  209.0 32.6 %collective-permute-start.2 = (bf16[1536,128]{1,0:T(8,128)(2,1)S(1)}, bf16[1536,128]{1,0:T(8,128)(2,1)}, u32[]{:S(2)}, u32[]{:S(2)}) collective-permute-start(bf16[1536,128]{1,0:T(8,128)(2,1)S(1)} %bitcast.163), channel_id=1, source_target_pairs={{0,8},{8,16},{16,24},{1,9},{9,17},{17,25},{2,10},{10,18},{18,26},{... | collective-permute-start | bytes 1179656 | tf_op jit(solution)/shard_map/ppermute | solution.py:1525
  211.1 30.5 %collective-permute-start.3 = (bf16[1536,128]{1,0:T(8,128)(2,1)S(1)}, bf16[1536,128]{1,0:T(8,128)(2,1)}, u32[]{:S(2)}, u32[]{:S(2)}) collective-permute-start(bf16[1536,128]{1,0:T(8,128)(2,1)S(1)} %bitcast.162), channel_id=1, source_target_pairs={{8,0},{16,8},{24,16},{9,1},{17,9},{25,17},{10,2},{18,10},{26,18},{... | collective-permute-start | bytes 1179656 | tf_op jit(solution)/shard_map/ppermute | solution.py:1525
  229.1 26.4 %collective-permute-start.1 = (bf16[1536,128]{1,0:T(8,128)(2,1)}, bf16[1536,128]{1,0:T(8,128)(2,1)}, u32[]{:S(2)}, u32[]{:S(2)}) collective-permute-start(bf16[1536,128]{1,0:T(8,128)(2,1)} %bitcast.9), channel_id=1, source_target_pairs={{8,0},{16,8},{24,16},{9,1},{17,9},{25,17},{10,2},{18,10},{26,18},{... | collective-permute-start | bytes 1179656 | tf_op jit(solution)/shard_map/ppermute | solution.py:1525
  317.8 62.3 %all-to-all-start.5 = ((f32[32,2,1024]{2,1,0:T(2,128)}), f32[32,2,1024]{2,1,0:T(2,128)S(1)}, u32[]{:S(2)}, u32[]{:S(2)}) async-start(f32[32,2,1024]{2,1,0:T(2,128)} %get-tuple-element.114), calls=%async_computation.5 | async-start | bytes 524288 | tf_op jit(solution)/shard_map/all_to_all | solution.py:1536
  449.4 29.9 %all-to-all-start.7 = ((bf16[8,384,128]{2,1,0:T(8,128)(2,1)}), bf16[8,384,128]{2,1,0:T(8,128)(2,1)S(1)}, u32[]{:S(2)}, u32[]{:S(2)}) async-start(bf16[8,384,128]{2,1,0:T(8,128)(2,1)} %get-tuple-element.124), calls=%async_computation.7 | async-start | bytes 1572864 | tf_op jit(solution)/shard_map/all_to_all | solution.py:1514
  455.7 67.3 %collective-permute-start.12 = (bf16[2,512,1024]{2,1,0:T(8,128)(2,1)}, bf16[2,512,1024]{2,1,0:T(8,128)(2,1)}, u32[]{:S(2)}, u32[]{:S(2)}) collective-permute-start(bf16[2,512,1024]{2,1,0:T(8,128)(2,1)} %slab_grad.8.refs_0_), channel_id=1, source_target_pairs={{0,4},{4,0},{1,5},{5,1},{2,6},{6,2},{3,7},{7,3},{8,12},{12,8},{9,1... | collective-permute-start | bytes 6291464 | tf_op jit(solution)/shard_map/ppermute | solution.py:39
  457.9 68.0 %collective-permute-start.13 = (bf16[2,512,1024]{2,1,0:T(8,128)(2,1)}, bf16[2,512,1024]{2,1,0:T(8,128)(2,1)}, u32[]{:S(2)}, u32[]{:S(2)}) collective-permute-start(bf16[2,512,1024]{2,1,0:T(8,128)(2,1)} %slab_grad.9.refs_1_.refs_0_), channel_id=1, source_target_pairs={{0,2},{2,0},{1,3},{3,1},{4,6},{6,4},{5,7},{7,5},{8,10},{10,8},{9,1... | collective-permute-start | bytes 6291464 | tf_op jit(solution)/shard_map/ppermute | solution.py:39
  468.6 121.3 %collective-permute-start.16 = (bf16[512,4096]{1,0:T(8,128)(2,1)}, bf16[512,4096]{1,0:T(8,128)(2,1)}, u32[]{:S(2)}, u32[]{:S(2)}) collective-permute-start(bf16[512,4096]{1,0:T(8,128)(2,1)} %get-tuple-element.145), channel_id=1, source_target_pairs={{0,1},{1,0},{2,3},{3,2},{4,5},{5,4},{6,7},{7,6},{8,9},{9,8},{10,11... | collective-permute-start | bytes 12582920 | tf_op jit(solution)/shard_map/ppermute | solution.py:39
  508.7 26.4 %collective-permute-start.10 = (bf16[1536,256]{1,0:T(8,128)(2,1)}, bf16[1536,256]{1,0:T(8,128)(2,1)S(1)}, u32[]{:S(2)}, u32[]{:S(2)}) collective-permute-start(bf16[1536,256]{1,0:T(8,128)(2,1)} %get-tuple-element.135), channel_id=1, source_target_pairs={{0,8},{8,16},{16,24},{1,9},{9,17},{17,25},{2,10},{10,18},{18,26},{... | collective-permute-start | bytes 2359304 | tf_op jit(solution)/shard_map/ppermute | solution.py:1596
  545.8 49.9 %collective-permute-start.14 = (bf16[1,512,1024]{2,1,0:T(8,128)(2,1)}, bf16[1,512,1024]{2,1,0:T(8,128)(2,1)}, u32[]{:S(2)}, u32[]{:S(2)}) collective-permute-start(bf16[1,512,1024]{2,1,0:T(8,128)(2,1)} %get-tuple-element.137.refs_0_), channel_id=1, source_target_pairs={{0,2},{2,0},{1,3},{3,1},{4,6},{6,4},{5,7},{7,5},{8,10},{10,8},{9,1... | collective-permute-start | bytes 3145736 | tf_op jit(solution)/shard_map/ppermute | solution.py:39
  547.8 47.9 %collective-permute-start.15 = (bf16[4,128,1024]{2,1,0:T(8,128)(2,1)}, bf16[4,128,1024]{2,1,0:T(8,128)(2,1)}, u32[]{:S(2)}, u32[]{:S(2)}) collective-permute-start(bf16[4,128,1024]{2,1,0:T(8,128)(2,1)} %get-tuple-element.138.refs_1_), channel_id=1, source_target_pairs={{0,4},{4,0},{1,5},{5,1},{2,6},{6,2},{3,7},{7,3},{8,12},{12,8},{9,1... | collective-permute-start | bytes 3145736 | tf_op jit(solution)/shard_map/ppermute | solution.py:39
  584.0 73.7 %collective-permute-start.24 = (bf16[512,3072]{1,0:T(8,128)(2,1)}, bf16[512,3072]{1,0:T(8,128)(2,1)S(1)}, u32[]{:S(2)}, u32[]{:S(2)}) collective-permute-start(bf16[512,3072]{1,0:T(8,128)(2,1)} %get-tuple-element.148.refs_0_), channel_id=1, source_target_pairs={{0,1},{1,0},{2,3},{3,2},{4,5},{5,4},{6,7},{7,6},{8,9},{9,8},{10,11... | collective-permute-start | bytes 9437192 | tf_op jit(solution)/shard_map/ppermute | solution.py:39
  598.7 60.9 %collective-permute-start.23 = (bf16[2,512,1024]{2,1,0:T(8,128)(2,1)}, bf16[2,512,1024]{2,1,0:T(8,128)(2,1)}, u32[]{:S(2)}, u32[]{:S(2)}) collective-permute-start(bf16[2,512,1024]{2,1,0:T(8,128)(2,1)} %slab_grad.12.refs_0_), channel_id=1, source_target_pairs={{0,2},{2,0},{1,3},{3,1},{4,6},{6,4},{5,7},{7,5},{8,10},{10,8},{9,1... | collective-permute-start | bytes 6291464 | tf_op jit(solution)/shard_map/ppermute | solution.py:39
  600.2 62.9 %collective-permute-start.22 = (bf16[4,64,4096]{2,1,0:T(8,128)(2,1)}, bf16[4,64,4096]{2,1,0:T(8,128)(2,1)}, u32[]{:S(2)}, u32[]{:S(2)}) collective-permute-start(bf16[4,64,4096]{2,1,0:T(8,128)(2,1)} %get-tuple-element.149.refs_8_), channel_id=1, source_target_pairs={{0,4},{4,0},{1,5},{5,1},{2,6},{6,2},{3,7},{7,3},{8,12},{12,8},{9,1... | collective-permute-start | bytes 6291464 | tf_op jit(solution)/shard_map/ppermute | solution.py:39
  628.7 26.3 %collective-permute-start.25 = (bf16[1,256,1024]{2,1,0:T(8,128)(2,1)S(1)}, bf16[1,256,1024]{2,1,0:T(8,128)(2,1)S(1)}, u32[]{:S(2)}, u32[]{:S(2)}) collective-permute-start(bf16[1,256,1024]{2,1,0:T(8,128)(2,1)S(1)} %get-tuple-element.156.refs_0_), channel_id=1, source_target_pairs={{0,16},{8,24},{16,0},{24,8},{1,17},{9,25},{17,1},{25,9},{2,18},{10... | collective-permute-start | bytes 1572872 | tf_op jit(solution)/shard_map/ppermute | solution.py:39
  640.4 56.3 %collective-permute-start.21 = (bf16[2,512,1024]{2,1,0:T(8,128)(2,1)}, bf16[2,512,1024]{2,1,0:T(8,128)(2,1)}, u32[]{:S(2)}, u32[]{:S(2)}) collective-permute-start(bf16[2,512,1024]{2,1,0:T(8,128)(2,1)} %slab_grad.14.refs_1_), channel_id=1, source_target_pairs={{0,4},{4,0},{1,5},{5,1},{2,6},{6,2},{3,7},{7,3},{8,12},{12,8},{9,1... | collective-permute-start | bytes 6291464 | tf_op jit(solution)/shard_map/ppermute | solution.py:39
  659.5 36.4 %collective-permute-start.27 = (bf16[2,128,3072]{2,1,0:T(8,128)(2,1)S(1)}, bf16[2,128,3072]{2,1,0:T(8,128)(2,1)S(1)}, u32[]{:S(2)}, u32[]{:S(2)}) collective-permute-start(bf16[2,128,3072]{2,1,0:T(8,128)(2,1)S(1)} %get-tuple-element.161.refs_0_), channel_id=1, source_target_pairs={{0,8},{8,0},{16,24},{24,16},{1,9},{9,1},{17,25},{25,17},{2,10},{10... | collective-permute-start | bytes 4718600 | tf_op jit(solution)/shard_map/ppermute | solution.py:39
  665.7 30.6 %collective-permute-start.26 = (bf16[4,32,4096]{2,1,0:T(8,128)(2,1)S(1)}, bf16[4,32,4096]{2,1,0:T(8,128)(2,1)S(1)}, u32[]{:S(2)}, u32[]{:S(2)}) collective-permute-start(bf16[4,32,4096]{2,1,0:T(8,128)(2,1)S(1)} %get-tuple-element.164.refs_0_), channel_id=1, source_target_pairs={{0,2},{2,0},{1,3},{3,1},{4,6},{6,4},{5,7},{7,5},{8,10},{10,8},{9,1... | collective-permute-start | bytes 3145736 | tf_op jit(solution)/shard_map/ppermute | solution.py:39
  667.3 49.1 %collective-permute-start.30 = (bf16[4,128,1024]{2,1,0:T(8,128)(2,1)S(1)}, bf16[4,128,1024]{2,1,0:T(8,128)(2,1)S(1)}, u32[]{:S(2)}, u32[]{:S(2)}) collective-permute-start(bf16[4,128,1024]{2,1,0:T(8,128)(2,1)S(1)} %get-tuple-element.162.refs_0_), channel_id=1, source_target_pairs={{0,4},{4,0},{1,5},{5,1},{2,6},{6,2},{3,7},{7,3},{8,12},{12,8},{9,1... | collective-permute-start | bytes 3145736 | tf_op jit(solution)/shard_map/ppermute | solution.py:39
  701.9 37.0 %collective-permute-start.32 = (bf16[2,64,3072]{2,1,0:T(8,128)(2,1)S(1)}, bf16[2,64,3072]{2,1,0:T(8,128)(2,1)S(1)}, u32[]{:S(2)}, u32[]{:S(2)}) collective-permute-start(bf16[2,64,3072]{2,1,0:T(8,128)(2,1)S(1)} %get-tuple-element.166.refs_0_), channel_id=1, source_target_pairs={{0,4},{4,0},{1,5},{5,1},{2,6},{6,2},{3,7},{7,3},{8,12},{12,8},{9,1... | collective-permute-start | bytes 2359304 | tf_op jit(solution)/shard_map/ppermute | solution.py:39
  (88 other events, 1028.9 us)
Sparse Core Ops, SparseCore 0:
  12.3 147.2 all-gather.3
  163.1 93.8 all-gather.5
  260.4 119.6 all-gather.7
